TPU v7x, 32 devices: a whole 2x2x4 slice. The times are simulated.
32 devices in a mesh: groups: 2 (over y), frame: 4 (over z), quarter: 2 (over x), sub: 2 (over core).
Axes of the slice: x: 2, y: 2, z: 4, core: 2. Of those that a mesh axis runs over, the one named last changes fastest.
Arguments:
- queries: bfloat16 [16, 1024, 256], P(('groups', 'frame'), ('quarter', 'sub')), parts along dimension 0, may hold values from -36 to 36
- keys: bfloat16 [16, 1024, 256], P(('groups', 'frame'), ('quarter', 'sub')), parts along dimension 0, may hold values from -6 to 6
- values: bfloat16 [16, 1024, 256], P(('groups', 'frame'), ('quarter', 'sub')), parts along dimension 0, may hold values from -6 to 6
Outputs:
- attended: bfloat16 [16, 1024, 256], P(('groups', 'frame'), ('quarter', 'sub')), parts along dimension 0
There are 2 independent parts, one for each index of `groups`. A program takes and returns all parts, laid end to end along the dimension named above; each array names one. Nothing has to cross between parts.
All inputs are finite; a program needn't handle non-finite values.
Results may differ from a plain program's by a relative error of at most 0.0028.
Values may be sent and summed in bfloat16 or wider, within the bound.
No kernel may reach another device: no remote copies, remote signals or barrier semaphores. Data moves between devices by JAX's collectives and lax.ppermute only.
A program may use at most 64 MiB of HBM per device.

v0:
```python
import math

import jax
import jax.numpy as jnp
from jax import lax
from jax.sharding import PartitionSpec as P

STRIP = 16


def partial_attend(query_rows, key_rows, value_rows, running, score_scale):
    top_run, sum_run, acc_run = running
    scores = (
        jnp.einsum("frd,fnd->frn", query_rows, key_rows, preferred_element_type=jnp.float32)
        * score_scale
    )
    highest = jnp.maximum(top_run, jnp.max(scores, axis=-1, keepdims=True))
    expo = jnp.exp(scores - highest)
    factor = jnp.exp(top_run - highest)
    sum_next = sum_run * factor + jnp.sum(expo, axis=-1, keepdims=True)
    acc_next = acc_run * factor + jnp.einsum(
        "frn,fnd->frd", expo.astype(jnp.bfloat16), value_rows, preferred_element_type=jnp.float32
    )
    return (highest, sum_next, acc_next)


def fold_keys(query_rows, score_scale, running, pieces):
    key_piece, value_piece = pieces
    length = key_piece.shape[1]
    block_keys = math.gcd(length, 2048)
    for block_index in range(length // block_keys):
        lower = block_index * block_keys
        running = partial_attend(
            query_rows,
            key_piece[:, lower : lower + block_keys],
            value_piece[:, lower : lower + block_keys],
            running,
            score_scale,
        )
    return running


def empty_state(query_rows):
    frames_here, rows_here, width = query_rows.shape
    return (
        jnp.full((frames_here, rows_here, 1), -jnp.inf, jnp.float32),
        jnp.zeros((frames_here, rows_here, 1), jnp.float32),
        jnp.zeros((frames_here, rows_here, width), jnp.float32),
    )


def body(queries, keys, values):
    head_width = queries.shape[2] // 2
    frames_dev = queries.shape[0]
    tokens_dev = queries.shape[1]
    score_scale = 1.0 / math.sqrt(head_width)
    query_spatial = queries[:, :, :head_width]
    key_spatial = keys[:, :, :head_width]
    value_spatial = values[:, :, :head_width]
    frame_count = lax.axis_size("frame")
    local_strips = tokens_dev // (STRIP * frame_count)

    def to_strips(array):
        part_two = array[:, :, head_width:].reshape(
            frames_dev, frame_count, local_strips, STRIP, head_width
        )
        return part_two.transpose(1, 2, 0, 3, 4)

    query_strip = lax.all_to_all(
        to_strips(queries), "frame", split_axis=0, concat_axis=2, tiled=True
    )
    key_strip = lax.all_to_all(to_strips(keys), "frame", split_axis=0, concat_axis=2, tiled=True)
    value_strip = lax.all_to_all(
        to_strips(values), "frame", split_axis=0, concat_axis=2, tiled=True
    )
    item_count = query_strip.shape[1]
    frames_all = query_strip.shape[2]
    rows_strip = frames_all * STRIP
    query_flat = query_strip.reshape(item_count, rows_strip, head_width)
    key_flat = key_strip.reshape(item_count, rows_strip, head_width)
    value_flat = value_strip.reshape(item_count, rows_strip, head_width)
    scores = (
        jnp.einsum("nqd,nkd->nqk", query_flat, key_flat, preferred_element_type=jnp.float32)
        * score_scale
    )
    highest = jnp.max(scores, axis=-1, keepdims=True)
    expo = jnp.exp(scores - highest)
    totals = jnp.sum(expo, axis=-1, keepdims=True)
    mixed = jnp.einsum(
        "nqk,nkd->nqd", expo.astype(jnp.bfloat16), value_flat, preferred_element_type=jnp.float32
    )
    strip_out = (
        (mixed / totals).astype(jnp.bfloat16).reshape(1, item_count, frames_all, STRIP, head_width)
    )
    returned = lax.all_to_all(strip_out, "frame", split_axis=2, concat_axis=0, tiled=True)
    temporal = returned.transpose(2, 0, 1, 3, 4).reshape(frames_dev, tokens_dev, head_width)
    top_all, total_spatial, acc_spatial = fold_keys(
        query_spatial,
        score_scale,
        empty_state(query_spatial),
        (
            lax.all_gather(key_spatial, ("quarter", "sub"), axis=1, tiled=True),
            lax.all_gather(value_spatial, ("quarter", "sub"), axis=1, tiled=True),
        ),
    )
    spatial = (acc_spatial / total_spatial).astype(jnp.bfloat16)
    return jnp.concatenate([spatial, temporal], axis=-1)


def solution(mesh):
    in_specs = (
        P(("groups", "frame"), ("quarter", "sub"), None),
        P(("groups", "frame"), ("quarter", "sub"), None),
        P(("groups", "frame"), ("quarter", "sub"), None),
    )
    out_specs = P(("groups", "frame"), ("quarter", "sub"), None)
    return jax.shard_map(body, mesh=mesh, in_specs=in_specs, out_specs=out_specs, check_vma=False)
```

profile of v0, /device:TPU:0, one launch (start us, length us, event | category | flops | bytes accessed | tf_op | source)
XLA Modules:
  0.0 53.8 jit_solution(1499810248122373728)
XLA Ops:
  0.0 1.0 %fusion.16 = (bf16[2,256,128]{2,1,0:T(8,128)(2,1)S(1)}, bf16[2,256,128]{2,1,0:T(8,128)(2,1)S(1)}) fusion(bf16[2,256,256]{2,1,0:T(8,128)(2,1)} %param.4), kind=kLoop, calls=%fused_computation.22 | loop fusion | bytes 524288 | tf_op jit(solution)/shard_map/slice | solution.py:58
  1.0 0.0 copy-start
  1.0 0.7 %copy.31 = bf16[4,4,2,16,128]{4,3,2,1,0:T(8,128)(2,1)} copy(bf16[4,4,2,16,128]{4,3,1,0,2:T(8,128)(2,1)S(1)} %bitcast.42) | data formatting | bytes 262144 | tf_op jit(solution)/shard_map/transpose | solution.py:67
  1.7 6.3 %all-to-all-start.1 = ((bf16[4,4,2,16,128]{4,3,2,1,0:T(8,128)(2,1)}), bf16[4,4,2,16,128]{4,3,2,1,0:T(8,128)(2,1)S(1)}, u32[]{:S(2)}, u32[]{:S(2)}) async-start(bf16[4,4,2,16,128]{4,3,2,1,0:T(8,128)(2,1)} %copy.31), calls=%async_computation.1 | async-start | bytes 262144 | tf_op jit(solution)/shard_map/all_to_all | solution.py:72
  8.0 0.0 slice-start
  8.0 7.3 %all_gather.6 = bf16[2,1024,128]{2,1,0:T(8,128)(2,1)S(1)} all-gather(bf16[2,256,128]{2,1,0:T(8,128)(2,1)S(1)} %get-tuple-element.5), channel_id=1, replica_groups=mesh['groups'=2,'frame'=4,'quarter'=2,'sub'=2] {'quarter','sub'}, dimensions={1}, use_global_device_ids=true | all-gather | bytes 655360 | tf_op jit(solution)/shard_map/all_gather | solution.py:102
  15.3 1.4 %multiply_reduce_fusion = (f32[2,256]{1,0:T(2,128)S(1)}, f32[2,256,1024]{2,1,0:T(8,128)S(1)}) fusion(bf16[2,1024,128]{2,1,0:T(8,128)(2,1)S(1)} %all_gather.6, bf16[2,256,256]{2,1,0:T(8,128)(2,1)} %param.3), kind=kOutput, calls=%fused_computation.1 | convolution fusion | flops 135265792 | bytes 2754560 | tf_op jit(solution)/shard_map/frd,fnd->frn/dot_general | solution.py:14
  16.7 0.0 copy-done
  16.8 0.1 copy.43
  16.9 0.0 slice-done
  16.9 0.7 %copy.29 = bf16[4,4,2,16,128]{4,3,2,1,0:T(8,128)(2,1)} copy(bf16[4,4,2,16,128]{4,3,1,0,2:T(8,128)(2,1)S(1)} %bitcast.37) | data formatting | bytes 262144 | tf_op jit(solution)/shard_map/transpose | solution.py:67
  17.5 0.7 %copy.33 = bf16[4,4,2,16,128]{4,3,2,1,0:T(8,128)(2,1)} copy(bf16[4,4,2,16,128]{4,3,1,0,2:T(8,128)(2,1)S(1)} %bitcast.41) | data formatting | bytes 262144 | tf_op jit(solution)/shard_map/transpose | solution.py:67
  18.2 0.5 fusion
  18.7 0.0 all-to-all-done.1
  18.7 5.1 %all-to-all-start = ((bf16[4,4,2,16,128]{4,3,2,1,0:T(8,128)(2,1)}), bf16[4,4,2,16,128]{4,3,2,1,0:T(8,128)(2,1)S(1)}, u32[]{:S(2)}, u32[]{:S(2)}) async-start(bf16[4,4,2,16,128]{4,3,2,1,0:T(8,128)(2,1)} %copy.29), calls=%async_computation | async-start | bytes 262144 | tf_op jit(solution)/shard_map/all_to_all | solution.py:69
  23.8 6.4 %all-to-all-done = bf16[4,4,2,16,128]{4,3,2,1,0:T(8,128)(2,1)S(1)} async-done(((bf16[4,4,2,16,128]{4,3,2,1,0:T(8,128)(2,1)}), bf16[4,4,2,16,128]{4,3,2,1,0:T(8,128)(2,1)S(1)}, u32[]{:S(2)}, u32[]{:S(2)}) %all-to-all-start) | async-done | bytes 131104 | tf_op jit(solution)/shard_map/all_to_all | solution.py:69
  30.2 3.3 %all-to-all-start.2 = ((bf16[4,4,2,16,128]{4,3,2,1,0:T(8,128)(2,1)}), bf16[4,4,2,16,128]{4,3,2,1,0:T(8,128)(2,1)S(1)}, u32[]{:S(2)}, u32[]{:S(2)}) async-start(bf16[4,4,2,16,128]{4,3,2,1,0:T(8,128)(2,1)} %copy.33), calls=%async_computation.2 | async-start | bytes 262144 | tf_op jit(solution)/shard_map/all_to_all | solution.py:73
  33.6 6.5 %all_gather.7 = bf16[2,1024,128]{1,2,0:T(8,128)(2,1)S(1)} all-gather(bf16[2,256,128]{1,2,0:T(8,128)(2,1)S(1)} %copy.43), channel_id=1, replica_groups=mesh['groups'=2,'frame'=4,'quarter'=2,'sub'=2] {'quarter','sub'}, dimensions={1}, use_global_device_ids=true | all-gather | bytes 655360 | tf_op jit(solution)/shard_map/all_gather | solution.py:103
  40.1 0.0 all-to-all-done.2
  40.1 0.2 fusion.18
  40.4 0.1 fusion.8
  40.4 0.3 fusion.3
  40.7 0.7 %copy.36 = bf16[1,4,8,16,128]{4,3,1,0,2:T(8,128)(2,1)} copy(bf16[1,4,8,16,128]{4,3,2,1,0:T(8,128)(2,1)S(1)} %bitcast.44) | data formatting | bytes 262144 | tf_op jit(solution)/shard_map/reshape | solution.py:93
  41.4 5.0 %all-to-all-start.3 = ((bf16[1,4,8,16,128]{4,3,1,0,2:T(8,128)(2,1)}), bf16[1,4,8,16,128]{4,3,1,0,2:T(8,128)(2,1)S(1)}, u32[]{:S(2)}, u32[]{:S(2)}) async-start(bf16[1,4,8,16,128]{4,3,1,0,2:T(8,128)(2,1)} %copy.36), calls=%async_computation.3 | async-start | bytes 262144 | tf_op jit(solution)/shard_map/all_to_all | solution.py:95
  46.4 0.6 %fusion.4 = bf16[2,256,128]{1,2,0:T(8,128)(2,1)S(1)} fusion(bf16[2,1024,128]{1,2,0:T(8,128)(2,1)S(1)} %all_gather.7, f32[2,256,1024]{2,1,0:T(8,128)S(1)} %get-tuple-element.14, f32[2,256]{1,0:T(2,128)S(1)} %get-tuple-element.13, f32[2,256]{1,0:T(2,128)S(1)} %get-tuple-element.10, f32[2,256]{1,0:T(2,128)S(1)} %get-tuple-element.9), kind=kOutput, calls=%fused_computation.9 | convolution fusion | flops 135987200 | bytes 2758656 | tf_op jit(solution)/shard_map/frn,fnd->frd/dot_general | solution.py:21
  47.0 5.8 %all-to-all-done.3 = bf16[1,4,8,16,128]{4,3,1,0,2:T(8,128)(2,1)S(1)} async-done(((bf16[1,4,8,16,128]{4,3,1,0,2:T(8,128)(2,1)}), bf16[1,4,8,16,128]{4,3,1,0,2:T(8,128)(2,1)S(1)}, u32[]{:S(2)}, u32[]{:S(2)}) %all-to-all-start.3) | async-done | bytes 131104 | tf_op jit(solution)/shard_map/all_to_all | solution.py:95
  52.8 0.1 copy.39
  53.0 0.8 %copy.40 = bf16[2,256,256]{2,1,0:T(8,128)(2,1)} copy(bf16[2,256,256]{1,2,0:T(8,128)(2,1)S(1)} %pad_maximum_fusion) | data formatting | bytes 524288 | tf_op jit(solution)/shard_map/concatenate | solution.py:107
  (7 shorter events, 0.1 us)
Async XLA Ops:
  1.0 15.7 %copy-start = (bf16[2,256,256]{2,1,0:T(8,128)(2,1)S(1)}, bf16[2,256,256]{2,1,0:T(8,128)(2,1)}, u32[]{:S(2)}) copy-start(bf16[2,256,256]{2,1,0:T(8,128)(2,1)} %param.5) | copy-start | bytes 786436
  1.7 17.0 %all-to-all-start.1 = ((bf16[4,4,2,16,128]{4,3,2,1,0:T(8,128)(2,1)}), bf16[4,4,2,16,128]{4,3,2,1,0:T(8,128)(2,1)S(1)}, u32[]{:S(2)}, u32[]{:S(2)}) async-start(bf16[4,4,2,16,128]{4,3,2,1,0:T(8,128)(2,1)} %copy.31), calls=%async_computation.1 | async-start | bytes 262144 | tf_op jit(solution)/shard_map/all_to_all | solution.py:72
  8.0 8.9 %slice-start = ((bf16[2,256,256]{2,1,0:T(8,128)(2,1)}), bf16[2,256,128]{2,1,0:T(8,128)(2,1)S(1)}, s32[]{:S(2)}) async-start(bf16[2,256,256]{2,1,0:T(8,128)(2,1)} %param.3), calls=%async_computation.4 | async-start | bytes 262144 | tf_op jit(solution)/shard_map/slice | solution.py:64
  18.7 11.5 %all-to-all-start = ((bf16[4,4,2,16,128]{4,3,2,1,0:T(8,128)(2,1)}), bf16[4,4,2,16,128]{4,3,2,1,0:T(8,128)(2,1)S(1)}, u32[]{:S(2)}, u32[]{:S(2)}) async-start(bf16[4,4,2,16,128]{4,3,2,1,0:T(8,128)(2,1)} %copy.29), calls=%async_computation | async-start | bytes 262144 | tf_op jit(solution)/shard_map/all_to_all | solution.py:69
  30.2 9.9 %all-to-all-start.2 = ((bf16[4,4,2,16,128]{4,3,2,1,0:T(8,128)(2,1)}), bf16[4,4,2,16,128]{4,3,2,1,0:T(8,128)(2,1)S(1)}, u32[]{:S(2)}, u32[]{:S(2)}) async-start(bf16[4,4,2,16,128]{4,3,2,1,0:T(8,128)(2,1)} %copy.33), calls=%async_computation.2 | async-start | bytes 262144 | tf_op jit(solution)/shard_map/all_to_all | solution.py:73
  41.4 11.5 %all-to-all-start.3 = ((bf16[1,4,8,16,128]{4,3,1,0,2:T(8,128)(2,1)}), bf16[1,4,8,16,128]{4,3,1,0,2:T(8,128)(2,1)S(1)}, u32[]{:S(2)}, u32[]{:S(2)}) async-start(bf16[1,4,8,16,128]{4,3,1,0,2:T(8,128)(2,1)} %copy.36), calls=%async_computation.3 | async-start | bytes 262144 | tf_op jit(solution)/shard_map/all_to_all | solution.py:95
where the time goes:
time: 54.4 us; the launch traced here: 53.8 us
  starting transfers between devices  19.8 us (36%)
  blocking collectives  13.8 us (25%)
  waiting for transfers between devices  12.2 us (22%)
  local copies, waits for them, and re-layouts  4.8 us (9%)
  matrix products  2.5 us (5%)
  other arithmetic  0.58 us (1%)
    all_gather x1, blocking collectives, body(): lax.all_gather(key_spatial, ('quarter', 'sub'), axis=1, tiled=True)  7.29 us
    all_gather x1, blocking collectives, body(): lax.all_gather(value_spatial, ('quarter', 'sub'), axis=1, tiled=True)  6.51 us
    all_to_all x1, waiting for transfers between devices, body(): lax.all_to_all(to_strips(queries), 'frame', split_axis=0, concat_axis=2,...  6.41 us
    all_to_all x1, starting transfers between devices, body(): lax.all_to_all(to_strips(keys), 'frame', split_axis=0, concat_axis=2, til...  6.32 us
    all_to_all x1, waiting for transfers between devices, body(): lax.all_to_all(strip_out, 'frame', split_axis=2, concat_axis=0, tiled=True)  5.81 us
    all_to_all x1, starting transfers between devices, body(): lax.all_to_all(to_strips(queries), 'frame', split_axis=0, concat_axis=2,...  5.1 us
    all_to_all x1, starting transfers between devices, body(): lax.all_to_all(strip_out, 'frame', split_axis=2, concat_axis=0, tiled=True)  5.04 us
    all_to_all x1, starting transfers between devices, body(): lax.all_to_all(to_strips(values), 'frame', split_axis=0, concat_axis=2, t...  3.33 us
  transfers between devices with their start and end apart: 4, of which 2 were waited for; matrix products, arithmetic and copies ran while one was open for 7% of the time, Pallas kernels for 0%

commit v1 on v0

v1 whole, which is shorter than its diff:
```python
import functools
import math

import jax
import jax.numpy as jnp
from jax import lax
from jax.experimental import pallas as pl
from jax.experimental.pallas import tpu as pltpu
from jax.sharding import PartitionSpec as P

STRIP = 16
VMEM_LIMIT = 16 * 1024 * 1024


def partner_of(index, step, count):
    if count & (count - 1) == 0:
        return index ^ step
    return (index + step) % count


def prep_kernel(count, head_width, q_hbm, k_hbm, v_hbm, *refs):
    blocks, kv_ref, sems = refs[:count], refs[count], refs[count + 1]
    me = lax.axis_index("frame")
    rows = blocks[0].shape[2]
    copies = []
    for step in [*range(count - 1, 0, -1), 0]:
        start = pl.multiple_of(partner_of(me, step, count) * rows, rows)
        for which, array in enumerate((q_hbm, k_hbm, v_hbm)):
            copies.append((array.at[:, pl.ds(start, rows), head_width:], blocks[step].at[which]))
    for which, array in enumerate((k_hbm, v_hbm)):
        copies.append((array.at[:, :, :head_width], kv_ref.at[which]))
    started = [
        pltpu.make_async_copy(src, dst, sems.at[number]) for number, (src, dst) in enumerate(copies)
    ]
    for copy in started:
        copy.start()
    for copy in started:
        copy.wait()


def attend(query_rows, key_rows, value_rows, score_scale):
    scores = (
        lax.dot_general(
            query_rows, key_rows, (((1,), (1,)), ((), ())), preferred_element_type=jnp.float32
        )
        * score_scale
    )
    highest = jnp.max(scores, axis=-1, keepdims=True)
    expo = jnp.exp(scores - highest)
    totals = jnp.sum(expo, axis=-1, keepdims=True)
    mixed = jnp.dot(expo.astype(jnp.bfloat16), value_rows, preferred_element_type=jnp.float32)
    return (mixed / totals).astype(jnp.bfloat16)


def temporal_kernel(count, score_scale, *refs):
    ins, outs = refs[:count], refs[count:]
    frames_dev, rows = ins[0].shape[1:3]
    for strip in range(rows // STRIP):
        cut = slice(strip * STRIP, (strip + 1) * STRIP)
        query, key, value = (
            jnp.concatenate([ref[which, frame, cut] for ref in ins for frame in range(frames_dev)])
            for which in range(3)
        )
        out = attend(query, key, value, score_scale)
        for number, ref in enumerate(outs):
            for frame in range(frames_dev):
                lower = (number * frames_dev + frame) * STRIP
                ref[frame, cut] = out[lower : lower + STRIP]


def spatial_kernel(score_scale, pieces, q_hbm, *refs):
    kvs, out_hbm = refs[:pieces], refs[pieces]
    q_ref, o_ref, sems = refs[pieces + 1 :]
    head_width = q_ref.shape[-1]
    load = pltpu.make_async_copy(q_hbm.at[:, :, :head_width], q_ref, sems.at[0])
    load.start()
    load.wait()
    for frame in range(q_ref.shape[0]):
        key = jnp.concatenate([kv[0, frame] for kv in kvs])
        value = jnp.concatenate([kv[1, frame] for kv in kvs])
        o_ref[frame] = attend(q_ref[frame], key, value, score_scale)
    store = pltpu.make_async_copy(o_ref, out_hbm.at[:, :, :head_width], sems.at[1])
    store.start()
    store.wait()


def join_kernel(count, head_width, *refs):
    pieces, out_hbm, sems = refs[:count], refs[count + 1], refs[count + 2]
    me = lax.axis_index("frame")
    rows = pieces[0].shape[1]
    copies = []
    for step in range(count):
        start = pl.multiple_of(partner_of(me, step, count) * rows, rows)
        copies.append(
            pltpu.make_async_copy(
                pieces[step], out_hbm.at[:, pl.ds(start, rows), head_width:], sems.at[step]
            )
        )
    for copy in copies:
        copy.start()
    for copy in copies:
        copy.wait()


def body(queries, keys, values):
    frames_dev, tokens_dev, width = queries.shape
    head_width = width // 2
    score_scale = 1.0 / math.sqrt(head_width)
    count = lax.axis_size("frame")
    rows = tokens_dev // count
    dtype = queries.dtype
    hbm = pl.BlockSpec(memory_space=pl.ANY)
    vmem = pl.BlockSpec(memory_space=pltpu.VMEM)
    params = pltpu.CompilerParams(vmem_limit_bytes=VMEM_LIMIT)

    *blocks, kv_own = pl.pallas_call(
        functools.partial(prep_kernel, count, head_width),
        out_shape=[jax.ShapeDtypeStruct((3, frames_dev, rows, head_width), dtype)] * count
        + [jax.ShapeDtypeStruct((2, frames_dev, tokens_dev, head_width), dtype)],
        in_specs=[hbm] * 3,
        out_specs=[vmem] * (count + 1),
        scratch_shapes=[pltpu.SemaphoreType.DMA((3 * count + 2,))],
        compiler_params=params,
        name="prep",
    )(queries, keys, values)

    def frame_shift(array, step, back=False):
        pairs = [(i, partner_of(i, step, count)) for i in range(count)]
        if back:
            pairs = [(b, a) for a, b in pairs]
        return lax.ppermute(array, "frame", pairs)

    arrived = [blocks[0]] + [None] * (count - 1)
    for step in range(count - 1, 0, -1):
        arrived[step] = frame_shift(blocks[step], step)

    pieces = [kv_own]
    quarters, subs = lax.axis_size("quarter"), lax.axis_size("sub")
    for step in range(1, quarters):
        pairs = [(i, (i + step) % quarters) for i in range(quarters)]
        pieces.append(lax.ppermute(kv_own, "quarter", pairs))
    for piece in list(pieces):
        for step in range(1, subs):
            pairs = [(i, (i + step) % subs) for i in range(subs)]
            pieces.append(lax.ppermute(piece, "sub", pairs))

    out = pl.pallas_call(
        functools.partial(spatial_kernel, score_scale, len(pieces)),
        out_shape=jax.ShapeDtypeStruct(queries.shape, dtype),
        in_specs=[hbm] + [vmem] * len(pieces),
        out_specs=hbm,
        scratch_shapes=[
            pltpu.VMEM((frames_dev, tokens_dev, head_width), dtype),
            pltpu.VMEM((frames_dev, tokens_dev, head_width), dtype),
            pltpu.SemaphoreType.DMA((2,)),
        ],
        compiler_params=params,
        name="spatial",
    )(queries, *pieces)

    strip_out = pl.pallas_call(
        functools.partial(temporal_kernel, count, score_scale),
        out_shape=[jax.ShapeDtypeStruct((frames_dev, rows, head_width), dtype)] * count,
        in_specs=[vmem] * count,
        out_specs=[vmem] * count,
        compiler_params=params,
        name="temporal",
    )(*arrived)

    returned = [strip_out[0]] + [None] * (count - 1)
    for step in range(count - 1, 0, -1):
        returned[step] = frame_shift(strip_out[step], step, back=True)

    return pl.pallas_call(
        functools.partial(join_kernel, count, head_width),
        out_shape=jax.ShapeDtypeStruct(queries.shape, dtype),
        in_specs=[vmem] * count + [hbm],
        out_specs=hbm,
        scratch_shapes=[pltpu.SemaphoreType.DMA((count,))],
        input_output_aliases={count: 0},
        compiler_params=params,
        name="join",
    )(*returned, out)


def solution(mesh):
    spec = P(("groups", "frame"), ("quarter", "sub"), None)
    return jax.shard_map(
        body, mesh=mesh, in_specs=(spec,) * 3, out_specs=spec, check_vma=False
    )
```

time: 54.4 us -> 35.9 us (0.66)
  blocking collectives: 13.8 us -> 0 us
  starting transfers between devices: 19.8 us -> 12 us
  waiting for transfers between devices: 12.2 us -> 16.9 us
  Pallas kernels: 0 us -> 3.9 us
  matrix products: 2.5 us -> 0 us
  local copies, waits for them, and re-layouts: 4.8 us -> 2.85 us
  other arithmetic: 0.58 us -> 0 us
    all_to_all x4 -> x0, starting transfers between devices: 19.8 us -> none  [the longest x1 6.32 us: body(): lax.all_to_all(to_strips(keys), 'frame', split_axis=0, concat_axis=2, til...]
    ppermute x0 -> x9, waiting for transfers between devices: none -> 16.9 us  [the longest x6 10.6 us: frame_shift(): return lax.ppermute(array, 'frame', pairs)]
    all_gather x2 -> x0, blocking collectives: 13.8 us -> none  [the longest x1 7.29 us: body(): lax.all_gather(key_spatial, ('quarter', 'sub'), axis=1, tiled=True)]
    all_to_all x4 -> x0, waiting for transfers between devices: 12.2 us -> none  [the longest x1 6.41 us: body(): lax.all_to_all(to_strips(queries), 'frame', split_axis=0, concat_axis=2,...]
    ppermute x0 -> x9, starting transfers between devices: none -> 12 us  [the longest x6 8.97 us: frame_shift(): return lax.ppermute(array, 'frame', pairs)]
    pallas_call x0 -> x4, Pallas kernels: none -> 3.9 us  [the longest x1 1.88 us: body(): pl.pallas_call(functools.partial(spatial_kernel, score_scale, len(pieces)...]
    unnamed x3 -> x8, local copies, waits for them, and re-layouts: 0.12 us -> 2.85 us
    dot_general x4 -> x0, matrix products: 2.5 us -> none  [the longest x1 1.42 us: partial_attend(): jnp.einsum('frd,fnd->frn', query_rows, key_rows, preferred_element_type=j...]
  transfers between devices with their start and end apart: 4 -> 9, of which waited for: 2 -> 5; matrix products, arithmetic and copies ran while one was open for 7% -> 0% of each run, Pallas kernels for 0% -> 8%
where the time goes in v1:
time: 35.9 us; the launch traced here: 35.7 us
  waiting for transfers between devices  16.9 us (47%)
  starting transfers between devices  12 us (33%)
  Pallas kernels  3.9 us (11%)
  local copies, waits for them, and re-layouts  2.85 us (8%)
    ppermute x6, waiting for transfers between devices, frame_shift(): return lax.ppermute(array, 'frame', pairs)  10.6 us
    ppermute x6, starting transfers between devices, frame_shift(): return lax.ppermute(array, 'frame', pairs)  8.97 us
    ppermute x1, waiting for transfers between devices, body(): pieces.append(lax.ppermute(kv_own, 'quarter', pairs))  6.3 us
    ppermute x1, starting transfers between devices, body(): pieces.append(lax.ppermute(kv_own, 'quarter', pairs))  3 us
    unnamed x8, local copies, waits for them, and re-layouts  2.85 us
    pallas_call x1, Pallas kernels, body(): pl.pallas_call(functools.partial(spatial_kernel, score_scale, len(pieces)...  1.88 us
    pallas_call x1, Pallas kernels, body(): pl.pallas_call(functools.partial(temporal_kernel, count, score_scale), ou...  1.07 us
  transfers between devices with their start and end apart: 9, of which 5 were waited for; matrix products, arithmetic and copies ran while one was open for 0% of the time, Pallas kernels for 8%

profile of v1, /device:TPU:0, one launch (start us, length us, event | category | flops | bytes accessed | tf_op | source)
XLA Modules:
  0.0 35.7 jit_solution(3026728560771236576)
XLA Ops:
  0.0 0.0 copy-start
  0.0 0.9 %copy-done = bf16[2,256,256]{2,1,0:T(8,128)(2,1)S(1)} copy-done((bf16[2,256,256]{2,1,0:T(8,128)(2,1)S(1)}, bf16[2,256,256]{2,1,0:T(8,128)(2,1)}, u32[]{:S(2)}) %copy-start) | copy-done | bytes 262168
  1.0 0.0 copy-start.2
  1.0 0.9 %copy-done.2 = bf16[2,256,256]{2,1,0:T(8,128)(2,1)S(1)} copy-done((bf16[2,256,256]{2,1,0:T(8,128)(2,1)S(1)}, bf16[2,256,256]{2,1,0:T(8,128)(2,1)}, u32[]{:S(2)}) %copy-start.2) | copy-done | bytes 262168
  1.9 0.0 copy-start.3
  1.9 0.9 %copy-done.3 = bf16[2,256,256]{2,1,0:T(8,128)(2,1)S(1)} copy-done((bf16[2,256,256]{2,1,0:T(8,128)(2,1)S(1)}, bf16[2,256,256]{2,1,0:T(8,128)(2,1)}, u32[]{:S(2)}) %copy-start.3) | copy-done | bytes 262168
  2.9 0.3 prep.1
  3.1 0.0 copy-start.1
  3.1 3.0 %collective-permute-start.6 = (bf16[2,2,256,128]{3,2,1,0:T(8,128)(2,1)S(1)}, bf16[2,2,256,128]{3,2,1,0:T(8,128)(2,1)S(1)}, u32[]{:S(2)}, u32[]{:S(2)}) collective-permute-start(bf16[2,2,256,128]{3,2,1,0:T(8,128)(2,1)S(1)} %get-tuple-element.22.refs_0_), channel_id=1, source_target_pairs={{0,2},{2,0},{1,3},{3,1},{4,6},{6,4},{5,7},{7,5},{8,10},{10,8},{9,1... | collective-permute-start | bytes 786440 | tf_op jit(solution)/shard_map/ppermute | solution.py:141
  6.1 0.0 collective-permute-start.7
  6.1 6.3 %collective-permute-done.6.refs_1_ = bf16[2,2,256,128]{3,2,1,0:T(8,128)(2,1)S(1)} collective-permute-done((bf16[2,2,256,128]{3,2,1,0:T(8,128)(2,1)S(1)}, bf16[2,2,256,128]{3,2,1,0:T(8,128)(2,1)S(1)}, u32[]{:S(2)}, u32[]{:S(2)}) %collective-permute-start.6) | collective-permute-done | bytes 262176 | tf_op jit(solution)/shard_map/ppermute | solution.py:141
  12.5 0.0 collective-permute-start.8
  12.5 1.8 %collective-permute-start = (bf16[3,2,64,128]{3,2,1,0:T(8,128)(2,1)S(1)}, bf16[3,2,64,128]{3,2,1,0:T(8,128)(2,1)S(1)}, u32[]{:S(2)}, u32[]{:S(2)}) collective-permute-start(bf16[3,2,64,128]{3,2,1,0:T(8,128)(2,1)S(1)} %get-tuple-element.15), channel_id=1, source_target_pairs={{0,4},{4,0},{8,12},{12,8},{1,5},{5,1},{9,13},{13,9},{2,6},{6,2},{1... | collective-permute-start | bytes 294920 | tf_op jit(solution)/shard_map/ppermute | solution.py:131
  14.3 2.6 %collective-permute-start.1 = (bf16[3,2,64,128]{3,2,1,0:T(8,128)(2,1)S(1)}, bf16[3,2,64,128]{3,2,1,0:T(8,128)(2,1)S(1)}, u32[]{:S(2)}, u32[]{:S(2)}) collective-permute-start(bf16[3,2,64,128]{3,2,1,0:T(8,128)(2,1)S(1)} %get-tuple-element.16), channel_id=1, source_target_pairs={{0,8},{4,12},{8,0},{12,4},{1,9},{5,13},{9,1},{13,5},{2,10},{6,14},... | collective-permute-start | bytes 294920 | tf_op jit(solution)/shard_map/ppermute | solution.py:131
  16.9 0.0 collective-permute-start.2
  16.9 0.9 %collective-permute-done.refs_1_ = bf16[3,2,64,128]{3,2,1,0:T(8,128)(2,1)S(1)} collective-permute-done((bf16[3,2,64,128]{3,2,1,0:T(8,128)(2,1)S(1)}, bf16[3,2,64,128]{3,2,1,0:T(8,128)(2,1)S(1)}, u32[]{:S(2)}, u32[]{:S(2)}) %collective-permute-start) | collective-permute-done | bytes 98336 | tf_op jit(solution)/shard_map/ppermute | solution.py:131
  17.7 7.3 %collective-permute-done.1.refs_2_ = bf16[3,2,64,128]{3,2,1,0:T(8,128)(2,1)S(1)} collective-permute-done((bf16[3,2,64,128]{3,2,1,0:T(8,128)(2,1)S(1)}, bf16[3,2,64,128]{3,2,1,0:T(8,128)(2,1)S(1)}, u32[]{:S(2)}, u32[]{:S(2)}) %collective-permute-start.1) | collective-permute-done | bytes 98336 | tf_op jit(solution)/shard_map/ppermute | solution.py:131
  25.0 0.0 collective-permute-done.2.refs_3_
  25.0 1.1 %temporal.1 = (bf16[2,64,128]{2,1,0:T(8,128)(2,1)S(1)}, bf16[2,64,128]{2,1,0:T(8,128)(2,1)S(1)}, bf16[2,64,128]{2,1,0:T(8,128)(2,1)S(1)}, bf16[2,64,128]{2,1,0:T(8,128)(2,1)S(1)}) custom-call(bf16[3,2,64,128]{3,2,1,0:T(8,128)(2,1)S(1)} %get-tuple-element.14.refs_0_, bf16[3,2,64,128]{3,2,1,0:T(8,128)(2,1)S(1)} %collective-permute-done.refs_1_, ...), custom_call_target="tpu_custom_call" | custom-call | tf_op jit(solution)/shard_map/temporal/pallas_call | solution.py:161
  26.1 2.0 %collective-permute-start.3 = (bf16[2,64,128]{2,1,0:T(8,128)(2,1)S(1)}, bf16[2,64,128]{2,1,0:T(8,128)(2,1)S(1)}, u32[]{:S(2)}, u32[]{:S(2)}) collective-permute-start(bf16[2,64,128]{2,1,0:T(8,128)(2,1)S(1)} %get-tuple-element.19), channel_id=1, source_target_pairs={{4,0},{0,4},{12,8},{8,12},{5,1},{1,5},{13,9},{9,13},{6,2},{2,6},{1... | collective-permute-start | bytes 98312 | tf_op jit(solution)/shard_map/ppermute | solution.py:131
  28.1 1.1 %collective-permute-start.4 = (bf16[2,64,128]{2,1,0:T(8,128)(2,1)S(1)}, bf16[2,64,128]{2,1,0:T(8,128)(2,1)S(1)}, u32[]{:S(2)}, u32[]{:S(2)}) collective-permute-start(bf16[2,64,128]{2,1,0:T(8,128)(2,1)S(1)} %get-tuple-element.20), channel_id=1, source_target_pairs={{8,0},{12,4},{0,8},{4,12},{9,1},{13,5},{1,9},{5,13},{10,2},{14,6},... | collective-permute-start | bytes 98312 | tf_op jit(solution)/shard_map/ppermute | solution.py:131
  29.3 1.4 %collective-permute-start.5 = (bf16[2,64,128]{2,1,0:T(8,128)(2,1)S(1)}, bf16[2,64,128]{2,1,0:T(8,128)(2,1)S(1)}, u32[]{:S(2)}, u32[]{:S(2)}) collective-permute-start(bf16[2,64,128]{2,1,0:T(8,128)(2,1)S(1)} %get-tuple-element.21), channel_id=1, source_target_pairs={{12,0},{8,4},{4,8},{0,12},{13,1},{9,5},{5,9},{1,13},{14,2},{10,6},... | collective-permute-start | bytes 98312 | tf_op jit(solution)/shard_map/ppermute | solution.py:131
  30.7 0.0 collective-permute-done.7.refs_2_
  30.7 0.0 collective-permute-done.8.refs_3_
  30.7 0.0 copy-done.1
  30.7 1.9 %spatial.1.refs_4_ = bf16[2,256,256]{2,1,0:T(8,128)(2,1)} custom-call(bf16[2,256,256]{2,1,0:T(8,128)(2,1)S(1)} %copy-done.1, bf16[2,2,256,128]{3,2,1,0:T(8,128)(2,1)S(1)} %get-tuple-element.22.refs_0_, bf16[2,2,256,128]{3,2,1,0:T(8,128)(2,1)S(1)} %collective-permute-done.6.refs_1_, bf16[2,2,256,128]{3,2,1,0:T(8,128)(2,1)S(1)} %collective-permute-done.7.refs_2_, ...), custom_call_target="tpu_custom_call" | custom-call | tf_op jit(solution)/shard_map/spatial/pallas_call | solution.py:147
  32.6 0.0 collective-permute-done.3.refs_1_
  32.6 1.0 %collective-permute-done.4.refs_2_ = bf16[2,64,128]{2,1,0:T(8,128)(2,1)S(1)} collective-permute-done((bf16[2,64,128]{2,1,0:T(8,128)(2,1)S(1)}, bf16[2,64,128]{2,1,0:T(8,128)(2,1)S(1)}, u32[]{:S(2)}, u32[]{:S(2)}) %collective-permute-start.4) | collective-permute-done | bytes 32800 | tf_op jit(solution)/shard_map/ppermute | solution.py:131
  33.6 1.4 %collective-permute-done.5.refs_3_ = bf16[2,64,128]{2,1,0:T(8,128)(2,1)S(1)} collective-permute-done((bf16[2,64,128]{2,1,0:T(8,128)(2,1)S(1)}, bf16[2,64,128]{2,1,0:T(8,128)(2,1)S(1)}, u32[]{:S(2)}, u32[]{:S(2)}) %collective-permute-start.5) | collective-permute-done | bytes 32800 | tf_op jit(solution)/shard_map/ppermute | solution.py:131
  35.0 0.7 %join.1 = bf16[2,256,256]{2,1,0:T(8,128)(2,1)} custom-call(bf16[2,64,128]{2,1,0:T(8,128)(2,1)S(1)} %get-tuple-element.18.refs_0_, bf16[2,64,128]{2,1,0:T(8,128)(2,1)S(1)} %collective-permute-done.3.refs_1_, bf16[2,64,128]{2,1,0:T(8,128)(2,1)S(1)} %collective-permute-done.4.refs_2_, ...), custom_call_target="tpu_custom_call", output_to_operand_aliasing={{}: (4, {})} | custom-call | tf_op jit(solution)/shard_map/join/pallas_call | solution.py:174
Async XLA Ops:
  0.0 0.9 %copy-start = (bf16[2,256,256]{2,1,0:T(8,128)(2,1)S(1)}, bf16[2,256,256]{2,1,0:T(8,128)(2,1)}, u32[]{:S(2)}) copy-start(bf16[2,256,256]{2,1,0:T(8,128)(2,1)} %q_hbm.3) | copy-start | bytes 786436
  1.0 0.9 %copy-start.2 = (bf16[2,256,256]{2,1,0:T(8,128)(2,1)S(1)}, bf16[2,256,256]{2,1,0:T(8,128)(2,1)}, u32[]{:S(2)}) copy-start(bf16[2,256,256]{2,1,0:T(8,128)(2,1)} %k_hbm.1) | copy-start | bytes 786436
  1.9 0.9 %copy-start.3 = (bf16[2,256,256]{2,1,0:T(8,128)(2,1)S(1)}, bf16[2,256,256]{2,1,0:T(8,128)(2,1)}, u32[]{:S(2)}) copy-start(bf16[2,256,256]{2,1,0:T(8,128)(2,1)} %v_hbm.1) | copy-start | bytes 786436
  3.1 27.5 %copy-start.1 = (bf16[2,256,256]{2,1,0:T(8,128)(2,1)S(1)}, bf16[2,256,256]{2,1,0:T(8,128)(2,1)}, u32[]{:S(2)}) copy-start(bf16[2,256,256]{2,1,0:T(8,128)(2,1)} %q_hbm.3) | copy-start | bytes 786436
  3.1 9.3 %collective-permute-start.6 = (bf16[2,2,256,128]{3,2,1,0:T(8,128)(2,1)S(1)}, bf16[2,2,256,128]{3,2,1,0:T(8,128)(2,1)S(1)}, u32[]{:S(2)}, u32[]{:S(2)}) collective-permute-start(bf16[2,2,256,128]{3,2,1,0:T(8,128)(2,1)S(1)} %get-tuple-element.22.refs_0_), channel_id=1, source_target_pairs={{0,2},{2,0},{1,3},{3,1},{4,6},{6,4},{5,7},{7,5},{8,10},{10,8},{9,1... | collective-permute-start | bytes 786440 | tf_op jit(solution)/shard_map/ppermute | solution.py:141
  6.1 24.5 %collective-permute-start.7 = (bf16[2,2,256,128]{3,2,1,0:T(8,128)(2,1)S(1)}, bf16[2,2,256,128]{3,2,1,0:T(8,128)(2,1)S(1)}, u32[]{:S(2)}, u32[]{:S(2)}) collective-permute-start(bf16[2,2,256,128]{3,2,1,0:T(8,128)(2,1)S(1)} %get-tuple-element.22.refs_0_), channel_id=1, source_target_pairs={{0,1},{1,0},{2,3},{3,2},{4,5},{5,4},{6,7},{7,6},{8,9},{9,8},{10,11... | collective-permute-start | bytes 786440 | tf_op jit(solution)/shard_map/ppermute | solution.py:145
  12.5 18.2 %collective-permute-start.8 = (bf16[2,2,256,128]{3,2,1,0:T(8,128)(2,1)S(1)}, bf16[2,2,256,128]{3,2,1,0:T(8,128)(2,1)S(1)}, u32[]{:S(2)}, u32[]{:S(2)}) collective-permute-start(bf16[2,2,256,128]{3,2,1,0:T(8,128)(2,1)S(1)} %collective-permute-done.6.refs_1_), channel_id=1, source_target_pairs={{0,1},{1,0},{2,3},{3,2},{4,5},{5,4},{6,7},{7,6},{8,9},{9,8},{10,11... | collective-permute-start | bytes 786440 | tf_op jit(solution)/shard_map/ppermute | solution.py:145
  12.5 5.3 %collective-permute-start = (bf16[3,2,64,128]{3,2,1,0:T(8,128)(2,1)S(1)}, bf16[3,2,64,128]{3,2,1,0:T(8,128)(2,1)S(1)}, u32[]{:S(2)}, u32[]{:S(2)}) collective-permute-start(bf16[3,2,64,128]{3,2,1,0:T(8,128)(2,1)S(1)} %get-tuple-element.15), channel_id=1, source_target_pairs={{0,4},{4,0},{8,12},{12,8},{1,5},{5,1},{9,13},{13,9},{2,6},{6,2},{1... | collective-permute-start | bytes 294920 | tf_op jit(solution)/shard_map/ppermute | solution.py:131
  14.3 10.7 %collective-permute-start.1 = (bf16[3,2,64,128]{3,2,1,0:T(8,128)(2,1)S(1)}, bf16[3,2,64,128]{3,2,1,0:T(8,128)(2,1)S(1)}, u32[]{:S(2)}, u32[]{:S(2)}) collective-permute-start(bf16[3,2,64,128]{3,2,1,0:T(8,128)(2,1)S(1)} %get-tuple-element.16), channel_id=1, source_target_pairs={{0,8},{4,12},{8,0},{12,4},{1,9},{5,13},{9,1},{13,5},{2,10},{6,14},... | collective-permute-start | bytes 294920 | tf_op jit(solution)/shard_map/ppermute | solution.py:131
  16.9 8.2 %collective-permute-start.2 = (bf16[3,2,64,128]{3,2,1,0:T(8,128)(2,1)S(1)}, bf16[3,2,64,128]{3,2,1,0:T(8,128)(2,1)S(1)}, u32[]{:S(2)}, u32[]{:S(2)}) collective-permute-start(bf16[3,2,64,128]{3,2,1,0:T(8,128)(2,1)S(1)} %get-tuple-element.17), channel_id=1, source_target_pairs={{0,12},{4,8},{8,4},{12,0},{1,13},{5,9},{9,5},{13,1},{2,14},{6,10},... | collective-permute-start | bytes 294920 | tf_op jit(solution)/shard_map/ppermute | solution.py:131
  26.1 6.4 %collective-permute-start.3 = (bf16[2,64,128]{2,1,0:T(8,128)(2,1)S(1)}, bf16[2,64,128]{2,1,0:T(8,128)(2,1)S(1)}, u32[]{:S(2)}, u32[]{:S(2)}) collective-permute-start(bf16[2,64,128]{2,1,0:T(8,128)(2,1)S(1)} %get-tuple-element.19), channel_id=1, source_target_pairs={{4,0},{0,4},{12,8},{8,12},{5,1},{1,5},{13,9},{9,13},{6,2},{2,6},{1... | collective-permute-start | bytes 98312 | tf_op jit(solution)/shard_map/ppermute | solution.py:131
  28.1 5.5 %collective-permute-start.4 = (bf16[2,64,128]{2,1,0:T(8,128)(2,1)S(1)}, bf16[2,64,128]{2,1,0:T(8,128)(2,1)S(1)}, u32[]{:S(2)}, u32[]{:S(2)}) collective-permute-start(bf16[2,64,128]{2,1,0:T(8,128)(2,1)S(1)} %get-tuple-element.20), channel_id=1, source_target_pairs={{8,0},{12,4},{0,8},{4,12},{9,1},{13,5},{1,9},{5,13},{10,2},{14,6},... | collective-permute-start | bytes 98312 | tf_op jit(solution)/shard_map/ppermute | solution.py:131
  29.3 5.7 %collective-permute-start.5 = (bf16[2,64,128]{2,1,0:T(8,128)(2,1)S(1)}, bf16[2,64,128]{2,1,0:T(8,128)(2,1)S(1)}, u32[]{:S(2)}, u32[]{:S(2)}) collective-permute-start(bf16[2,64,128]{2,1,0:T(8,128)(2,1)S(1)} %get-tuple-element.21), channel_id=1, source_target_pairs={{12,0},{8,4},{4,8},{0,12},{13,1},{9,5},{5,9},{1,13},{14,2},{10,6},... | collective-permute-start | bytes 98312 | tf_op jit(solution)/shard_map/ppermute | solution.py:131

commit v2 on v1

v2 whole, which is shorter than its diff:
```python
import functools
import math

import jax
import jax.numpy as jnp
from jax import lax
from jax.experimental import pallas as pl
from jax.experimental.pallas import tpu as pltpu
from jax.sharding import PartitionSpec as P

STRIP = 16
VMEM_LIMIT = 16 * 1024 * 1024


def partner_of(index, step, count):
    if count & (count - 1) == 0:
        return index ^ step
    return (index + step) % count


def run_copies(copies, sems):
    started = [pltpu.make_async_copy(src, dst, sems.at[n]) for n, (src, dst) in enumerate(copies)]
    for copy in started:
        copy.start()
    for copy in started:
        copy.wait()


def prep_kernel(team, head_width, q_hbm, k_hbm, v_hbm, *refs):
    pairs, triples, refs = refs[:team], refs[team : 2 * team - 1], refs[2 * team - 1 :]
    q_own, kv_ref, q_spatial, sems = refs
    member = lax.axis_index("frame") % team
    rows = q_own.shape[1]
    starts = [pl.multiple_of((member + step) % team * rows, rows) for step in range(team)]

    def cut(array, step):
        return array.at[:, pl.ds(starts[step], rows), head_width:]

    copies = []
    for step in range(team):
        copies += [(cut(k_hbm, step), pairs[step].at[0]), (cut(v_hbm, step), pairs[step].at[1])]
    for step in range(1, team):
        copies += [
            (cut(array, step), triples[step - 1].at[which])
            for which, array in enumerate((k_hbm, v_hbm, q_hbm))
        ]
    copies.append((cut(q_hbm, 0), q_own))
    for which, array in enumerate((k_hbm, v_hbm)):
        copies.append((array.at[:, :, :head_width], kv_ref.at[which]))
    copies.append((q_hbm.at[:, :, :head_width], q_spatial))
    run_copies(copies, sems)


def score(query_rows, key_rows, score_scale):
    product = lax.dot_general(
        query_rows, key_rows, (((1,), (1,)), ((), ())), preferred_element_type=jnp.float32
    )
    return product * score_scale


def mix(expo, value_rows):
    return jnp.dot(expo.astype(jnp.bfloat16), value_rows, preferred_element_type=jnp.float32)


def temporal_kernel(team, count, passed, score_scale, *refs):
    own, own_query, mates, others = refs[0], refs[1], refs[2 : 1 + team], refs[1 + team : 1 + count]
    outs = refs[1 + count + passed : 1 + count + passed + team]
    frames_dev, rows = own_query.shape[:2]
    cuts = [slice(lower, lower + STRIP) for lower in range(0, rows, STRIP)]

    def gather(parts, cut):
        return jnp.concatenate([part[f, cut] for part in parts for f in range(frames_dev)])

    blocks = [own, *mates, *others]
    queries = [gather([own_query, *(m.at[2] for m in mates)], cut) for cut in cuts]
    keys = [gather([b.at[0] for b in blocks], cut) for cut in cuts]
    values = [gather([b.at[1] for b in blocks], cut) for cut in cuts]
    scores = [score(q, k, score_scale) for q, k in zip(queries, keys)]
    highest = [jnp.max(s, axis=-1, keepdims=True) for s in scores]
    expo = [jnp.exp(s - h) for s, h in zip(scores, highest)]
    totals = [jnp.sum(e, axis=-1, keepdims=True) for e in expo]
    mixed = [mix(e, v) for e, v in zip(expo, values)]
    results = [(m / t).astype(jnp.bfloat16) for m, t in zip(mixed, totals)]
    for cut, result in zip(cuts, results):
        for number, ref in enumerate(outs):
            for frame in range(frames_dev):
                lower = (number * frames_dev + frame) * STRIP
                ref[frame, cut] = result[lower : lower + STRIP]


def first_kernel(score_scale, pieces, q_ref, *refs):
    kvs, (top_ref, total_ref, acc_ref) = refs[:pieces], refs[pieces:]
    for frame in range(q_ref.shape[0]):
        key = jnp.concatenate([kv[0, frame] for kv in kvs])
        value = jnp.concatenate([kv[1, frame] for kv in kvs])
        scores = score(q_ref[frame], key, score_scale)
        highest = jnp.max(scores, axis=-1, keepdims=True)
        expo = jnp.exp(scores - highest)
        top_ref[frame] = highest
        total_ref[frame] = jnp.sum(expo, axis=-1, keepdims=True)
        acc_ref[frame] = mix(expo, value)


def last_kernel(score_scale, pieces, q_ref, *refs):
    kvs, (top_ref, total_ref, acc_ref, out_hbm, o_ref, sems) = refs[:pieces], refs[pieces:]
    head_width = q_ref.shape[-1]
    for frame in range(q_ref.shape[0]):
        key = jnp.concatenate([kv[0, frame] for kv in kvs])
        value = jnp.concatenate([kv[1, frame] for kv in kvs])
        scores = score(q_ref[frame], key, score_scale)
        highest = jnp.maximum(top_ref[frame], jnp.max(scores, axis=-1, keepdims=True))
        expo = jnp.exp(scores - highest)
        factor = jnp.exp(top_ref[frame] - highest)
        total = total_ref[frame] * factor + jnp.sum(expo, axis=-1, keepdims=True)
        o_ref[frame] = ((acc_ref[frame] * factor + mix(expo, value)) / total).astype(jnp.bfloat16)
    run_copies([(o_ref, out_hbm.at[:, :, :head_width])], sems)


def join_kernel(team, head_width, *refs):
    pieces, out_hbm, sems = refs[:team], refs[team + 1], refs[team + 2]
    member = lax.axis_index("frame") % team
    rows = pieces[0].shape[1]
    copies = []
    for step, piece in enumerate(pieces):
        start = pl.multiple_of((member + step) % team * rows, rows)
        copies.append((piece, out_hbm.at[:, pl.ds(start, rows), head_width:]))
    run_copies(copies, sems)


def body(queries, keys, values):
    frames_dev, tokens_dev, width = queries.shape
    head_width = width // 2
    score_scale = 1.0 / math.sqrt(head_width)
    count = lax.axis_size("frame")
    team = 2 if count & (count - 1) == 0 and count > 1 else 1
    rows = tokens_dev // team
    dtype = queries.dtype
    hbm = pl.BlockSpec(memory_space=pltpu.HBM)
    vmem = pl.BlockSpec(memory_space=pltpu.VMEM)
    anywhere = pl.BlockSpec(memory_space=pl.ANY)

    def call(kernel, name, **rest):
        return pl.pallas_call(
            kernel,
            name=name,
            compiler_params=pltpu.CompilerParams(vmem_limit_bytes=VMEM_LIMIT),
            cost_estimate=pl.CostEstimate(flops=1, bytes_accessed=1, transcendentals=0),
            **rest,
        )

    def in_vmem(*shape, of=dtype):
        return pltpu.VMEM(shape, of)

    pair, triple = ((size, frames_dev, rows, head_width) for size in (2, 3))
    whole = (frames_dev, tokens_dev, head_width)
    cut = call(
        functools.partial(prep_kernel, team, head_width),
        "prep",
        out_shape=[in_vmem(*pair)] * team
        + [in_vmem(*triple)] * (team - 1)
        + [in_vmem(*pair[1:]), in_vmem(2, *whole), in_vmem(*whole)],
        in_specs=[hbm] * 3,
        out_specs=[vmem] * (2 * team + 2),
        scratch_shapes=[pltpu.SemaphoreType.DMA((5 * team + 1,))],
    )(*(pltpu.with_memory_space_constraint(array, pltpu.HBM) for array in (queries, keys, values)))
    pairs, triples, (query_own, kv_own, query_spatial) = cut[:team], cut[team:-3], cut[-3:]

    def exchange(array, axis, step):
        size = lax.axis_size(axis)
        return lax.ppermute(array, axis, [(i, partner_of(i, step, size)) for i in range(size)])

    subs, quarters = lax.axis_size("sub"), lax.axis_size("quarter")
    others = [exchange(pairs[step % team], "frame", step) for step in range(team, count)]
    across = [exchange(kv_own, "quarter", step) for step in range(1, quarters)]
    near = [exchange(kv_own, "sub", step) for step in range(1, subs)]
    mates = [exchange(triples[step - 1], "frame", step) for step in range(1, team)]

    early = [kv_own, *near]
    state = [in_vmem(*whole[:2], size, of=jnp.float32) for size in (1, 1, head_width)]
    running = call(
        functools.partial(first_kernel, score_scale, len(early)),
        "first",
        out_shape=state,
        in_specs=[vmem] * (1 + len(early)),
        out_specs=[vmem] * 3,
    )(query_spatial, *early)

    passed = len(across)
    *strip_out, = call(
        functools.partial(temporal_kernel, team, count, passed, score_scale),
        "temporal",
        out_shape=[in_vmem(*pair[1:])] * team + [in_vmem(*kv_own.shape)] * passed,
        in_specs=[vmem] * (1 + count) + [anywhere] * passed,
        out_specs=[vmem] * team + [anywhere] * passed,
        input_output_aliases={1 + count + n: team + n for n in range(passed)},
    )(pairs[0], query_own, *mates, *others, *across)
    strip_out, across = strip_out[:team], strip_out[team:]
    far = [exchange(piece, "sub", step) for piece in across for step in range(1, subs)]
    returned = strip_out[:1] + [exchange(strip_out[step], "frame", step) for step in range(1, team)]

    late = [*across, *far]
    out = call(
        functools.partial(last_kernel, score_scale, len(late)),
        "last",
        out_shape=jax.ShapeDtypeStruct(queries.shape, dtype),
        in_specs=[vmem] * (4 + len(late)),
        out_specs=hbm,
        scratch_shapes=[pltpu.VMEM(whole, dtype), pltpu.SemaphoreType.DMA((1,))],
    )(query_spatial, *late, *running)

    return call(
        functools.partial(join_kernel, team, head_width),
        "join",
        out_shape=jax.ShapeDtypeStruct(queries.shape, dtype),
        in_specs=[vmem] * team + [hbm],
        out_specs=hbm,
        scratch_shapes=[pltpu.SemaphoreType.DMA((team,))],
        input_output_aliases={team: 0},
    )(*returned, out)


def solution(mesh):
    spec = P(("groups", "frame"), ("quarter", "sub"), None)
    return jax.shard_map(
        body, mesh=mesh, in_specs=(spec,) * 3, out_specs=spec, check_vma=False
    )
```

time: 35.9 us -> 25.8 us (0.72)
  starting transfers between devices: 12 us -> 7.32 us
  waiting for transfers between devices: 16.9 us -> 13.4 us
  local copies, waits for them, and re-layouts: 2.85 us -> 0 us
  Pallas kernels: 3.9 us -> 4.95 us
    ppermute x9 -> x7, starting transfers between devices: 12 us -> 7.32 us  [exchange(): lax.ppermute(array, axis, [(i, partner_of(i, step, size)) for i in range(...]
    ppermute x9 -> x7, waiting for transfers between devices: 16.9 us -> 13.4 us  [exchange(): lax.ppermute(array, axis, [(i, partner_of(i, step, size)) for i in range(...]
    unnamed x8 -> x0, local copies, waits for them, and re-layouts: 2.85 us -> none
    pallas_call x4 -> x5, Pallas kernels: 3.9 us -> 4.95 us  [the longest x1 1.65 us: body(): call(functools.partial(last_kernel, score_scale, len(late)), 'last', out_...]
  transfers between devices with their start and end apart: 9 -> 7, of which waited for: 5 -> 4; matrix products, arithmetic and copies ran while one was open for 0% -> 0% of each run, Pallas kernels for 8% -> 11%
where the time goes in v2:
time: 25.8 us; the launch traced here: 25.7 us
  waiting for transfers between devices  13.4 us (52%)
  starting transfers between devices  7.32 us (28%)
  Pallas kernels  4.95 us (19%)
    ppermute x7, waiting for transfers between devices, exchange(): lax.ppermute(array, axis, [(i, partner_of(i, step, size)) for i in range(...  13.4 us
    ppermute x7, starting transfers between devices, exchange(): lax.ppermute(array, axis, [(i, partner_of(i, step, size)) for i in range(...  7.32 us
    pallas_call x1, Pallas kernels, body(): call(functools.partial(last_kernel, score_scale, len(late)), 'last', out_...  1.65 us
    pallas_call x1, Pallas kernels, body(): call(functools.partial(prep_kernel, team, head_width), 'prep', out_shape=...  1.35 us
    pallas_call x1, Pallas kernels, body(): call(functools.partial(first_kernel, score_scale, len(early)), 'first', o...  0.77 us
    pallas_call x1, Pallas kernels, body(): call(functools.partial(join_kernel, team, head_width), 'join', out_shape=...  0.67 us
  transfers between devices with their start and end apart: 7, of which 4 were waited for; matrix products, arithmetic and copies ran while one was open for 0% of the time, Pallas kernels for 11%

profile of v2, /device:TPU:0, one launch (start us, length us, event | category | flops | bytes accessed | tf_op | source)
XLA Modules:
  0.0 25.7 jit_solution(4383782027261239632)
XLA Ops:
  0.0 1.3 %prep.1 = (bf16[2,2,128,128]{3,2,1,0:T(8,128)(2,1)S(1)}, bf16[2,2,128,128]{3,2,1,0:T(8,128)(2,1)S(1)}, bf16[3,2,128,128]{3,2,1,0:T(8,128)(2,1)S(1)}, bf16[2,128,...) custom-call(bf16[2,256,256]{2,1,0:T(8,128)(2,1)} %q_hbm.1, ...), custom_call_target="tpu_custom_call" | custom-call | flops 1 | bytes 1 | tf_op jit(solution)/shard_map/prep/pallas_call | solution.py:156
  1.4 3.0 %collective-permute-start.3 = (bf16[2,2,256,128]{3,2,1,0:T(8,128)(2,1)S(1)}, bf16[2,2,256,128]{3,2,1,0:T(8,128)(2,1)S(1)}, u32[]{:S(2)}, u32[]{:S(2)}) collective-permute-start(bf16[2,2,256,128]{3,2,1,0:T(8,128)(2,1)S(1)} %get-tuple-element.21.refs_0_), channel_id=1, source_target_pairs={{0,2},{2,0},{1,3},{3,1},{4,6},{6,4},{5,7},{7,5},{8,10},{10,8},{9,1... | collective-permute-start | bytes 786440 | tf_op jit(solution)/shard_map/ppermute | solution.py:170
  4.4 1.6 %collective-permute-start = (bf16[3,2,128,128]{3,2,1,0:T(8,128)(2,1)S(1)}, bf16[3,2,128,128]{3,2,1,0:T(8,128)(2,1)S(1)}, u32[]{:S(2)}, u32[]{:S(2)}) collective-permute-start(bf16[3,2,128,128]{3,2,1,0:T(8,128)(2,1)S(1)} %get-tuple-element.19), channel_id=1, source_target_pairs={{0,4},{4,0},{8,12},{12,8},{1,5},{5,1},{9,13},{13,9},{2,6},{6,2},{1... | collective-permute-start | bytes 589832 | tf_op jit(solution)/shard_map/ppermute | solution.py:170
  5.9 2.5 %collective-permute-start.2 = (bf16[2,2,128,128]{3,2,1,0:T(8,128)(2,1)S(1)}, bf16[2,2,128,128]{3,2,1,0:T(8,128)(2,1)S(1)}, u32[]{:S(2)}, u32[]{:S(2)}) collective-permute-start(bf16[2,2,128,128]{3,2,1,0:T(8,128)(2,1)S(1)} %get-tuple-element.20), channel_id=1, source_target_pairs={{0,12},{4,8},{8,4},{12,0},{1,13},{5,9},{9,5},{13,1},{2,14},{6,10},... | collective-permute-start | bytes 393224 | tf_op jit(solution)/shard_map/ppermute | solution.py:170
  8.4 0.1 collective-permute-start.1
  8.5 0.0 collective-permute-start.6
  8.5 8.5 %collective-permute-done.2.refs_4_ = bf16[2,2,128,128]{3,2,1,0:T(8,128)(2,1)S(1)} collective-permute-done((bf16[2,2,128,128]{3,2,1,0:T(8,128)(2,1)S(1)}, bf16[2,2,128,128]{3,2,1,0:T(8,128)(2,1)S(1)}, u32[]{:S(2)}, u32[]{:S(2)}) %collective-permute-start.2) | collective-permute-done | bytes 131104 | tf_op jit(solution)/shard_map/ppermute | solution.py:170
  17.1 2.8 %collective-permute-done.1.refs_3_ = bf16[2,2,128,128]{3,2,1,0:T(8,128)(2,1)S(1)} collective-permute-done((bf16[2,2,128,128]{3,2,1,0:T(8,128)(2,1)S(1)}, bf16[2,2,128,128]{3,2,1,0:T(8,128)(2,1)S(1)}, u32[]{:S(2)}, u32[]{:S(2)}) %collective-permute-start.1) | collective-permute-done | bytes 131104 | tf_op jit(solution)/shard_map/ppermute | solution.py:170
  19.9 0.0 collective-permute-done.refs_2_
  19.9 0.0 collective-permute-done.3.refs_5_
  19.9 0.5 %temporal.1 = (bf16[2,128,128]{2,1,0:T(8,128)(2,1)S(1)}, bf16[2,128,128]{2,1,0:T(8,128)(2,1)S(1)}, bf16[2,2,256,128]{3,2,1,0:T(8,128)(2,1)S(1)}) custom-call(bf16[2,2,128,128]{3,2,1,0:T(8,128)(2,1)S(1)} %get-tuple-element.17.refs_0_, bf16[2,128,128]{2,1,0:T(8,128)(2,1)S(1)} %get-tuple-element.18.refs_1_, ...), custom_call_target="tpu_custom_call", output_to_operand_aliasing={{2}: (5, {})} | custom-call | flops 1 | bytes 1 | tf_op jit(solution)/shard_map/temporal/pallas_call | solution.py:189
  20.4 0.1 collective-permute-start.5
  20.5 0.1 collective-permute-start.4
  20.6 0.0 collective-permute-done.6.refs_1_
  20.6 0.8 %first.1 = (f32[2,256,1]{2,1,0:T(8,128)S(1)}, f32[2,256,1]{2,1,0:T(8,128)S(1)}, f32[2,256,128]{2,1,0:T(8,128)S(1)}) custom-call(bf16[2,256,128]{2,1,0:T(8,128)(2,1)S(1)} %get-tuple-element.24.q_ref, bf16[2,2,256,128]{3,2,1,0:T(8,128)(2,1)S(1)} %get-tuple-element.21.refs_0_, bf16[2,2,256,128]{3,2,1,0:T(8,128)(2,1)S(1)} %collective-permute-done.6.refs_1_), custom_call_target="tpu_custom_call" | custom-call | flops 1 | bytes 1 | tf_op jit(solution)/shard_map/first/pallas_call | solution.py:180
  21.4 0.7 %collective-permute-done.5.refs_1_ = bf16[2,2,256,128]{3,2,1,0:T(8,128)(2,1)S(1)} collective-permute-done((bf16[2,2,256,128]{3,2,1,0:T(8,128)(2,1)S(1)}, bf16[2,2,256,128]{3,2,1,0:T(8,128)(2,1)S(1)}, u32[]{:S(2)}, u32[]{:S(2)}) %collective-permute-start.5) | collective-permute-done | bytes 262176 | tf_op jit(solution)/shard_map/ppermute | solution.py:170
  22.0 1.6 %last.1.refs_2_ = bf16[2,256,256]{2,1,0:T(8,128)(2,1)} custom-call(bf16[2,256,128]{2,1,0:T(8,128)(2,1)S(1)} %get-tuple-element.24.q_ref, bf16[2,2,256,128]{3,2,1,0:T(8,128)(2,1)S(1)} %get-tuple-element.25.refs_0_, bf16[2,2,256,128]{3,2,1,0:T(8,128)(2,1)S(1)} %collective-permute-done.5.refs_1_, f32[2,256,1]{2,1,0:T(8,128)S(1)} %get-tuple-element.26.refs_2_, ...), custom_call_target="tpu_custom_call" | custom-call | flops 1 | bytes 1 | tf_op jit(solution)/shard_map/last/pallas_call | solution.py:202
  23.7 1.3 %collective-permute-done.4.refs_1_ = bf16[2,128,128]{2,1,0:T(8,128)(2,1)S(1)} collective-permute-done((bf16[2,128,128]{2,1,0:T(8,128)(2,1)S(1)}, bf16[2,128,128]{2,1,0:T(8,128)(2,1)S(1)}, u32[]{:S(2)}, u32[]{:S(2)}) %collective-permute-start.4) | collective-permute-done | bytes 65568 | tf_op jit(solution)/shard_map/ppermute | solution.py:170
  25.0 0.7 %join.1 = bf16[2,256,256]{2,1,0:T(8,128)(2,1)} custom-call(bf16[2,128,128]{2,1,0:T(8,128)(2,1)S(1)} %get-tuple-element.22.refs_0_, bf16[2,128,128]{2,1,0:T(8,128)(2,1)S(1)} %collective-permute-done.4.refs_1_, bf16[2,256,256]{2,1,0:T(8,128)(2,1)} %last.1.refs_2_), custom_call_target="tpu_custom_call", output_to_operand_aliasing={{}: (2, {})} | custom-call | flops 1 | bytes 1 | tf_op jit(solution)/shard_map/join/pallas_call | solution.py:211
Async XLA Ops:
  1.4 18.5 %collective-permute-start.3 = (bf16[2,2,256,128]{3,2,1,0:T(8,128)(2,1)S(1)}, bf16[2,2,256,128]{3,2,1,0:T(8,128)(2,1)S(1)}, u32[]{:S(2)}, u32[]{:S(2)}) collective-permute-start(bf16[2,2,256,128]{3,2,1,0:T(8,128)(2,1)S(1)} %get-tuple-element.21.refs_0_), channel_id=1, source_target_pairs={{0,2},{2,0},{1,3},{3,1},{4,6},{6,4},{5,7},{7,5},{8,10},{10,8},{9,1... | collective-permute-start | bytes 786440 | tf_op jit(solution)/shard_map/ppermute | solution.py:170
  4.4 15.5 %collective-permute-start = (bf16[3,2,128,128]{3,2,1,0:T(8,128)(2,1)S(1)}, bf16[3,2,128,128]{3,2,1,0:T(8,128)(2,1)S(1)}, u32[]{:S(2)}, u32[]{:S(2)}) collective-permute-start(bf16[3,2,128,128]{3,2,1,0:T(8,128)(2,1)S(1)} %get-tuple-element.19), channel_id=1, source_target_pairs={{0,4},{4,0},{8,12},{12,8},{1,5},{5,1},{9,13},{13,9},{2,6},{6,2},{1... | collective-permute-start | bytes 589832 | tf_op jit(solution)/shard_map/ppermute | solution.py:170
  5.9 11.1 %collective-permute-start.2 = (bf16[2,2,128,128]{3,2,1,0:T(8,128)(2,1)S(1)}, bf16[2,2,128,128]{3,2,1,0:T(8,128)(2,1)S(1)}, u32[]{:S(2)}, u32[]{:S(2)}) collective-permute-start(bf16[2,2,128,128]{3,2,1,0:T(8,128)(2,1)S(1)} %get-tuple-element.20), channel_id=1, source_target_pairs={{0,12},{4,8},{8,4},{12,0},{1,13},{5,9},{9,5},{13,1},{2,14},{6,10},... | collective-permute-start | bytes 393224 | tf_op jit(solution)/shard_map/ppermute | solution.py:170
  8.4 11.5 %collective-permute-start.1 = (bf16[2,2,128,128]{3,2,1,0:T(8,128)(2,1)S(1)}, bf16[2,2,128,128]{3,2,1,0:T(8,128)(2,1)S(1)}, u32[]{:S(2)}, u32[]{:S(2)}) collective-permute-start(bf16[2,2,128,128]{3,2,1,0:T(8,128)(2,1)S(1)} %get-tuple-element.17.refs_0_), channel_id=1, source_target_pairs={{0,8},{4,12},{8,0},{12,4},{1,9},{5,13},{9,1},{13,5},{2,10},{6,14},... | collective-permute-start | bytes 393224 | tf_op jit(solution)/shard_map/ppermute | solution.py:170
  8.5 12.1 %collective-permute-start.6 = (bf16[2,2,256,128]{3,2,1,0:T(8,128)(2,1)S(1)}, bf16[2,2,256,128]{3,2,1,0:T(8,128)(2,1)S(1)}, u32[]{:S(2)}, u32[]{:S(2)}) collective-permute-start(bf16[2,2,256,128]{3,2,1,0:T(8,128)(2,1)S(1)} %get-tuple-element.21.refs_0_), channel_id=1, source_target_pairs={{0,1},{1,0},{2,3},{3,2},{4,5},{5,4},{6,7},{7,6},{8,9},{9,8},{10,11... | collective-permute-start | bytes 786440 | tf_op jit(solution)/shard_map/ppermute | solution.py:170
  20.4 1.6 %collective-permute-start.5 = (bf16[2,2,256,128]{3,2,1,0:T(8,128)(2,1)S(1)}, bf16[2,2,256,128]{3,2,1,0:T(8,128)(2,1)S(1)}, u32[]{:S(2)}, u32[]{:S(2)}) collective-permute-start(bf16[2,2,256,128]{3,2,1,0:T(8,128)(2,1)S(1)} %get-tuple-element.25.refs_0_), channel_id=1, source_target_pairs={{0,1},{1,0},{2,3},{3,2},{4,5},{5,4},{6,7},{7,6},{8,9},{9,8},{10,11... | collective-permute-start | bytes 786440 | tf_op jit(solution)/shard_map/ppermute | solution.py:170
  20.5 4.5 %collective-permute-start.4 = (bf16[2,128,128]{2,1,0:T(8,128)(2,1)S(1)}, bf16[2,128,128]{2,1,0:T(8,128)(2,1)S(1)}, u32[]{:S(2)}, u32[]{:S(2)}) collective-permute-start(bf16[2,128,128]{2,1,0:T(8,128)(2,1)S(1)} %get-tuple-element.23), channel_id=1, source_target_pairs={{0,4},{4,0},{8,12},{12,8},{1,5},{5,1},{9,13},{13,9},{2,6},{6,2},{1... | collective-permute-start | bytes 196616 | tf_op jit(solution)/shard_map/ppermute | solution.py:170

commit v3 on v2

--- a/solution.py
+++ b/solution.py
@@ -64,7 +64,7 @@
 
 def temporal_kernel(team, count, passed, score_scale, *refs):
     own, own_query, mates, others = refs[0], refs[1], refs[2 : 1 + team], refs[1 + team : 1 + count]
-    outs = refs[1 + count + passed : 1 + count + passed + team]
+    outs = refs[1 + count + passed :][:team]
     frames_dev, rows = own_query.shape[:2]
     cuts = [slice(lower, lower + STRIP) for lower in range(0, rows, STRIP)]
 
@@ -139,12 +139,12 @@
     vmem = pl.BlockSpec(memory_space=pltpu.VMEM)
     anywhere = pl.BlockSpec(memory_space=pl.ANY)
 
-    def call(kernel, name, **rest):
+    def call(kernel, name, flops=1, **rest):
         return pl.pallas_call(
             kernel,
             name=name,
             compiler_params=pltpu.CompilerParams(vmem_limit_bytes=VMEM_LIMIT),
-            cost_estimate=pl.CostEstimate(flops=1, bytes_accessed=1, transcendentals=0),
+            cost_estimate=pl.CostEstimate(flops=flops, bytes_accessed=1, transcendentals=0),
             **rest,
         )
 
@@ -165,17 +165,43 @@
     )(*(pltpu.with_memory_space_constraint(array, pltpu.HBM) for array in (queries, keys, values)))
     pairs, triples, (query_own, kv_own, query_spatial) = cut[:team], cut[team:-3], cut[-3:]
 
+    def hold(arrays, flops):
+        return call(
+            lambda *refs: None,
+            "hold",
+            flops=flops,
+            out_shape=[in_vmem(*array.shape) for array in arrays],
+            in_specs=[anywhere] * len(arrays),
+            out_specs=[anywhere] * len(arrays),
+            input_output_aliases={n: n for n in range(len(arrays))},
+        )(*arrays)
+
     def exchange(array, axis, step):
         size = lax.axis_size(axis)
         return lax.ppermute(array, axis, [(i, partner_of(i, step, size)) for i in range(size)])
 
+    others = [exchange(pairs[step % team], "frame", step) for step in range(team, count)]
+    others = hold(others, 1000 * 10**6)
+    mates = [exchange(triples[step - 1], "frame", step) for step in range(1, team)]
+    held = hold([*mates, *others], 1000 * 10**6)
+    mates, others = held[: team - 1], held[team - 1 :]
     subs, quarters = lax.axis_size("sub"), lax.axis_size("quarter")
-    others = [exchange(pairs[step % team], "frame", step) for step in range(team, count)]
+    near = [exchange(kv_own, "sub", step) for step in range(1, subs)]
     across = [exchange(kv_own, "quarter", step) for step in range(1, quarters)]
-    near = [exchange(kv_own, "sub", step) for step in range(1, subs)]
-    mates = [exchange(triples[step - 1], "frame", step) for step in range(1, team)]
-
-    early = [kv_own, *near]
+
+    strip_out = call(
+        functools.partial(temporal_kernel, team, count, len(across), score_scale),
+        "temporal",
+        out_shape=[in_vmem(*pair[1:])] * team + [in_vmem(*kv_own.shape)] * len(across),
+        in_specs=[vmem] * (1 + count) + [anywhere] * len(across),
+        out_specs=[vmem] * team + [anywhere] * len(across),
+        input_output_aliases={1 + count + n: team + n for n in range(len(across))},
+    )(pairs[0], query_own, *mates, *others, *across)
+    strip_out, across = strip_out[:team], strip_out[team:]
+    returned = [exchange(strip_out[step], "frame", step) for step in range(1, team)]
+    late = [exchange(piece, "sub", step) for step in range(1, subs) for piece in across]
+
+    early = [kv_own, *near, *across]
     state = [in_vmem(*whole[:2], size, of=jnp.float32) for size in (1, 1, head_width)]
     running = call(
         functools.partial(first_kernel, score_scale, len(early)),
@@ -185,20 +211,6 @@
         out_specs=[vmem] * 3,
     )(query_spatial, *early)
 
-    passed = len(across)
-    *strip_out, = call(
-        functools.partial(temporal_kernel, team, count, passed, score_scale),
-        "temporal",
-        out_shape=[in_vmem(*pair[1:])] * team + [in_vmem(*kv_own.shape)] * passed,
-        in_specs=[vmem] * (1 + count) + [anywhere] * passed,
-        out_specs=[vmem] * team + [anywhere] * passed,
-        input_output_aliases={1 + count + n: team + n for n in range(passed)},
-    )(pairs[0], query_own, *mates, *others, *across)
-    strip_out, across = strip_out[:team], strip_out[team:]
-    far = [exchange(piece, "sub", step) for piece in across for step in range(1, subs)]
-    returned = strip_out[:1] + [exchange(strip_out[step], "frame", step) for step in range(1, team)]
-
-    late = [*across, *far]
     out = call(
         functools.partial(last_kernel, score_scale, len(late)),
         "last",
@@ -216,7 +228,7 @@
         out_specs=hbm,
         scratch_shapes=[pltpu.SemaphoreType.DMA((team,))],
         input_output_aliases={team: 0},
-    )(*returned, out)
+    )(strip_out[0], *returned, out)
 
 
 def solution(mesh):

time: 25.8 us -> 23.3 us (0.903)
  waiting for transfers between devices: 13.4 us -> 9.9 us
  starting transfers between devices: 7.32 us -> 8.1 us
    ppermute x7, waiting for transfers between devices: 13.4 us -> 9.9 us  [exchange(): lax.ppermute(array, axis, [(i, partner_of(i, step, size)) for i in range(...]
    ppermute x7, starting transfers between devices: 7.32 us -> 8.1 us  [exchange(): lax.ppermute(array, axis, [(i, partner_of(i, step, size)) for i in range(...]
    pallas_call x1, Pallas kernels: 0.77 us -> 1.03 us  [body(): call(functools.partial(first_kernel, score_scale, len(early)), 'first', o...]
  transfers between devices with their start and end apart: 7 -> 7, of which waited for: 4 -> 3; matrix products, arithmetic and copies ran while one was open for 0% -> 0% of each run, Pallas kernels for 11% -> 13%
where the time goes in v3:
time: 23.3 us; the launch traced here: 23.1 us
  waiting for transfers between devices  9.9 us (42%)
  starting transfers between devices  8.1 us (35%)
  Pallas kernels  5.1 us (22%)
    ppermute x7, waiting for transfers between devices, exchange(): lax.ppermute(array, axis, [(i, partner_of(i, step, size)) for i in range(...  9.9 us
    ppermute x7, starting transfers between devices, exchange(): lax.ppermute(array, axis, [(i, partner_of(i, step, size)) for i in range(...  8.1 us
    pallas_call x1, Pallas kernels, body(): call(functools.partial(last_kernel, score_scale, len(late)), 'last', out_...  1.54 us
    pallas_call x1, Pallas kernels, body(): call(functools.partial(prep_kernel, team, head_width), 'prep', out_shape=...  1.35 us
    pallas_call x1, Pallas kernels, body(): call(functools.partial(first_kernel, score_scale, len(early)), 'first', o...  1.03 us
    pallas_call x1, Pallas kernels, body(): call(functools.partial(join_kernel, team, head_width), 'join', out_shape=...  0.67 us
    pallas_call x1, Pallas kernels, body(): call(functools.partial(temporal_kernel, team, count, len(across), score_s...  0.51 us
  transfers between devices with their start and end apart: 7, of which 3 were waited for; matrix products, arithmetic and copies ran while one was open for 0% of the time, Pallas kernels for 13%

profile of v3, /device:TPU:0, one launch (start us, length us, event | category | flops | bytes accessed | tf_op | source)
XLA Modules:
  0.0 23.1 jit_solution(1038624058032146276)
XLA Ops:
  0.0 1.3 %prep.1 = (bf16[2,2,128,128]{3,2,1,0:T(8,128)(2,1)S(1)}, bf16[2,2,128,128]{3,2,1,0:T(8,128)(2,1)S(1)}, bf16[3,2,128,128]{3,2,1,0:T(8,128)(2,1)S(1)}, bf16[2,128,...) custom-call(bf16[2,256,256]{2,1,0:T(8,128)(2,1)} %q_hbm.1, ...), custom_call_target="tpu_custom_call" | custom-call | flops 1 | bytes 1 | tf_op jit(solution)/shard_map/prep/pallas_call | solution.py:156
  1.4 4.1 %collective-permute-start.1 = (bf16[2,2,128,128]{3,2,1,0:T(8,128)(2,1)S(1)}, bf16[2,2,128,128]{3,2,1,0:T(8,128)(2,1)S(1)}, u32[]{:S(2)}, u32[]{:S(2)}) collective-permute-start(bf16[2,2,128,128]{3,2,1,0:T(8,128)(2,1)S(1)} %get-tuple-element.22.refs_0_), channel_id=1, source_target_pairs={{0,8},{4,12},{8,0},{12,4},{1,9},{5,13},{9,1},{13,5},{2,10},{6,14},... | collective-permute-start | bytes 393224 | tf_op jit(solution)/shard_map/ppermute | solution.py:181
  5.5 1.3 %collective-permute-start.2 = (bf16[2,2,128,128]{3,2,1,0:T(8,128)(2,1)S(1)}, bf16[2,2,128,128]{3,2,1,0:T(8,128)(2,1)S(1)}, u32[]{:S(2)}, u32[]{:S(2)}) collective-permute-start(bf16[2,2,128,128]{3,2,1,0:T(8,128)(2,1)S(1)} %get-tuple-element.25), channel_id=1, source_target_pairs={{0,12},{4,8},{8,4},{12,0},{1,13},{5,9},{9,5},{13,1},{2,14},{6,10},... | collective-permute-start | bytes 393224 | tf_op jit(solution)/shard_map/ppermute | solution.py:181
  6.8 0.2 collective-permute-start
  7.0 1.5 %collective-permute-start.3 = (bf16[2,2,256,128]{3,2,1,0:T(8,128)(2,1)S(1)}, bf16[2,2,256,128]{3,2,1,0:T(8,128)(2,1)S(1)}, u32[]{:S(2)}, u32[]{:S(2)}) collective-permute-start(bf16[2,2,256,128]{3,2,1,0:T(8,128)(2,1)S(1)} %get-tuple-element.31.refs_0_), channel_id=1, source_target_pairs={{0,2},{2,0},{1,3},{3,1},{4,6},{6,4},{5,7},{7,5},{8,10},{10,8},{9,1... | collective-permute-start | bytes 786440 | tf_op jit(solution)/shard_map/ppermute | solution.py:181
  8.5 0.0 collective-permute-start.6
  8.5 6.9 %collective-permute-done.1.refs_0_ = bf16[2,2,128,128]{3,2,1,0:T(8,128)(2,1)S(1)} collective-permute-done((bf16[2,2,128,128]{3,2,1,0:T(8,128)(2,1)S(1)}, bf16[2,2,128,128]{3,2,1,0:T(8,128)(2,1)S(1)}, u32[]{:S(2)}, u32[]{:S(2)}) %collective-permute-start.1) | collective-permute-done | bytes 131104 | tf_op jit(solution)/shard_map/ppermute | solution.py:181
  15.4 0.0 collective-permute-done.2.refs_1_
  15.4 1.9 %collective-permute-done.refs_0_ = bf16[3,2,128,128]{3,2,1,0:T(8,128)(2,1)S(1)} collective-permute-done((bf16[3,2,128,128]{3,2,1,0:T(8,128)(2,1)S(1)}, bf16[3,2,128,128]{3,2,1,0:T(8,128)(2,1)S(1)}, u32[]{:S(2)}, u32[]{:S(2)}) %collective-permute-start) | collective-permute-done | bytes 196640 | tf_op jit(solution)/shard_map/ppermute | solution.py:181
  17.4 0.0 collective-permute-done.3.refs_5_
  17.4 0.5 %temporal.1 = (bf16[2,128,128]{2,1,0:T(8,128)(2,1)S(1)}, bf16[2,128,128]{2,1,0:T(8,128)(2,1)S(1)}, bf16[2,2,256,128]{3,2,1,0:T(8,128)(2,1)S(1)}) custom-call(bf16[2,2,128,128]{3,2,1,0:T(8,128)(2,1)S(1)} %get-tuple-element.22.refs_0_, bf16[2,128,128]{2,1,0:T(8,128)(2,1)S(1)} %get-tuple-element.23.refs_1_, ...), custom_call_target="tpu_custom_call", output_to_operand_aliasing={{2}: (5, {})} | custom-call | flops 1 | bytes 1 | tf_op jit(solution)/shard_map/temporal/pallas_call | solution.py:192
  17.9 0.1 collective-permute-start.5
  18.0 0.9 %collective-permute-start.4 = (bf16[2,128,128]{2,1,0:T(8,128)(2,1)S(1)}, bf16[2,128,128]{2,1,0:T(8,128)(2,1)S(1)}, u32[]{:S(2)}, u32[]{:S(2)}) collective-permute-start(bf16[2,128,128]{2,1,0:T(8,128)(2,1)S(1)} %get-tuple-element.33), channel_id=1, source_target_pairs={{0,4},{4,0},{8,12},{12,8},{1,5},{5,1},{9,13},{13,9},{2,6},{6,2},{1... | collective-permute-start | bytes 196616 | tf_op jit(solution)/shard_map/ppermute | solution.py:181
  18.8 0.0 collective-permute-done.6.refs_1_
  18.8 1.0 %first.1 = (f32[2,256,1]{2,1,0:T(8,128)S(1)}, f32[2,256,1]{2,1,0:T(8,128)S(1)}, f32[2,256,128]{2,1,0:T(8,128)S(1)}) custom-call(bf16[2,256,128]{2,1,0:T(8,128)(2,1)S(1)} %get-tuple-element.34.q_ref, bf16[2,2,256,128]{3,2,1,0:T(8,128)(2,1)S(1)} %get-tuple-element.31.refs_0_, bf16[2,2,256,128]{3,2,1,0:T(8,128)(2,1)S(1)} %collective-permute-done.6.refs_1_, ...), custom_call_target="tpu_custom_call" | custom-call | flops 1 | bytes 1 | tf_op jit(solution)/shard_map/first/pallas_call | solution.py:206
  19.9 0.0 collective-permute-done.5.refs_0_
  19.9 1.5 %last.1.refs_2_ = bf16[2,256,256]{2,1,0:T(8,128)(2,1)} custom-call(bf16[2,256,128]{2,1,0:T(8,128)(2,1)S(1)} %get-tuple-element.34.q_ref, bf16[2,2,256,128]{3,2,1,0:T(8,128)(2,1)S(1)} %collective-permute-done.5.refs_0_, f32[2,256,1]{2,1,0:T(8,128)S(1)} %get-tuple-element.36.refs_1_, f32[2,256,1]{2,1,0:T(8,128)S(1)} %get-tuple-element.37.refs_2_, ...), custom_call_target="tpu_custom_call" | custom-call | flops 1 | bytes 1 | tf_op jit(solution)/shard_map/last/pallas_call | solution.py:214
  21.4 1.1 %collective-permute-done.4.refs_1_ = bf16[2,128,128]{2,1,0:T(8,128)(2,1)S(1)} collective-permute-done((bf16[2,128,128]{2,1,0:T(8,128)(2,1)S(1)}, bf16[2,128,128]{2,1,0:T(8,128)(2,1)S(1)}, u32[]{:S(2)}, u32[]{:S(2)}) %collective-permute-start.4) | collective-permute-done | bytes 65568 | tf_op jit(solution)/shard_map/ppermute | solution.py:181
  22.5 0.7 %join.1 = bf16[2,256,256]{2,1,0:T(8,128)(2,1)} custom-call(bf16[2,128,128]{2,1,0:T(8,128)(2,1)S(1)} %get-tuple-element.32.refs_0_, bf16[2,128,128]{2,1,0:T(8,128)(2,1)S(1)} %collective-permute-done.4.refs_1_, bf16[2,256,256]{2,1,0:T(8,128)(2,1)} %last.1.refs_2_), custom_call_target="tpu_custom_call", output_to_operand_aliasing={{}: (2, {})} | custom-call | flops 1 | bytes 1 | tf_op jit(solution)/shard_map/join/pallas_call | solution.py:223
  (2 shorter events, 0.0 us)
Async XLA Ops:
  1.4 14.1 %collective-permute-start.1 = (bf16[2,2,128,128]{3,2,1,0:T(8,128)(2,1)S(1)}, bf16[2,2,128,128]{3,2,1,0:T(8,128)(2,1)S(1)}, u32[]{:S(2)}, u32[]{:S(2)}) collective-permute-start(bf16[2,2,128,128]{3,2,1,0:T(8,128)(2,1)S(1)} %get-tuple-element.22.refs_0_), channel_id=1, source_target_pairs={{0,8},{4,12},{8,0},{12,4},{1,9},{5,13},{9,1},{13,5},{2,10},{6,14},... | collective-permute-start | bytes 393224 | tf_op jit(solution)/shard_map/ppermute | solution.py:181
  5.5 10.0 %collective-permute-start.2 = (bf16[2,2,128,128]{3,2,1,0:T(8,128)(2,1)S(1)}, bf16[2,2,128,128]{3,2,1,0:T(8,128)(2,1)S(1)}, u32[]{:S(2)}, u32[]{:S(2)}) collective-permute-start(bf16[2,2,128,128]{3,2,1,0:T(8,128)(2,1)S(1)} %get-tuple-element.25), channel_id=1, source_target_pairs={{0,12},{4,8},{8,4},{12,0},{1,13},{5,9},{9,5},{13,1},{2,14},{6,10},... | collective-permute-start | bytes 393224 | tf_op jit(solution)/shard_map/ppermute | solution.py:181
  6.8 10.6 %collective-permute-start = (bf16[3,2,128,128]{3,2,1,0:T(8,128)(2,1)S(1)}, bf16[3,2,128,128]{3,2,1,0:T(8,128)(2,1)S(1)}, u32[]{:S(2)}, u32[]{:S(2)}) collective-permute-start(bf16[3,2,128,128]{3,2,1,0:T(8,128)(2,1)S(1)} %get-tuple-element.24), channel_id=1, source_target_pairs={{0,4},{4,0},{8,12},{12,8},{1,5},{5,1},{9,13},{13,9},{2,6},{6,2},{1... | collective-permute-start | bytes 589832 | tf_op jit(solution)/shard_map/ppermute | solution.py:181
  7.0 10.3 %collective-permute-start.3 = (bf16[2,2,256,128]{3,2,1,0:T(8,128)(2,1)S(1)}, bf16[2,2,256,128]{3,2,1,0:T(8,128)(2,1)S(1)}, u32[]{:S(2)}, u32[]{:S(2)}) collective-permute-start(bf16[2,2,256,128]{3,2,1,0:T(8,128)(2,1)S(1)} %get-tuple-element.31.refs_0_), channel_id=1, source_target_pairs={{0,2},{2,0},{1,3},{3,1},{4,6},{6,4},{5,7},{7,5},{8,10},{10,8},{9,1... | collective-permute-start | bytes 786440 | tf_op jit(solution)/shard_map/ppermute | solution.py:181
  8.5 10.3 %collective-permute-start.6 = (bf16[2,2,256,128]{3,2,1,0:T(8,128)(2,1)S(1)}, bf16[2,2,256,128]{3,2,1,0:T(8,128)(2,1)S(1)}, u32[]{:S(2)}, u32[]{:S(2)}) collective-permute-start(bf16[2,2,256,128]{3,2,1,0:T(8,128)(2,1)S(1)} %get-tuple-element.31.refs_0_), channel_id=1, source_target_pairs={{0,1},{1,0},{2,3},{3,2},{4,5},{5,4},{6,7},{7,6},{8,9},{9,8},{10,11... | collective-permute-start | bytes 786440 | tf_op jit(solution)/shard_map/ppermute | solution.py:181
  17.9 2.0 %collective-permute-start.5 = (bf16[2,2,256,128]{3,2,1,0:T(8,128)(2,1)S(1)}, bf16[2,2,256,128]{3,2,1,0:T(8,128)(2,1)S(1)}, u32[]{:S(2)}, u32[]{:S(2)}) collective-permute-start(bf16[2,2,256,128]{3,2,1,0:T(8,128)(2,1)S(1)} %get-tuple-element.35.refs_2_), channel_id=1, source_target_pairs={{0,1},{1,0},{2,3},{3,2},{4,5},{5,4},{6,7},{7,6},{8,9},{9,8},{10,11... | collective-permute-start | bytes 786440 | tf_op jit(solution)/shard_map/ppermute | solution.py:181
  18.0 4.5 %collective-permute-start.4 = (bf16[2,128,128]{2,1,0:T(8,128)(2,1)S(1)}, bf16[2,128,128]{2,1,0:T(8,128)(2,1)S(1)}, u32[]{:S(2)}, u32[]{:S(2)}) collective-permute-start(bf16[2,128,128]{2,1,0:T(8,128)(2,1)S(1)} %get-tuple-element.33), channel_id=1, source_target_pairs={{0,4},{4,0},{8,12},{12,8},{1,5},{5,1},{9,13},{13,9},{2,6},{6,2},{1... | collective-permute-start | bytes 196616 | tf_op jit(solution)/shard_map/ppermute | solution.py:181

commit v4 on v3

--- a/solution.py
+++ b/solution.py
@@ -26,28 +26,26 @@
         copy.wait()
 
 
-def prep_kernel(team, head_width, q_hbm, k_hbm, v_hbm, *refs):
-    pairs, triples, refs = refs[:team], refs[team : 2 * team - 1], refs[2 * team - 1 :]
-    q_own, kv_ref, q_spatial, sems = refs
+def strips_kernel(team, head_width, q_hbm, k_hbm, v_hbm, *refs):
+    pairs, triples, sems = refs[:team], refs[team:-1], refs[-1]
     member = lax.axis_index("frame") % team
-    rows = q_own.shape[1]
-    starts = [pl.multiple_of((member + step) % team * rows, rows) for step in range(team)]
-
-    def cut(array, step):
-        return array.at[:, pl.ds(starts[step], rows), head_width:]
-
+    rows = pairs[0].shape[2]
     copies = []
     for step in range(team):
-        copies += [(cut(k_hbm, step), pairs[step].at[0]), (cut(v_hbm, step), pairs[step].at[1])]
-    for step in range(1, team):
-        copies += [
-            (cut(array, step), triples[step - 1].at[which])
-            for which, array in enumerate((k_hbm, v_hbm, q_hbm))
-        ]
-    copies.append((cut(q_hbm, 0), q_own))
-    for which, array in enumerate((k_hbm, v_hbm)):
-        copies.append((array.at[:, :, :head_width], kv_ref.at[which]))
+        start = pl.multiple_of((member + step) % team * rows, rows)
+        cuts = [array.at[:, pl.ds(start, rows), head_width:] for array in (k_hbm, v_hbm, q_hbm)]
+        copies += [(cut, pairs[step].at[which]) for which, cut in enumerate(cuts[:2])]
+        if step:
+            copies += [(cut, triples[step - 1].at[which]) for which, cut in enumerate(cuts)]
+    run_copies(copies, sems)
+
+
+def rest_kernel(team, q_hbm, k_hbm, v_hbm, _, q_own, kv_ref, q_spatial, sems):
+    rows, head_width = q_own.shape[1:]
+    start = pl.multiple_of(lax.axis_index("frame") % team * rows, rows)
+    copies = [(array.at[:, :, :head_width], kv_ref.at[n]) for n, array in enumerate((k_hbm, v_hbm))]
     copies.append((q_hbm.at[:, :, :head_width], q_spatial))
+    copies.append((q_hbm.at[:, pl.ds(start, rows), head_width:], q_own))
     run_copies(copies, sems)
 
 
@@ -153,17 +151,26 @@
 
     pair, triple = ((size, frames_dev, rows, head_width) for size in (2, 3))
     whole = (frames_dev, tokens_dev, head_width)
+    arrays = [
+        pltpu.with_memory_space_constraint(array, pltpu.HBM) for array in (queries, keys, values)
+    ]
     cut = call(
-        functools.partial(prep_kernel, team, head_width),
-        "prep",
-        out_shape=[in_vmem(*pair)] * team
-        + [in_vmem(*triple)] * (team - 1)
-        + [in_vmem(*pair[1:]), in_vmem(2, *whole), in_vmem(*whole)],
+        functools.partial(strips_kernel, team, head_width),
+        "strips",
+        out_shape=[in_vmem(*pair)] * team + [in_vmem(*triple)] * (team - 1),
         in_specs=[hbm] * 3,
-        out_specs=[vmem] * (2 * team + 2),
-        scratch_shapes=[pltpu.SemaphoreType.DMA((5 * team + 1,))],
-    )(*(pltpu.with_memory_space_constraint(array, pltpu.HBM) for array in (queries, keys, values)))
-    pairs, triples, (query_own, kv_own, query_spatial) = cut[:team], cut[team:-3], cut[-3:]
+        out_specs=[vmem] * (2 * team - 1),
+        scratch_shapes=[pltpu.SemaphoreType.DMA((5 * team - 3,))],
+    )(*arrays)
+    pairs, triples = cut[:team], cut[team:]
+    query_own, kv_own, query_spatial = call(
+        functools.partial(rest_kernel, team),
+        "rest",
+        out_shape=[in_vmem(*pair[1:]), in_vmem(2, *whole), in_vmem(*whole)],
+        in_specs=[hbm] * 3 + [anywhere],
+        out_specs=[vmem] * 3,
+        scratch_shapes=[pltpu.SemaphoreType.DMA((4,))],
+    )(*arrays, pairs[0])
 
     def hold(arrays, flops):
         return call(
@@ -180,11 +187,16 @@
         size = lax.axis_size(axis)
         return lax.ppermute(array, axis, [(i, partner_of(i, step, size)) for i in range(size)])
 
-    others = [exchange(pairs[step % team], "frame", step) for step in range(team, count)]
-    others = hold(others, 1000 * 10**6)
-    mates = [exchange(triples[step - 1], "frame", step) for step in range(1, team)]
-    held = hold([*mates, *others], 1000 * 10**6)
-    mates, others = held[: team - 1], held[team - 1 :]
+    waves = [(range(team, team + 1), 1000), ([*range(1, team), *range(team + 1, count)], 1750)]
+    arrived = {}
+    for steps, mflops in waves:
+        for step in steps:
+            if step < count:
+                block = triples[step - 1] if step < team else pairs[step % team]
+                arrived[step] = exchange(block, "frame", step)
+        if arrived:
+            arrived = dict(zip(arrived, hold(list(arrived.values()), mflops * 10**6)))
+    mates, others = ([arrived[n] for n in steps] for steps in (range(1, team), range(team, count)))
     subs, quarters = lax.axis_size("sub"), lax.axis_size("quarter")
     near = [exchange(kv_own, "sub", step) for step in range(1, subs)]
     across = [exchange(kv_own, "quarter", step) for step in range(1, quarters)]

time: 23.3 us -> 22.9 us (0.983)
  waiting for transfers between devices: 9.9 us -> 8.2 us
  Pallas kernels: 5.1 us -> 5.9 us
  starting transfers between devices: 8.1 us -> 8.55 us
    ppermute x7, waiting for transfers between devices: 9.9 us -> 8.2 us  [exchange(): lax.ppermute(array, axis, [(i, partner_of(i, step, size)) for i in range(...]
    pallas_call x1 -> x2, Pallas kernels: 1.35 us -> 2.16 us  [the longest x1 1.09 us: body(): call(functools.partial(strips_kernel, team, head_width), 'strips', out_sh...]
    ppermute x7, starting transfers between devices: 8.1 us -> 8.55 us  [exchange(): lax.ppermute(array, axis, [(i, partner_of(i, step, size)) for i in range(...]
  transfers between devices with their start and end apart: 7 -> 7, of which waited for: 3 -> 3; matrix products, arithmetic and copies ran while one was open for 0% -> 0% of each run, Pallas kernels for 13% -> 18%
where the time goes in v4:
time: 22.9 us; the launch traced here: 22.7 us
  starting transfers between devices  8.55 us (37%)
  waiting for transfers between devices  8.2 us (36%)
  Pallas kernels  5.9 us (26%)
    ppermute x7, starting transfers between devices, exchange(): lax.ppermute(array, axis, [(i, partner_of(i, step, size)) for i in range(...  8.55 us
    ppermute x7, waiting for transfers between devices, exchange(): lax.ppermute(array, axis, [(i, partner_of(i, step, size)) for i in range(...  8.2 us
    pallas_call x1, Pallas kernels, body(): call(functools.partial(last_kernel, score_scale, len(late)), 'last', out_...  1.53 us
    pallas_call x1, Pallas kernels, body(): call(functools.partial(strips_kernel, team, head_width), 'strips', out_sh...  1.09 us
    pallas_call x1, Pallas kernels, body(): call(functools.partial(rest_kernel, team), 'rest', out_shape=[in_vmem(*pa...  1.07 us
    pallas_call x1, Pallas kernels, body(): call(functools.partial(first_kernel, score_scale, len(early)), 'first', o...  1.03 us
    pallas_call x1, Pallas kernels, body(): call(functools.partial(join_kernel, team, head_width), 'join', out_shape=...  0.67 us
    pallas_call x1, Pallas kernels, body(): call(functools.partial(temporal_kernel, team, count, len(across), score_s...  0.51 us
  transfers between devices with their start and end apart: 7, of which 3 were waited for; matrix products, arithmetic and copies ran while one was open for 0% of the time, Pallas kernels for 18%

profile of v4, /device:TPU:0, one launch (start us, length us, event | category | flops | bytes accessed | tf_op | source)
XLA Modules:
  0.0 22.7 jit_solution(1326754992187166417)
XLA Ops:
  0.0 1.1 %strips.1 = (bf16[2,2,128,128]{3,2,1,0:T(8,128)(2,1)S(1)}, bf16[2,2,128,128]{3,2,1,0:T(8,128)(2,1)S(1)}, bf16[3,2,128,128]{3,2,1,0:T(8,128)(2,1)S(1)}) custom-call(bf16[2,256,256]{2,1,0:T(8,128)(2,1)} %q_hbm.3, bf16[2,256,256]{2,1,0:T(8,128)(2,1)} %k_hbm.3, bf16[2,256,256]{2,1,0:T(8,128)(2,1)} %v_hbm.3), custom_call_target="tpu_custom_call" | custom-call | flops 1 | bytes 1 | tf_op jit(solution)/shard_map/strips/pallas_call | solution.py:157
  1.1 4.1 %collective-permute-start = (bf16[2,2,128,128]{3,2,1,0:T(8,128)(2,1)S(1)}, bf16[2,2,128,128]{3,2,1,0:T(8,128)(2,1)S(1)}, u32[]{:S(2)}, u32[]{:S(2)}) collective-permute-start(bf16[2,2,128,128]{3,2,1,0:T(8,128)(2,1)S(1)} %get-tuple-element.20._.refs_0_), channel_id=1, source_target_pairs={{0,8},{4,12},{8,0},{12,4},{1,9},{5,13},{9,1},{13,5},{2,10},{6,14},... | collective-permute-start | bytes 393224 | tf_op jit(solution)/shard_map/ppermute | solution.py:188
  5.2 1.6 %collective-permute-start.1 = (bf16[3,2,128,128]{3,2,1,0:T(8,128)(2,1)S(1)}, bf16[3,2,128,128]{3,2,1,0:T(8,128)(2,1)S(1)}, u32[]{:S(2)}, u32[]{:S(2)}) collective-permute-start(bf16[3,2,128,128]{3,2,1,0:T(8,128)(2,1)S(1)} %get-tuple-element.22), channel_id=1, source_target_pairs={{0,4},{4,0},{8,12},{12,8},{1,5},{5,1},{9,13},{13,9},{2,6},{6,2},{1... | collective-permute-start | bytes 589832 | tf_op jit(solution)/shard_map/ppermute | solution.py:188
  6.8 0.0 collective-permute-start.2
  6.8 1.1 %rest.1 = (bf16[2,128,128]{2,1,0:T(8,128)(2,1)S(1)}, bf16[2,2,256,128]{3,2,1,0:T(8,128)(2,1)S(1)}, bf16[2,256,128]{2,1,0:T(8,128)(2,1)S(1)}) custom-call(bf16[2,256,256]{2,1,0:T(8,128)(2,1)} %q_hbm.3, bf16[2,256,256]{2,1,0:T(8,128)(2,1)} %k_hbm.3, bf16[2,256,256]{2,1,0:T(8,128)(2,1)} %v_hbm.3, bf16[2,2,128,128]{3,2,1,0:T(8,128)(2,1)S(1)} %get-tuple-element.20._.refs_0_), custom_call_target="tpu_custom_call" | custom-call | flops 1 | bytes 1 | tf_op jit(solution)/shard_map/rest/pallas_call | solution.py:166
  7.9 1.8 %collective-permute-start.3 = (bf16[2,2,256,128]{3,2,1,0:T(8,128)(2,1)S(1)}, bf16[2,2,256,128]{3,2,1,0:T(8,128)(2,1)S(1)}, u32[]{:S(2)}, u32[]{:S(2)}) collective-permute-start(bf16[2,2,256,128]{3,2,1,0:T(8,128)(2,1)S(1)} %get-tuple-element.27.refs_0_), channel_id=1, source_target_pairs={{0,2},{2,0},{1,3},{3,1},{4,6},{6,4},{5,7},{7,5},{8,10},{10,8},{9,1... | collective-permute-start | bytes 786440 | tf_op jit(solution)/shard_map/ppermute | solution.py:188
  9.6 0.0 collective-permute-start.6
  9.6 2.7 %collective-permute-done.refs_0_ = bf16[2,2,128,128]{3,2,1,0:T(8,128)(2,1)S(1)} collective-permute-done((bf16[2,2,128,128]{3,2,1,0:T(8,128)(2,1)S(1)}, bf16[2,2,128,128]{3,2,1,0:T(8,128)(2,1)S(1)}, u32[]{:S(2)}, u32[]{:S(2)}) %collective-permute-start) | collective-permute-done | bytes 131104 | tf_op jit(solution)/shard_map/ppermute | solution.py:188
  12.3 4.6 %collective-permute-done.2.refs_2_ = bf16[2,2,128,128]{3,2,1,0:T(8,128)(2,1)S(1)} collective-permute-done((bf16[2,2,128,128]{3,2,1,0:T(8,128)(2,1)S(1)}, bf16[2,2,128,128]{3,2,1,0:T(8,128)(2,1)S(1)}, u32[]{:S(2)}, u32[]{:S(2)}) %collective-permute-start.2) | collective-permute-done | bytes 131104 | tf_op jit(solution)/shard_map/ppermute | solution.py:188
  16.9 0.0 collective-permute-done.1.refs_1_
  16.9 0.0 collective-permute-done.3.refs_5_
  16.9 0.5 %temporal.1 = (bf16[2,128,128]{2,1,0:T(8,128)(2,1)S(1)}, bf16[2,128,128]{2,1,0:T(8,128)(2,1)S(1)}, bf16[2,2,256,128]{3,2,1,0:T(8,128)(2,1)S(1)}) custom-call(bf16[2,2,128,128]{3,2,1,0:T(8,128)(2,1)S(1)} %get-tuple-element.20._.refs_0_, bf16[2,128,128]{2,1,0:T(8,128)(2,1)S(1)} %get-tuple-element.21.refs_1_, ...), custom_call_target="tpu_custom_call", output_to_operand_aliasing={{2}: (5, {})} | custom-call | flops 1 | bytes 1 | tf_op jit(solution)/shard_map/temporal/pallas_call | solution.py:204
  17.5 0.1 collective-permute-start.5
  17.5 1.0 %collective-permute-start.4 = (bf16[2,128,128]{2,1,0:T(8,128)(2,1)S(1)}, bf16[2,128,128]{2,1,0:T(8,128)(2,1)S(1)}, u32[]{:S(2)}, u32[]{:S(2)}) collective-permute-start(bf16[2,128,128]{2,1,0:T(8,128)(2,1)S(1)} %get-tuple-element.29), channel_id=1, source_target_pairs={{0,4},{4,0},{8,12},{12,8},{1,5},{5,1},{9,13},{13,9},{2,6},{6,2},{1... | collective-permute-start | bytes 196616 | tf_op jit(solution)/shard_map/ppermute | solution.py:188
  18.6 0.0 collective-permute-done.6.refs_1_
  18.6 1.0 %first.1 = (f32[2,256,1]{2,1,0:T(8,128)S(1)}, f32[2,256,1]{2,1,0:T(8,128)S(1)}, f32[2,256,128]{2,1,0:T(8,128)S(1)}) custom-call(bf16[2,256,128]{2,1,0:T(8,128)(2,1)S(1)} %get-tuple-element.30.q_ref, bf16[2,2,256,128]{3,2,1,0:T(8,128)(2,1)S(1)} %get-tuple-element.27.refs_0_, bf16[2,2,256,128]{3,2,1,0:T(8,128)(2,1)S(1)} %collective-permute-done.6.refs_1_, ...), custom_call_target="tpu_custom_call" | custom-call | flops 1 | bytes 1 | tf_op jit(solution)/shard_map/first/pallas_call | solution.py:218
  19.6 0.0 collective-permute-done.5.refs_0_
  19.6 1.5 %last.1.refs_2_ = bf16[2,256,256]{2,1,0:T(8,128)(2,1)} custom-call(bf16[2,256,128]{2,1,0:T(8,128)(2,1)S(1)} %get-tuple-element.30.q_ref, bf16[2,2,256,128]{3,2,1,0:T(8,128)(2,1)S(1)} %collective-permute-done.5.refs_0_, f32[2,256,1]{2,1,0:T(8,128)S(1)} %get-tuple-element.32.refs_1_, f32[2,256,1]{2,1,0:T(8,128)S(1)} %get-tuple-element.33.refs_2_, ...), custom_call_target="tpu_custom_call" | custom-call | flops 1 | bytes 1 | tf_op jit(solution)/shard_map/last/pallas_call | solution.py:226
  21.2 0.9 %collective-permute-done.4.refs_1_ = bf16[2,128,128]{2,1,0:T(8,128)(2,1)S(1)} collective-permute-done((bf16[2,128,128]{2,1,0:T(8,128)(2,1)S(1)}, bf16[2,128,128]{2,1,0:T(8,128)(2,1)S(1)}, u32[]{:S(2)}, u32[]{:S(2)}) %collective-permute-start.4) | collective-permute-done | bytes 65568 | tf_op jit(solution)/shard_map/ppermute | solution.py:188
  22.1 0.7 %join.1 = bf16[2,256,256]{2,1,0:T(8,128)(2,1)} custom-call(bf16[2,128,128]{2,1,0:T(8,128)(2,1)S(1)} %get-tuple-element.28.refs_0_, bf16[2,128,128]{2,1,0:T(8,128)(2,1)S(1)} %collective-permute-done.4.refs_1_, bf16[2,256,256]{2,1,0:T(8,128)(2,1)} %last.1.refs_2_), custom_call_target="tpu_custom_call", output_to_operand_aliasing={{}: (2, {})} | custom-call | flops 1 | bytes 1 | tf_op jit(solution)/shard_map/join/pallas_call | solution.py:235
  (2 shorter events, 0.0 us)
Async XLA Ops:
  1.1 11.2 %collective-permute-start = (bf16[2,2,128,128]{3,2,1,0:T(8,128)(2,1)S(1)}, bf16[2,2,128,128]{3,2,1,0:T(8,128)(2,1)S(1)}, u32[]{:S(2)}, u32[]{:S(2)}) collective-permute-start(bf16[2,2,128,128]{3,2,1,0:T(8,128)(2,1)S(1)} %get-tuple-element.20._.refs_0_), channel_id=1, source_target_pairs={{0,8},{4,12},{8,0},{12,4},{1,9},{5,13},{9,1},{13,5},{2,10},{6,14},... | collective-permute-start | bytes 393224 | tf_op jit(solution)/shard_map/ppermute | solution.py:188
  5.2 11.7 %collective-permute-start.1 = (bf16[3,2,128,128]{3,2,1,0:T(8,128)(2,1)S(1)}, bf16[3,2,128,128]{3,2,1,0:T(8,128)(2,1)S(1)}, u32[]{:S(2)}, u32[]{:S(2)}) collective-permute-start(bf16[3,2,128,128]{3,2,1,0:T(8,128)(2,1)S(1)} %get-tuple-element.22), channel_id=1, source_target_pairs={{0,4},{4,0},{8,12},{12,8},{1,5},{5,1},{9,13},{13,9},{2,6},{6,2},{1... | collective-permute-start | bytes 589832 | tf_op jit(solution)/shard_map/ppermute | solution.py:188
  6.8 10.2 %collective-permute-start.2 = (bf16[2,2,128,128]{3,2,1,0:T(8,128)(2,1)S(1)}, bf16[2,2,128,128]{3,2,1,0:T(8,128)(2,1)S(1)}, u32[]{:S(2)}, u32[]{:S(2)}) collective-permute-start(bf16[2,2,128,128]{3,2,1,0:T(8,128)(2,1)S(1)} %get-tuple-element.23), channel_id=1, source_target_pairs={{0,12},{4,8},{8,4},{12,0},{1,13},{5,9},{9,5},{13,1},{2,14},{6,10},... | collective-permute-start | bytes 393224 | tf_op jit(solution)/shard_map/ppermute | solution.py:188
  7.9 9.1 %collective-permute-start.3 = (bf16[2,2,256,128]{3,2,1,0:T(8,128)(2,1)S(1)}, bf16[2,2,256,128]{3,2,1,0:T(8,128)(2,1)S(1)}, u32[]{:S(2)}, u32[]{:S(2)}) collective-permute-start(bf16[2,2,256,128]{3,2,1,0:T(8,128)(2,1)S(1)} %get-tuple-element.27.refs_0_), channel_id=1, source_target_pairs={{0,2},{2,0},{1,3},{3,1},{4,6},{6,4},{5,7},{7,5},{8,10},{10,8},{9,1... | collective-permute-start | bytes 786440 | tf_op jit(solution)/shard_map/ppermute | solution.py:188
  9.6 8.9 %collective-permute-start.6 = (bf16[2,2,256,128]{3,2,1,0:T(8,128)(2,1)S(1)}, bf16[2,2,256,128]{3,2,1,0:T(8,128)(2,1)S(1)}, u32[]{:S(2)}, u32[]{:S(2)}) collective-permute-start(bf16[2,2,256,128]{3,2,1,0:T(8,128)(2,1)S(1)} %get-tuple-element.27.refs_0_), channel_id=1, source_target_pairs={{0,1},{1,0},{2,3},{3,2},{4,5},{5,4},{6,7},{7,6},{8,9},{9,8},{10,11... | collective-permute-start | bytes 786440 | tf_op jit(solution)/shard_map/ppermute | solution.py:188
  17.5 2.1 %collective-permute-start.5 = (bf16[2,2,256,128]{3,2,1,0:T(8,128)(2,1)S(1)}, bf16[2,2,256,128]{3,2,1,0:T(8,128)(2,1)S(1)}, u32[]{:S(2)}, u32[]{:S(2)}) collective-permute-start(bf16[2,2,256,128]{3,2,1,0:T(8,128)(2,1)S(1)} %get-tuple-element.31.refs_2_), channel_id=1, source_target_pairs={{0,1},{1,0},{2,3},{3,2},{4,5},{5,4},{6,7},{7,6},{8,9},{9,8},{10,11... | collective-permute-start | bytes 786440 | tf_op jit(solution)/shard_map/ppermute | solution.py:188
  17.5 4.5 %collective-permute-start.4 = (bf16[2,128,128]{2,1,0:T(8,128)(2,1)S(1)}, bf16[2,128,128]{2,1,0:T(8,128)(2,1)S(1)}, u32[]{:S(2)}, u32[]{:S(2)}) collective-permute-start(bf16[2,128,128]{2,1,0:T(8,128)(2,1)S(1)} %get-tuple-element.29), channel_id=1, source_target_pairs={{0,4},{4,0},{8,12},{12,8},{1,5},{5,1},{9,13},{13,9},{2,6},{6,2},{1... | collective-permute-start | bytes 196616 | tf_op jit(solution)/shard_map/ppermute | solution.py:188

commit v5 on v4

v5 whole, which is shorter than its diff:
```python
import functools
import math

import jax
import jax.numpy as jnp
from jax import lax
from jax.experimental import pallas as pl
from jax.experimental.pallas import tpu as pltpu
from jax.sharding import PartitionSpec as P

STRIP = 16
SHARE = 8
VMEM_LIMIT = 16 * 1024 * 1024


def partner_of(index, step, count):
    if count & (count - 1) == 0:
        return index ^ step
    return (index + step) % count


def run_copies(copies, sems):
    started = [pltpu.make_async_copy(src, dst, sems.at[n]) for n, (src, dst) in enumerate(copies)]
    for copy in started:
        copy.start()
    for copy in started:
        copy.wait()


def strips_kernel(team, homed, head_width, q_hbm, k_hbm, v_hbm, *refs):
    pairs, mates, sems = refs[:team], refs[team:-1], refs[-1]
    member = lax.axis_index("frame") % team
    free = k_hbm.shape[1] - team * homed
    copies = []
    for step in range(team):
        start = pl.multiple_of((member + step) % team * homed, STRIP)
        cuts = [array.at[:, pl.ds(start, homed), head_width:] for array in (k_hbm, v_hbm, q_hbm)]
        copies += [(cut, pairs[step].at[which]) for which, cut in enumerate(cuts[:2])]
        if step:
            mate = mates[step - 1]
            copies += [(cut, mate.at[:, pl.ds(n * homed, homed)]) for n, cut in enumerate(cuts)]
            if free:
                for n, array in enumerate((k_hbm, v_hbm)):
                    cut = array.at[:, team * homed :, head_width:]
                    copies.append((cut, mate.at[:, pl.ds(3 * homed + n * free, free)]))
    run_copies(copies, sems)


def rest_kernel(team, homed, q_hbm, k_hbm, v_hbm, _, q_own, kv_ref, q_spatial, *refs):
    sems, head_width = refs[-1], q_spatial.shape[2]
    start = pl.multiple_of(lax.axis_index("frame") % team * homed, STRIP)
    copies = [(array.at[:, :, :head_width], kv_ref.at[n]) for n, array in enumerate((k_hbm, v_hbm))]
    copies.append((q_hbm.at[:, :, :head_width], q_spatial))
    copies.append((q_hbm.at[:, pl.ds(start, homed), head_width:], q_own))
    if len(refs) > 1:
        for n, array in enumerate((k_hbm, v_hbm, q_hbm)):
            dst = refs[1] if n == 2 else refs[0].at[n]
            copies.append((array.at[:, team * homed :, head_width:], dst))
    run_copies(copies, sems)


def score(query_rows, key_rows, score_scale):
    product = lax.dot_general(
        query_rows, key_rows, (((1,), (1,)), ((), ())), preferred_element_type=jnp.float32
    )
    return product * score_scale


def mix(expo, value_rows):
    return jnp.dot(expo.astype(jnp.bfloat16), value_rows, preferred_element_type=jnp.float32)


def attend_strips(queries, keys, values, outs, score_scale):
    frames_dev, rows = outs[0].shape[:2]
    cuts = [slice(lower, lower + STRIP) for lower in range(0, rows, STRIP)]

    def gather(parts, cut):
        return jnp.concatenate([part[f, cut] for part in parts for f in range(frames_dev)])

    scores = [score(gather(queries, cut), gather(keys, cut), score_scale) for cut in cuts]
    highest = [jnp.max(s, axis=-1, keepdims=True) for s in scores]
    expo = [jnp.exp(s - h) for s, h in zip(scores, highest)]
    totals = [jnp.sum(e, axis=-1, keepdims=True) for e in expo]
    mixed = [mix(e, gather(values, cut)) for e, cut in zip(expo, cuts)]
    results = [(m / t).astype(jnp.bfloat16) for m, t in zip(mixed, totals)]
    for cut, result in zip(cuts, results):
        for number, ref in enumerate(outs):
            for frame in range(frames_dev):
                lower = (number * frames_dev + frame) * STRIP
                ref[frame, cut] = result[lower : lower + STRIP]


def homed_kernel(team, others, passed, score_scale, own, query, *refs):
    mates, others = refs[: team - 1], refs[team - 1 : team - 1 + others]
    outs = refs[len(mates) + len(others) + passed :][:team]
    homed = query.shape[1]

    def part(which):
        return [mate.at[:, pl.ds(which * homed, homed)] for mate in mates]

    keys, values = (
        [own.at[n], *part(n), *(block.at[n] for block in others)] for n in range(2)
    )
    attend_strips([query, *part(2)], keys, values, outs, score_scale)


def pack_kernel(team, homed, arrived, own, *refs):
    mates, (packed, sems) = refs[: team - 1], (refs[-2], refs[-1])
    free = own.shape[2]
    copies = [(own, packed.at[0])]
    for number, mate in enumerate(mates):
        for n in range(2):
            src = mate.at[:, pl.ds(3 * homed + n * free, free)]
            copies.append((src, packed.at[1 + number, n]))
    run_copies(copies, sems)


def free_kernel(team, score_scale, query, *refs):
    packs, out = refs[:-1], refs[-1]
    keys, values = ([p.at[m, n] for p in packs for m in range(team)] for n in range(2))
    attend_strips([query], keys, values, [out], score_scale)


def first_kernel(score_scale, pieces, q_ref, *refs):
    kvs, (top_ref, total_ref, acc_ref) = refs[:pieces], refs[pieces:]
    for frame in range(q_ref.shape[0]):
        key = jnp.concatenate([kv[0, frame] for kv in kvs])
        value = jnp.concatenate([kv[1, frame] for kv in kvs])
        scores = score(q_ref[frame], key, score_scale)
        highest = jnp.max(scores, axis=-1, keepdims=True)
        expo = jnp.exp(scores - highest)
        top_ref[frame] = highest
        total_ref[frame] = jnp.sum(expo, axis=-1, keepdims=True)
        acc_ref[frame] = mix(expo, value)


def last_kernel(score_scale, pieces, q_ref, *refs):
    kvs, (top_ref, total_ref, acc_ref, out_hbm, o_ref, sems) = refs[:pieces], refs[pieces:]
    head_width = q_ref.shape[-1]
    for frame in range(q_ref.shape[0]):
        key = jnp.concatenate([kv[0, frame] for kv in kvs])
        value = jnp.concatenate([kv[1, frame] for kv in kvs])
        scores = score(q_ref[frame], key, score_scale)
        highest = jnp.maximum(top_ref[frame], jnp.max(scores, axis=-1, keepdims=True))
        expo = jnp.exp(scores - highest)
        factor = jnp.exp(top_ref[frame] - highest)
        total = total_ref[frame] * factor + jnp.sum(expo, axis=-1, keepdims=True)
        o_ref[frame] = ((acc_ref[frame] * factor + mix(expo, value)) / total).astype(jnp.bfloat16)
    run_copies([(o_ref, out_hbm.at[:, :, :head_width])], sems)


def join_kernel(team, homed, head_width, *refs):
    pieces, out_hbm, sems = refs[:-3], refs[-2], refs[-1]
    member = lax.axis_index("frame") % team
    copies = []
    for step, piece in enumerate(pieces):
        start, rows = team * homed, piece.shape[1]
        if step < team:
            start = pl.multiple_of((member + step) % team * homed, STRIP)
        copies.append((piece, out_hbm.at[:, pl.ds(start, rows), head_width:]))
    run_copies(copies, sems)


def body(queries, keys, values):
    frames_dev, tokens_dev, width = queries.shape
    head_width = width // 2
    score_scale = 1.0 / math.sqrt(head_width)
    count = lax.axis_size("frame")
    subs, quarters = lax.axis_size("sub"), lax.axis_size("quarter")
    team = 2 if count & (count - 1) == 0 and count > 1 else 1
    strips = tokens_dev // STRIP
    homed = (strips - strips // SHARE) // team * STRIP if team > 1 else tokens_dev
    free = tokens_dev - team * homed
    dtype = queries.dtype
    hbm = pl.BlockSpec(memory_space=pltpu.HBM)
    vmem = pl.BlockSpec(memory_space=pltpu.VMEM)
    anywhere = pl.BlockSpec(memory_space=pl.ANY)

    def call(kernel, name, mflops=0, **rest):
        return pl.pallas_call(
            kernel,
            name=name,
            compiler_params=pltpu.CompilerParams(vmem_limit_bytes=VMEM_LIMIT),
            cost_estimate=pl.CostEstimate(
                flops=mflops * 10**6 + 1, bytes_accessed=1, transcendentals=0
            ),
            **rest,
        )

    def in_vmem(*shape, of=dtype):
        return pltpu.VMEM(shape, of)

    block, spare, whole = (
        (frames_dev, rows, head_width) for rows in (homed, free, tokens_dev)
    )
    arrays = [
        pltpu.with_memory_space_constraint(array, pltpu.HBM) for array in (queries, keys, values)
    ]
    cut = call(
        functools.partial(strips_kernel, team, homed, head_width),
        "strips",
        out_shape=[in_vmem(2, *block)] * team
        + [in_vmem(frames_dev, 3 * homed + 2 * free, head_width)] * (team - 1),
        in_specs=[hbm] * 3,
        out_specs=[vmem] * (2 * team - 1),
        scratch_shapes=[pltpu.SemaphoreType.DMA((7 * team,))],
    )(*arrays)
    pairs, triples = cut[:team], cut[team:]
    spares = [in_vmem(2, *spare), in_vmem(*spare)] if free else []
    query_own, kv_own, query_spatial, *spares = call(
        functools.partial(rest_kernel, team, homed),
        "rest",
        out_shape=[in_vmem(*block), in_vmem(2, *whole), in_vmem(*whole), *spares],
        in_specs=[hbm] * 3 + [anywhere],
        out_specs=[vmem] * (3 + len(spares)),
        scratch_shapes=[pltpu.SemaphoreType.DMA((7,))],
    )(*arrays, pairs[0])

    def hold(arrays, mflops, far=()):
        total = len(arrays) + len(far)
        return call(
            lambda *refs: None,
            "hold",
            mflops=mflops,
            out_shape=[in_vmem(*array.shape, of=array.dtype) for array in arrays]
            + [jax.ShapeDtypeStruct(array.shape, dtype) for array in far],
            in_specs=[anywhere] * len(arrays) + [hbm] * len(far),
            out_specs=[anywhere] * len(arrays) + [hbm] * len(far),
            input_output_aliases={n: n for n in range(total)},
        )(*arrays, *far)

    def exchange(array, axis, step):
        size = lax.axis_size(axis)
        return lax.ppermute(array, axis, [(i, partner_of(i, step, size)) for i in range(size)])

    cross = {step: exchange(pairs[step % team], "frame", step) for step in range(team, count)}
    mates = [exchange(triples[step - 1], "frame", step) for step in range(1, team)]
    across = [exchange(kv_own, "quarter", step) for step in range(1, quarters)]
    near = [exchange(kv_own, "sub", step) for step in range(1, subs)]
    if cross:
        [cross[team]] = hold([cross[team]], 1150)
    if free:
        gate = [cross[team]] if cross else []
        *gate, packed = call(
            functools.partial(pack_kernel, team, homed, 0),
            "pack",
            mflops=0,
            out_shape=[in_vmem(*g.shape) for g in gate] + [in_vmem(team, 2, *spare)],
            in_specs=[vmem] * team + [anywhere] * len(gate),
            out_specs=[anywhere] * len(gate) + [vmem],
            scratch_shapes=[pltpu.SemaphoreType.DMA((1 + 2 * (team - 1),))],
            input_output_aliases={team: 0} if gate else {},
        )(spares[0], *mates, *gate)
        if gate:
            [cross[team]] = gate
        spread = [exchange(packed, "frame", step) for step in range(team, count, team)]
    held = hold([*mates, *cross.values()], 1900)
    mates, others = held[: team - 1], held[team - 1 :]
    across = hold(across, 100)

    strip_out = call(
        functools.partial(homed_kernel, team, len(others), 0, score_scale),
        "homed",
        mflops=0,
        out_shape=[in_vmem(*block)] * team,
        in_specs=[vmem] * (1 + count),
        out_specs=[vmem] * team,
    )(pairs[0], query_own, *mates, *others)
    returned = [exchange(strip_out[step], "frame", step) for step in range(1, team)]

    early = [kv_own, *near, *across]
    late = [exchange(piece, "sub", step) for step in range(1, subs) for piece in across]
    running = call(
        functools.partial(first_kernel, score_scale, len(early)),
        "first",
        out_shape=[in_vmem(*whole[:2], size, of=jnp.float32) for size in (1, 1, head_width)],
        in_specs=[vmem] * (1 + len(early)),
        out_specs=[vmem] * 3,
    )(query_spatial, *early)
    if free:
        held = hold([*spread, *running], 4000)
        spread, running = held[: len(spread)], held[len(spread) :]
    out = call(
        functools.partial(last_kernel, score_scale, len(late)),
        "last",
        out_shape=jax.ShapeDtypeStruct(queries.shape, dtype),
        in_specs=[vmem] * (4 + len(late)),
        out_specs=hbm,
        scratch_shapes=[pltpu.VMEM(whole, dtype), pltpu.SemaphoreType.DMA((1,))],
    )(query_spatial, *late, *running)

    pieces = [strip_out[0], *returned]
    if free:
        pieces.append(
            call(
                functools.partial(free_kernel, team, score_scale),
                "free",
                out_shape=in_vmem(*spare),
                in_specs=[vmem] * (2 + len(spread)),
                out_specs=vmem,
            )(spares[1], packed, *spread)
        )
    return call(
        functools.partial(join_kernel, team, homed, head_width),
        "join",
        out_shape=jax.ShapeDtypeStruct(queries.shape, dtype),
        in_specs=[vmem] * len(pieces) + [hbm],
        out_specs=hbm,
        scratch_shapes=[pltpu.SemaphoreType.DMA((len(pieces),))],
        input_output_aliases={len(pieces): 0},
    )(*pieces, out)


def solution(mesh):
    spec = P(("groups", "frame"), ("quarter", "sub"), None)
    return jax.shard_map(
        body, mesh=mesh, in_specs=(spec,) * 3, out_specs=spec, check_vma=False
    )
```

time: 22.9 us -> 22 us (0.961)
  waiting for transfers between devices: 8.2 us -> 4.79 us
  starting transfers between devices: 8.55 us -> 10.6 us
  Pallas kernels: 5.9 us -> 6.35 us
    ppermute x7 -> x8, waiting for transfers between devices: 8.2 us -> 4.79 us  [exchange(): lax.ppermute(array, axis, [(i, partner_of(i, step, size)) for i in range(...]
    ppermute x7 -> x8, starting transfers between devices: 8.55 us -> 10.6 us  [exchange(): lax.ppermute(array, axis, [(i, partner_of(i, step, size)) for i in range(...]
    pallas_call x6 -> x10, Pallas kernels: 3.34 us -> 3.79 us  [the longest x1 1.11 us: body(): call(functools.partial(strips_kernel, team, homed, head_width), 'strips',...]
  transfers between devices with their start and end apart: 7 -> 8, of which waited for: 3 -> 5; matrix products, arithmetic and copies ran while one was open for 0% -> 0% of each run, Pallas kernels for 18% -> 21%
where the time goes in v5:
time: 22 us; the launch traced here: 21.8 us
  starting transfers between devices  10.6 us (48%)
  Pallas kernels  6.35 us (29%)
  waiting for transfers between devices  4.79 us (22%)
    ppermute x8, starting transfers between devices, exchange(): lax.ppermute(array, axis, [(i, partner_of(i, step, size)) for i in range(...  10.6 us
    ppermute x8, waiting for transfers between devices, exchange(): lax.ppermute(array, axis, [(i, partner_of(i, step, size)) for i in range(...  4.79 us
    pallas_call x1, Pallas kernels, body(): call(functools.partial(last_kernel, score_scale, len(late)), 'last', out_...  1.53 us
    pallas_call x1, Pallas kernels, body(): call(functools.partial(strips_kernel, team, homed, head_width), 'strips',...  1.11 us
    pallas_call x1, Pallas kernels, body(): call(functools.partial(rest_kernel, team, homed), 'rest', out_shape=[in_v...  1.1 us
    pallas_call x1, Pallas kernels, body(): call(functools.partial(first_kernel, score_scale, len(early)), 'first', o...  1.03 us
    pallas_call x1, Pallas kernels, body(): call(functools.partial(join_kernel, team, homed, head_width), 'join', out...  0.67 us
    pallas_call x1, Pallas kernels, body(): call(functools.partial(homed_kernel, team, len(others), 0, score_scale),...  0.49 us
  transfers between devices with their start and end apart: 8, of which 5 were waited for; matrix products, arithmetic and copies ran while one was open for 0% of the time, Pallas kernels for 21%

profile of v5, /device:TPU:0, one launch (start us, length us, event | category | flops | bytes accessed | tf_op | source)
XLA Modules:
  0.0 21.8 jit_solution(10778619245120566199)
XLA Ops:
  0.0 1.1 %strips.1 = (bf16[2,2,112,128]{3,2,1,0:T(8,128)(2,1)S(1)}, bf16[2,2,112,128]{3,2,1,0:T(8,128)(2,1)S(1)}, bf16[2,400,128]{2,1,0:T(8,128)(2,1)S(1)}) custom-call(bf16[2,256,256]{2,1,0:T(8,128)(2,1)} %q_hbm.3, bf16[2,256,256]{2,1,0:T(8,128)(2,1)} %k_hbm.3, bf16[2,256,256]{2,1,0:T(8,128)(2,1)} %v_hbm.3), custom_call_target="tpu_custom_call" | custom-call | flops 1 | bytes 1 | tf_op jit(solution)/shard_map/strips/pallas_call | solution.py:199
  1.1 4.1 %collective-permute-start.1 = (bf16[2,2,112,128]{3,2,1,0:T(8,128)(2,1)S(1)}, bf16[2,2,112,128]{3,2,1,0:T(8,128)(2,1)S(1)}, u32[]{:S(2)}, u32[]{:S(2)}) collective-permute-start(bf16[2,2,112,128]{3,2,1,0:T(8,128)(2,1)S(1)} %get-tuple-element.27._.own), channel_id=1, source_target_pairs={{0,8},{4,12},{8,0},{12,4},{1,9},{5,13},{9,1},{13,5},{2,10},{6,14},... | collective-permute-start | bytes 344072 | tf_op jit(solution)/shard_map/ppermute | solution.py:234
  5.2 1.6 %collective-permute-start = (bf16[2,400,128]{2,1,0:T(8,128)(2,1)S(1)}, bf16[2,400,128]{2,1,0:T(8,128)(2,1)S(1)}, u32[]{:S(2)}, u32[]{:S(2)}) collective-permute-start(bf16[2,400,128]{2,1,0:T(8,128)(2,1)S(1)} %get-tuple-element.29), channel_id=1, source_target_pairs={{0,4},{4,0},{8,12},{12,8},{1,5},{5,1},{9,13},{13,9},{2,6},{6,2},{1... | collective-permute-start | bytes 614408 | tf_op jit(solution)/shard_map/ppermute | solution.py:234
  6.8 0.0 collective-permute-start.2
  6.8 1.1 %rest.1 = (bf16[2,112,128]{2,1,0:T(8,128)(2,1)S(1)}, bf16[2,2,256,128]{3,2,1,0:T(8,128)(2,1)S(1)}, bf16[2,256,128]{2,1,0:T(8,128)(2,1)S(1)}, bf16[2,2,32,128]{3,2,1,0:T(8,128)(2,1)S(1)}, bf16[2,32,128]{2,1,0:T(8,128)(2,1)S(1)}) custom-call(bf16[2,256,256]{2,1,0:T(8,128)(2,1)} %q_hbm.3, bf16[2,256,256]{2,1,0:T(8,128)(2,1)} %k_hbm.3, ...), custom_call_target="tpu_custom_call" | custom-call | flops 1 | bytes 1 | tf_op jit(solution)/shard_map/rest/pallas_call | solution.py:210
  7.9 1.8 %collective-permute-start.6 = (bf16[2,2,256,128]{3,2,1,0:T(8,128)(2,1)S(1)}, bf16[2,2,256,128]{3,2,1,0:T(8,128)(2,1)S(1)}, u32[]{:S(2)}, u32[]{:S(2)}) collective-permute-start(bf16[2,2,256,128]{3,2,1,0:T(8,128)(2,1)S(1)} %get-tuple-element.41.refs_0_), channel_id=1, source_target_pairs={{0,2},{2,0},{1,3},{3,1},{4,6},{6,4},{5,7},{7,5},{8,10},{10,8},{9,1... | collective-permute-start | bytes 786440 | tf_op jit(solution)/shard_map/ppermute | solution.py:234
  9.7 0.0 collective-permute-start.5
  9.7 2.0 %collective-permute-done.1.refs_0_ = bf16[2,2,112,128]{3,2,1,0:T(8,128)(2,1)S(1)} collective-permute-done((bf16[2,2,112,128]{3,2,1,0:T(8,128)(2,1)S(1)}, bf16[2,2,112,128]{3,2,1,0:T(8,128)(2,1)S(1)}, u32[]{:S(2)}, u32[]{:S(2)}) %collective-permute-start.1) | collective-permute-done | bytes 114720 | tf_op jit(solution)/shard_map/ppermute | solution.py:234
  11.7 1.7 %collective-permute-done.refs_0_ = bf16[2,400,128]{2,1,0:T(8,128)(2,1)S(1)} collective-permute-done((bf16[2,400,128]{2,1,0:T(8,128)(2,1)S(1)}, bf16[2,400,128]{2,1,0:T(8,128)(2,1)S(1)}, u32[]{:S(2)}, u32[]{:S(2)}) %collective-permute-start) | collective-permute-done | bytes 204832 | tf_op jit(solution)/shard_map/ppermute | solution.py:234
  13.3 0.1 pack.1
  13.4 2.3 %collective-permute-start.4 = (bf16[2,2,2,32,128]{4,3,2,1,0:T(8,128)(2,1)S(1)}, bf16[2,2,2,32,128]{4,3,2,1,0:T(8,128)(2,1)S(1)}, u32[]{:S(2)}, u32[]{:S(2)}) collective-permute-start(bf16[2,2,2,32,128]{4,3,2,1,0:T(8,128)(2,1)S(1)} %get-tuple-element.39.refs_0_), channel_id=1, source_target_pairs={{0,8},{4,12},{8,0},{12,4},{1,9},{5,13},{9,1},{13,5},{2,10},{6,14},... | collective-permute-start | bytes 196616 | tf_op jit(solution)/shard_map/ppermute | solution.py:234
  15.7 0.7 %collective-permute-done.2.refs_2_ = bf16[2,2,112,128]{3,2,1,0:T(8,128)(2,1)S(1)} collective-permute-done((bf16[2,2,112,128]{3,2,1,0:T(8,128)(2,1)S(1)}, bf16[2,2,112,128]{3,2,1,0:T(8,128)(2,1)S(1)}, u32[]{:S(2)}, u32[]{:S(2)}) %collective-permute-start.2) | collective-permute-done | bytes 114720 | tf_op jit(solution)/shard_map/ppermute | solution.py:234
  16.4 0.5 %homed.1 = (bf16[2,112,128]{2,1,0:T(8,128)(2,1)S(1)}, bf16[2,112,128]{2,1,0:T(8,128)(2,1)S(1)}) custom-call(bf16[2,2,112,128]{3,2,1,0:T(8,128)(2,1)S(1)} %get-tuple-element.27._.own, bf16[2,112,128]{2,1,0:T(8,128)(2,1)S(1)} %get-tuple-element.28.query, bf16[2,400,128]{2,1,0:T(8,128)(2,1)S(1)} %get-tuple-element.33.refs_0_, ...), custom_call_target="tpu_custom_call" | custom-call | flops 1 | bytes 1 | tf_op jit(solution)/shard_map/homed/pallas_call | solution.py:261
  16.9 0.9 %collective-permute-start.3 = (bf16[2,112,128]{2,1,0:T(8,128)(2,1)S(1)}, bf16[2,112,128]{2,1,0:T(8,128)(2,1)S(1)}, u32[]{:S(2)}, u32[]{:S(2)}) collective-permute-start(bf16[2,112,128]{2,1,0:T(8,128)(2,1)S(1)} %get-tuple-element.37), channel_id=1, source_target_pairs={{0,4},{4,0},{8,12},{12,8},{1,5},{5,1},{9,13},{13,9},{2,6},{6,2},{1... | collective-permute-start | bytes 172040 | tf_op jit(solution)/shard_map/ppermute | solution.py:234
  17.8 0.0 collective-permute-done.6.refs_0_
  17.8 0.0 collective-permute-start.7
  17.8 0.0 collective-permute-done.5.refs_1_
  17.8 1.0 %first.1 = (f32[2,256,1]{2,1,0:T(8,128)S(1)}, f32[2,256,1]{2,1,0:T(8,128)S(1)}, f32[2,256,128]{2,1,0:T(8,128)S(1)}) custom-call(bf16[2,256,128]{2,1,0:T(8,128)(2,1)S(1)} %get-tuple-element.40.q_ref, bf16[2,2,256,128]{3,2,1,0:T(8,128)(2,1)S(1)} %get-tuple-element.41.refs_0_, bf16[2,2,256,128]{3,2,1,0:T(8,128)(2,1)S(1)} %collective-permute-done.5.refs_1_, ...), custom_call_target="tpu_custom_call" | custom-call | flops 1 | bytes 1 | tf_op jit(solution)/shard_map/first/pallas_call | solution.py:273
  18.8 0.0 collective-permute-done.4.refs_0_
  18.9 0.4 %free.1.refs_2_ = bf16[2,32,128]{2,1,0:T(8,128)(2,1)S(1)} custom-call(bf16[2,32,128]{2,1,0:T(8,128)(2,1)S(1)} %get-tuple-element.38.query, bf16[2,2,2,32,128]{4,3,2,1,0:T(8,128)(2,1)S(1)} %get-tuple-element.39.refs_0_, bf16[2,2,2,32,128]{4,3,2,1,0:T(8,128)(2,1)S(1)} %get-tuple-element.45.refs_1_), custom_call_target="tpu_custom_call" | custom-call | flops 1 | bytes 1 | tf_op jit(solution)/shard_map/free/pallas_call | solution.py:295
  19.2 0.1 collective-permute-done.7.refs_0_
  19.3 1.5 %last.1.refs_3_ = bf16[2,256,256]{2,1,0:T(8,128)(2,1)} custom-call(bf16[2,256,128]{2,1,0:T(8,128)(2,1)S(1)} %get-tuple-element.40.q_ref, bf16[2,2,256,128]{3,2,1,0:T(8,128)(2,1)S(1)} %collective-permute-done.7.refs_0_, f32[2,256,1]{2,1,0:T(8,128)S(1)} %get-tuple-element.46.refs_1_, f32[2,256,1]{2,1,0:T(8,128)S(1)} %get-tuple-element.47.refs_2_, ...), custom_call_target="tpu_custom_call" | custom-call | flops 1 | bytes 1 | tf_op jit(solution)/shard_map/last/pallas_call | solution.py:283
  20.9 0.3 %collective-permute-done.3.refs_1_ = bf16[2,112,128]{2,1,0:T(8,128)(2,1)S(1)} collective-permute-done((bf16[2,112,128]{2,1,0:T(8,128)(2,1)S(1)}, bf16[2,112,128]{2,1,0:T(8,128)(2,1)S(1)}, u32[]{:S(2)}, u32[]{:S(2)}) %collective-permute-start.3) | collective-permute-done | bytes 57376 | tf_op jit(solution)/shard_map/ppermute | solution.py:234
  21.1 0.7 %join.1 = bf16[2,256,256]{2,1,0:T(8,128)(2,1)} custom-call(bf16[2,112,128]{2,1,0:T(8,128)(2,1)S(1)} %get-tuple-element.36.refs_0_, bf16[2,112,128]{2,1,0:T(8,128)(2,1)S(1)} %collective-permute-done.3.refs_1_, bf16[2,32,128]{2,1,0:T(8,128)(2,1)S(1)} %free.1.refs_2_, bf16[2,256,256]{2,1,0:T(8,128)(2,1)} %last.1.refs_3_), custom_call_target="tpu_custom_call", output_to_operand_aliasing={{}: (3, {})} | custom-call | flops 1 | bytes 1 | tf_op jit(solution)/shard_map/join/pallas_call | solution.py:303
  (4 shorter events, 0.0 us)
Async XLA Ops:
  1.1 10.5 %collective-permute-start.1 = (bf16[2,2,112,128]{3,2,1,0:T(8,128)(2,1)S(1)}, bf16[2,2,112,128]{3,2,1,0:T(8,128)(2,1)S(1)}, u32[]{:S(2)}, u32[]{:S(2)}) collective-permute-start(bf16[2,2,112,128]{3,2,1,0:T(8,128)(2,1)S(1)} %get-tuple-element.27._.own), channel_id=1, source_target_pairs={{0,8},{4,12},{8,0},{12,4},{1,9},{5,13},{9,1},{13,5},{2,10},{6,14},... | collective-permute-start | bytes 344072 | tf_op jit(solution)/shard_map/ppermute | solution.py:234
  5.2 8.1 %collective-permute-start = (bf16[2,400,128]{2,1,0:T(8,128)(2,1)S(1)}, bf16[2,400,128]{2,1,0:T(8,128)(2,1)S(1)}, u32[]{:S(2)}, u32[]{:S(2)}) collective-permute-start(bf16[2,400,128]{2,1,0:T(8,128)(2,1)S(1)} %get-tuple-element.29), channel_id=1, source_target_pairs={{0,4},{4,0},{8,12},{12,8},{1,5},{5,1},{9,13},{13,9},{2,6},{6,2},{1... | collective-permute-start | bytes 614408 | tf_op jit(solution)/shard_map/ppermute | solution.py:234
  6.8 9.6 %collective-permute-start.2 = (bf16[2,2,112,128]{3,2,1,0:T(8,128)(2,1)S(1)}, bf16[2,2,112,128]{3,2,1,0:T(8,128)(2,1)S(1)}, u32[]{:S(2)}, u32[]{:S(2)}) collective-permute-start(bf16[2,2,112,128]{3,2,1,0:T(8,128)(2,1)S(1)} %get-tuple-element.32), channel_id=1, source_target_pairs={{0,12},{4,8},{8,4},{12,0},{1,13},{5,9},{9,5},{13,1},{2,14},{6,10},... | collective-permute-start | bytes 344072 | tf_op jit(solution)/shard_map/ppermute | solution.py:234
  7.9 9.9 %collective-permute-start.6 = (bf16[2,2,256,128]{3,2,1,0:T(8,128)(2,1)S(1)}, bf16[2,2,256,128]{3,2,1,0:T(8,128)(2,1)S(1)}, u32[]{:S(2)}, u32[]{:S(2)}) collective-permute-start(bf16[2,2,256,128]{3,2,1,0:T(8,128)(2,1)S(1)} %get-tuple-element.41.refs_0_), channel_id=1, source_target_pairs={{0,2},{2,0},{1,3},{3,1},{4,6},{6,4},{5,7},{7,5},{8,10},{10,8},{9,1... | collective-permute-start | bytes 786440 | tf_op jit(solution)/shard_map/ppermute | solution.py:234
  9.7 8.1 %collective-permute-start.5 = (bf16[2,2,256,128]{3,2,1,0:T(8,128)(2,1)S(1)}, bf16[2,2,256,128]{3,2,1,0:T(8,128)(2,1)S(1)}, u32[]{:S(2)}, u32[]{:S(2)}) collective-permute-start(bf16[2,2,256,128]{3,2,1,0:T(8,128)(2,1)S(1)} %get-tuple-element.41.refs_0_), channel_id=1, source_target_pairs={{0,1},{1,0},{2,3},{3,2},{4,5},{5,4},{6,7},{7,6},{8,9},{9,8},{10,11... | collective-permute-start | bytes 786440 | tf_op jit(solution)/shard_map/ppermute | solution.py:234
  13.4 5.4 %collective-permute-start.4 = (bf16[2,2,2,32,128]{4,3,2,1,0:T(8,128)(2,1)S(1)}, bf16[2,2,2,32,128]{4,3,2,1,0:T(8,128)(2,1)S(1)}, u32[]{:S(2)}, u32[]{:S(2)}) collective-permute-start(bf16[2,2,2,32,128]{4,3,2,1,0:T(8,128)(2,1)S(1)} %get-tuple-element.39.refs_0_), channel_id=1, source_target_pairs={{0,8},{4,12},{8,0},{12,4},{1,9},{5,13},{9,1},{13,5},{2,10},{6,14},... | collective-permute-start | bytes 196616 | tf_op jit(solution)/shard_map/ppermute | solution.py:234
  16.9 4.2 %collective-permute-start.3 = (bf16[2,112,128]{2,1,0:T(8,128)(2,1)S(1)}, bf16[2,112,128]{2,1,0:T(8,128)(2,1)S(1)}, u32[]{:S(2)}, u32[]{:S(2)}) collective-permute-start(bf16[2,112,128]{2,1,0:T(8,128)(2,1)S(1)} %get-tuple-element.37), channel_id=1, source_target_pairs={{0,4},{4,0},{8,12},{12,8},{1,5},{5,1},{9,13},{13,9},{2,6},{6,2},{1... | collective-permute-start | bytes 172040 | tf_op jit(solution)/shard_map/ppermute | solution.py:234
  17.8 1.5 %collective-permute-start.7 = (bf16[2,2,256,128]{3,2,1,0:T(8,128)(2,1)S(1)}, bf16[2,2,256,128]{3,2,1,0:T(8,128)(2,1)S(1)}, u32[]{:S(2)}, u32[]{:S(2)}) collective-permute-start(bf16[2,2,256,128]{3,2,1,0:T(8,128)(2,1)S(1)} %hold.6.refs_2_), channel_id=1, source_target_pairs={{0,1},{1,0},{2,3},{3,2},{4,5},{5,4},{6,7},{7,6},{8,9},{9,8},{10,11... | collective-permute-start | bytes 786440 | tf_op jit(solution)/shard_map/ppermute | solution.py:234

commit v6 on v5

--- a/solution.py
+++ b/solution.py
@@ -27,35 +27,40 @@
         copy.wait()
 
 
-def strips_kernel(team, homed, head_width, q_hbm, k_hbm, v_hbm, *refs):
+def first_row(member, homed, free):
+    return pl.multiple_of(member * (homed + free), STRIP)
+
+
+def strips_kernel(team, free, head_width, q_hbm, k_hbm, v_hbm, *refs):
     pairs, mates, sems = refs[:team], refs[team:-1], refs[-1]
-    member = lax.axis_index("frame") % team
-    free = k_hbm.shape[1] - team * homed
+    homed = pairs[0].shape[2]
+    span = homed + free
     copies = []
     for step in range(team):
-        start = pl.multiple_of((member + step) % team * homed, STRIP)
-        cuts = [array.at[:, pl.ds(start, homed), head_width:] for array in (k_hbm, v_hbm, q_hbm)]
-        copies += [(cut, pairs[step].at[which]) for which, cut in enumerate(cuts[:2])]
+        member = (lax.axis_index("frame") + step) % team
+        start = first_row(member, homed, free)
+        for n, array in enumerate((k_hbm, v_hbm)):
+            copies.append((array.at[:, pl.ds(start, homed), head_width:], pairs[step].at[n]))
         if step:
-            mate = mates[step - 1]
-            copies += [(cut, mate.at[:, pl.ds(n * homed, homed)]) for n, cut in enumerate(cuts)]
-            if free:
-                for n, array in enumerate((k_hbm, v_hbm)):
-                    cut = array.at[:, team * homed :, head_width:]
-                    copies.append((cut, mate.at[:, pl.ds(3 * homed + n * free, free)]))
+            mate, wide = mates[step - 1], pl.multiple_of(member * homed, STRIP)
+            for n, array in enumerate((k_hbm, v_hbm)):
+                cut = array.at[:, pl.ds(wide, span), head_width:]
+                copies.append((cut, mate.at[:, pl.ds(n * span, span)]))
+            cut = q_hbm.at[:, pl.ds(start, homed), head_width:]
+            copies.append((cut, mate.at[:, pl.ds(2 * span, homed)]))
     run_copies(copies, sems)
 
 
-def rest_kernel(team, homed, q_hbm, k_hbm, v_hbm, _, q_own, kv_ref, q_spatial, *refs):
-    sems, head_width = refs[-1], q_spatial.shape[2]
-    start = pl.multiple_of(lax.axis_index("frame") % team * homed, STRIP)
+def rest_kernel(team, free, q_hbm, k_hbm, v_hbm, _, q_own, kv_ref, q_spatial, *refs):
+    sems, head_width, homed = refs[-1], q_spatial.shape[2], q_own.shape[1]
+    start = first_row(lax.axis_index("frame") % team, homed, free)
     copies = [(array.at[:, :, :head_width], kv_ref.at[n]) for n, array in enumerate((k_hbm, v_hbm))]
     copies.append((q_hbm.at[:, :, :head_width], q_spatial))
     copies.append((q_hbm.at[:, pl.ds(start, homed), head_width:], q_own))
-    if len(refs) > 1:
+    if free:
         for n, array in enumerate((k_hbm, v_hbm, q_hbm)):
             dst = refs[1] if n == 2 else refs[0].at[n]
-            copies.append((array.at[:, team * homed :, head_width:], dst))
+            copies.append((array.at[:, homed : homed + free, head_width:], dst))
     run_copies(copies, sems)
 
 
@@ -77,7 +82,12 @@
     def gather(parts, cut):
         return jnp.concatenate([part[f, cut] for part in parts for f in range(frames_dev)])
 
-    scores = [score(gather(queries, cut), gather(keys, cut), score_scale) for cut in cuts]
+    scores = []
+    for at in range(0, len(cuts), 2):
+        query, key = ([gather(parts, cut) for cut in cuts[at : at + 2]] for parts in (queries, keys))
+        both = score(jnp.concatenate(query), jnp.concatenate(key), score_scale)
+        q, k = query[0].shape[0], key[0].shape[0]
+        scores += [both[n * q : (n + 1) * q, n * k : (n + 1) * k] for n in range(len(query))]
     highest = [jnp.max(s, axis=-1, keepdims=True) for s in scores]
     expo = [jnp.exp(s - h) for s, h in zip(scores, highest)]
     totals = [jnp.sum(e, axis=-1, keepdims=True) for e in expo]
@@ -90,28 +100,29 @@
                 ref[frame, cut] = result[lower : lower + STRIP]
 
 
-def homed_kernel(team, others, passed, score_scale, own, query, *refs):
-    mates, others = refs[: team - 1], refs[team - 1 : team - 1 + others]
-    outs = refs[len(mates) + len(others) + passed :][:team]
+def homed_kernel(team, others, free, score_scale, own, query, *refs):
+    mates, others, outs = refs[: team - 1], refs[team - 1 : team - 1 + others], refs[-team:]
     homed = query.shape[1]
-
-    def part(which):
-        return [mate.at[:, pl.ds(which * homed, homed)] for mate in mates]
+    span, skip = homed + free, lax.axis_index("frame") % team * free
+
+    def part(start):
+        return [mate.at[:, pl.ds(pl.multiple_of(start, STRIP), homed)] for mate in mates]
 
     keys, values = (
-        [own.at[n], *part(n), *(block.at[n] for block in others)] for n in range(2)
+        [own.at[n], *part(n * span + skip), *(block.at[n] for block in others)] for n in range(2)
     )
-    attend_strips([query, *part(2)], keys, values, outs, score_scale)
-
-
-def pack_kernel(team, homed, arrived, own, *refs):
-    mates, (packed, sems) = refs[: team - 1], (refs[-2], refs[-1])
+    attend_strips([query, *part(2 * span)], keys, values, outs, score_scale)
+
+
+def pack_kernel(team, homed, own, *refs):
+    mates, packed, sems = refs[: team - 1], refs[-2], refs[-1]
     free = own.shape[2]
+    skip = (team - 1 - lax.axis_index("frame") % team) * homed
     copies = [(own, packed.at[0])]
     for number, mate in enumerate(mates):
         for n in range(2):
-            src = mate.at[:, pl.ds(3 * homed + n * free, free)]
-            copies.append((src, packed.at[1 + number, n]))
+            start = pl.multiple_of(n * (homed + free) + skip, STRIP)
+            copies.append((mate.at[:, pl.ds(start, free)], packed.at[1 + number, n]))
     run_copies(copies, sems)
 
 
@@ -134,10 +145,21 @@
         acc_ref[frame] = mix(expo, value)
 
 
-def last_kernel(score_scale, pieces, q_ref, *refs):
-    kvs, (top_ref, total_ref, acc_ref, out_hbm, o_ref, sems) = refs[:pieces], refs[pieces:]
-    head_width = q_ref.shape[-1]
-    for frame in range(q_ref.shape[0]):
+def last_kernel(score_scale, pieces, team, q_ref, *refs):
+    kvs, (top_ref, total_ref, acc_ref), refs = refs[:pieces], refs[pieces : pieces + 3], refs[pieces + 3 :]
+    ready, (out_hbm, o_ref, sems) = refs[:-3], refs[-3:]
+    frames, _, head_width = q_ref.shape
+    homed, free = ready[0].shape[1], sum(ref.shape[1] for ref in ready[1:])
+    starts = [first_row(lax.axis_index("frame") % team, homed, free), homed]
+    copies = []
+
+    def send(src, dst):
+        copies.append(pltpu.make_async_copy(src, dst, sems.at[len(copies)]))
+        copies[-1].start()
+
+    for start, ref in zip(starts, ready):
+        send(ref, out_hbm.at[:, pl.ds(start, ref.shape[1]), head_width:])
+    for frame in range(frames):
         key = jnp.concatenate([kv[0, frame] for kv in kvs])
         value = jnp.concatenate([kv[1, frame] for kv in kvs])
         scores = score(q_ref[frame], key, score_scale)
@@ -146,17 +168,17 @@
         factor = jnp.exp(top_ref[frame] - highest)
         total = total_ref[frame] * factor + jnp.sum(expo, axis=-1, keepdims=True)
         o_ref[frame] = ((acc_ref[frame] * factor + mix(expo, value)) / total).astype(jnp.bfloat16)
-    run_copies([(o_ref, out_hbm.at[:, :, :head_width])], sems)
-
-
-def join_kernel(team, homed, head_width, *refs):
+        send(o_ref.at[frame], out_hbm.at[frame, :, :head_width])
+    for copy in copies:
+        copy.wait()
+
+
+def join_kernel(team, free, head_width, *refs):
     pieces, out_hbm, sems = refs[:-3], refs[-2], refs[-1]
-    member = lax.axis_index("frame") % team
     copies = []
-    for step, piece in enumerate(pieces):
-        start, rows = team * homed, piece.shape[1]
-        if step < team:
-            start = pl.multiple_of((member + step) % team * homed, STRIP)
+    for number, piece in enumerate(pieces):
+        rows = piece.shape[1]
+        start = first_row((lax.axis_index("frame") + 1 + number) % team, rows, free)
         copies.append((piece, out_hbm.at[:, pl.ds(start, rows), head_width:]))
     run_copies(copies, sems)
 
@@ -197,18 +219,18 @@
         pltpu.with_memory_space_constraint(array, pltpu.HBM) for array in (queries, keys, values)
     ]
     cut = call(
-        functools.partial(strips_kernel, team, homed, head_width),
+        functools.partial(strips_kernel, team, free, head_width),
         "strips",
         out_shape=[in_vmem(2, *block)] * team
         + [in_vmem(frames_dev, 3 * homed + 2 * free, head_width)] * (team - 1),
         in_specs=[hbm] * 3,
         out_specs=[vmem] * (2 * team - 1),
-        scratch_shapes=[pltpu.SemaphoreType.DMA((7 * team,))],
+        scratch_shapes=[pltpu.SemaphoreType.DMA((5 * team - 3,))],
     )(*arrays)
     pairs, triples = cut[:team], cut[team:]
     spares = [in_vmem(2, *spare), in_vmem(*spare)] if free else []
     query_own, kv_own, query_spatial, *spares = call(
-        functools.partial(rest_kernel, team, homed),
+        functools.partial(rest_kernel, team, free),
         "rest",
         out_shape=[in_vmem(*block), in_vmem(2, *whole), in_vmem(*whole), *spares],
         in_specs=[hbm] * 3 + [anywhere],
@@ -240,26 +262,21 @@
     if cross:
         [cross[team]] = hold([cross[team]], 1150)
     if free:
-        gate = [cross[team]] if cross else []
-        *gate, packed = call(
-            functools.partial(pack_kernel, team, homed, 0),
+        packed = call(
+            functools.partial(pack_kernel, team, homed),
             "pack",
-            mflops=0,
-            out_shape=[in_vmem(*g.shape) for g in gate] + [in_vmem(team, 2, *spare)],
-            in_specs=[vmem] * team + [anywhere] * len(gate),
-            out_specs=[anywhere] * len(gate) + [vmem],
-            scratch_shapes=[pltpu.SemaphoreType.DMA((1 + 2 * (team - 1),))],
-            input_output_aliases={team: 0} if gate else {},
-        )(spares[0], *mates, *gate)
-        if gate:
-            [cross[team]] = gate
+            out_shape=in_vmem(team, 2, *spare),
+            in_specs=[vmem] * team,
+            out_specs=vmem,
+            scratch_shapes=[pltpu.SemaphoreType.DMA((2 * team - 1,))],
+        )(spares[0], *mates)
         spread = [exchange(packed, "frame", step) for step in range(team, count, team)]
     held = hold([*mates, *cross.values()], 1900)
     mates, others = held[: team - 1], held[team - 1 :]
     across = hold(across, 100)
 
     strip_out = call(
-        functools.partial(homed_kernel, team, len(others), 0, score_scale),
+        functools.partial(homed_kernel, team, len(others), free, score_scale),
         "homed",
         mflops=0,
         out_shape=[in_vmem(*block)] * team,
@@ -280,18 +297,9 @@
     if free:
         held = hold([*spread, *running], 4000)
         spread, running = held[: len(spread)], held[len(spread) :]
-    out = call(
-        functools.partial(last_kernel, score_scale, len(late)),
-        "last",
-        out_shape=jax.ShapeDtypeStruct(queries.shape, dtype),
-        in_specs=[vmem] * (4 + len(late)),
-        out_specs=hbm,
-        scratch_shapes=[pltpu.VMEM(whole, dtype), pltpu.SemaphoreType.DMA((1,))],
-    )(query_spatial, *late, *running)
-
-    pieces = [strip_out[0], *returned]
+    ready = [strip_out[0]]
     if free:
-        pieces.append(
+        ready.append(
             call(
                 functools.partial(free_kernel, team, score_scale),
                 "free",
@@ -300,15 +308,27 @@
                 out_specs=vmem,
             )(spares[1], packed, *spread)
         )
+    out = call(
+        functools.partial(last_kernel, score_scale, len(late), team),
+        "last",
+        out_shape=jax.ShapeDtypeStruct(queries.shape, dtype),
+        in_specs=[vmem] * (4 + len(late) + len(ready)),
+        out_specs=hbm,
+        scratch_shapes=[
+            pltpu.VMEM(whole, dtype),
+            pltpu.SemaphoreType.DMA((frames_dev + len(ready),)),
+        ],
+    )(query_spatial, *late, *running, *ready)
+
     return call(
-        functools.partial(join_kernel, team, homed, head_width),
+        functools.partial(join_kernel, team, free, head_width),
         "join",
         out_shape=jax.ShapeDtypeStruct(queries.shape, dtype),
-        in_specs=[vmem] * len(pieces) + [hbm],
+        in_specs=[vmem] * len(returned) + [hbm],
         out_specs=hbm,
-        scratch_shapes=[pltpu.SemaphoreType.DMA((len(pieces),))],
-        input_output_aliases={len(pieces): 0},
-    )(*pieces, out)
+        scratch_shapes=[pltpu.SemaphoreType.DMA((max(1, len(returned)),))],
+        input_output_aliases={len(returned): 0},
+    )(*returned, out)
 
 
 def solution(mesh):

time: 22 us -> 21.9 us (level)
  no operation moved by 1% of the time
where the time goes in v6:
time: 21.9 us; the launch traced here: 21.7 us
  starting transfers between devices  10.7 us (49%)
  Pallas kernels  6.28 us (29%)
  waiting for transfers between devices  4.68 us (21%)
    ppermute x8, starting transfers between devices, exchange(): lax.ppermute(array, axis, [(i, partner_of(i, step, size)) for i in range(...  10.7 us
    ppermute x8, waiting for transfers between devices, exchange(): lax.ppermute(array, axis, [(i, partner_of(i, step, size)) for i in range(...  4.68 us
    pallas_call x1, Pallas kernels, body(): call(functools.partial(last_kernel, score_scale, len(late), team), 'last'...  1.54 us
    pallas_call x1, Pallas kernels, body(): call(functools.partial(strips_kernel, team, free, head_width), 'strips',...  1.11 us
    pallas_call x1, Pallas kernels, body(): call(functools.partial(rest_kernel, team, free), 'rest', out_shape=[in_vm...  1.1 us
    pallas_call x1, Pallas kernels, body(): call(functools.partial(first_kernel, score_scale, len(early)), 'first', o...  1.03 us
    pallas_call x1, Pallas kernels, body(): call(functools.partial(join_kernel, team, free, head_width), 'join', out_...  0.63 us
  transfers between devices with their start and end apart: 8, of which 5 were waited for; matrix products, arithmetic and copies ran while one was open for 0% of the time, Pallas kernels for 21%

profile of v6, /device:TPU:0, one launch (start us, length us, event | category | flops | bytes accessed | tf_op | source)
XLA Modules:
  0.0 21.7 jit_solution(6247868636863590924)
XLA Ops:
  0.0 1.1 %strips.1 = (bf16[2,2,112,128]{3,2,1,0:T(8,128)(2,1)S(1)}, bf16[2,2,112,128]{3,2,1,0:T(8,128)(2,1)S(1)}, bf16[2,400,128]{2,1,0:T(8,128)(2,1)S(1)}) custom-call(bf16[2,256,256]{2,1,0:T(8,128)(2,1)} %q_hbm.3, bf16[2,256,256]{2,1,0:T(8,128)(2,1)} %k_hbm.3, bf16[2,256,256]{2,1,0:T(8,128)(2,1)} %v_hbm.3), custom_call_target="tpu_custom_call" | custom-call | flops 1 | bytes 1 | tf_op jit(solution)/shard_map/strips/pallas_call | solution.py:221
  1.1 4.1 %collective-permute-start.1 = (bf16[2,2,112,128]{3,2,1,0:T(8,128)(2,1)S(1)}, bf16[2,2,112,128]{3,2,1,0:T(8,128)(2,1)S(1)}, u32[]{:S(2)}, u32[]{:S(2)}) collective-permute-start(bf16[2,2,112,128]{3,2,1,0:T(8,128)(2,1)S(1)} %get-tuple-element.25._.own), channel_id=1, source_target_pairs={{0,8},{4,12},{8,0},{12,4},{1,9},{5,13},{9,1},{13,5},{2,10},{6,14},... | collective-permute-start | bytes 344072 | tf_op jit(solution)/shard_map/ppermute | solution.py:256
  5.2 1.6 %collective-permute-start = (bf16[2,400,128]{2,1,0:T(8,128)(2,1)S(1)}, bf16[2,400,128]{2,1,0:T(8,128)(2,1)S(1)}, u32[]{:S(2)}, u32[]{:S(2)}) collective-permute-start(bf16[2,400,128]{2,1,0:T(8,128)(2,1)S(1)} %get-tuple-element.27), channel_id=1, source_target_pairs={{0,4},{4,0},{8,12},{12,8},{1,5},{5,1},{9,13},{13,9},{2,6},{6,2},{1... | collective-permute-start | bytes 614408 | tf_op jit(solution)/shard_map/ppermute | solution.py:256
  6.8 0.0 collective-permute-start.2
  6.8 1.1 %rest.1 = (bf16[2,112,128]{2,1,0:T(8,128)(2,1)S(1)}, bf16[2,2,256,128]{3,2,1,0:T(8,128)(2,1)S(1)}, bf16[2,256,128]{2,1,0:T(8,128)(2,1)S(1)}, bf16[2,2,32,128]{3,2,1,0:T(8,128)(2,1)S(1)}, bf16[2,32,128]{2,1,0:T(8,128)(2,1)S(1)}) custom-call(bf16[2,256,256]{2,1,0:T(8,128)(2,1)} %q_hbm.3, bf16[2,256,256]{2,1,0:T(8,128)(2,1)} %k_hbm.3, ...), custom_call_target="tpu_custom_call" | custom-call | flops 1 | bytes 1 | tf_op jit(solution)/shard_map/rest/pallas_call | solution.py:232
  7.9 0.1 collective-permute-start.7
  8.0 1.8 %collective-permute-start.4 = (bf16[2,2,256,128]{3,2,1,0:T(8,128)(2,1)S(1)}, bf16[2,2,256,128]{3,2,1,0:T(8,128)(2,1)S(1)}, u32[]{:S(2)}, u32[]{:S(2)}) collective-permute-start(bf16[2,2,256,128]{3,2,1,0:T(8,128)(2,1)S(1)} %get-tuple-element.34.refs_0_), channel_id=1, source_target_pairs={{0,2},{2,0},{1,3},{3,1},{4,6},{6,4},{5,7},{7,5},{8,10},{10,8},{9,1... | collective-permute-start | bytes 786440 | tf_op jit(solution)/shard_map/ppermute | solution.py:256
  9.8 1.9 %collective-permute-done.1.refs_0_ = bf16[2,2,112,128]{3,2,1,0:T(8,128)(2,1)S(1)} collective-permute-done((bf16[2,2,112,128]{3,2,1,0:T(8,128)(2,1)S(1)}, bf16[2,2,112,128]{3,2,1,0:T(8,128)(2,1)S(1)}, u32[]{:S(2)}, u32[]{:S(2)}) %collective-permute-start.1) | collective-permute-done | bytes 114720 | tf_op jit(solution)/shard_map/ppermute | solution.py:256
  11.7 1.7 %collective-permute-done.refs_0_ = bf16[2,400,128]{2,1,0:T(8,128)(2,1)S(1)} collective-permute-done((bf16[2,400,128]{2,1,0:T(8,128)(2,1)S(1)}, bf16[2,400,128]{2,1,0:T(8,128)(2,1)S(1)}, u32[]{:S(2)}, u32[]{:S(2)}) %collective-permute-start) | collective-permute-done | bytes 204832 | tf_op jit(solution)/shard_map/ppermute | solution.py:256
  13.3 0.1 pack.1.refs_0_
  13.4 2.3 %collective-permute-start.6 = (bf16[2,2,2,32,128]{4,3,2,1,0:T(8,128)(2,1)S(1)}, bf16[2,2,2,32,128]{4,3,2,1,0:T(8,128)(2,1)S(1)}, u32[]{:S(2)}, u32[]{:S(2)}) collective-permute-start(bf16[2,2,2,32,128]{4,3,2,1,0:T(8,128)(2,1)S(1)} %pack.1.refs_0_), channel_id=1, source_target_pairs={{0,8},{4,12},{8,0},{12,4},{1,9},{5,13},{9,1},{13,5},{2,10},{6,14},... | collective-permute-start | bytes 196616 | tf_op jit(solution)/shard_map/ppermute | solution.py:256
  15.7 0.7 %collective-permute-done.2.refs_2_ = bf16[2,2,112,128]{3,2,1,0:T(8,128)(2,1)S(1)} collective-permute-done((bf16[2,2,112,128]{3,2,1,0:T(8,128)(2,1)S(1)}, bf16[2,2,112,128]{3,2,1,0:T(8,128)(2,1)S(1)}, u32[]{:S(2)}, u32[]{:S(2)}) %collective-permute-start.2) | collective-permute-done | bytes 114720 | tf_op jit(solution)/shard_map/ppermute | solution.py:256
  16.4 0.4 %homed.1 = (bf16[2,112,128]{2,1,0:T(8,128)(2,1)S(1)}, bf16[2,112,128]{2,1,0:T(8,128)(2,1)S(1)}) custom-call(bf16[2,2,112,128]{3,2,1,0:T(8,128)(2,1)S(1)} %get-tuple-element.25._.own, bf16[2,112,128]{2,1,0:T(8,128)(2,1)S(1)} %get-tuple-element.26.query, bf16[2,400,128]{2,1,0:T(8,128)(2,1)S(1)} %get-tuple-element.29.refs_0_, ...), custom_call_target="tpu_custom_call" | custom-call | flops 1 | bytes 1 | tf_op jit(solution)/shard_map/homed/pallas_call | solution.py:278
  16.8 0.9 %collective-permute-start.3 = (bf16[2,112,128]{2,1,0:T(8,128)(2,1)S(1)}, bf16[2,112,128]{2,1,0:T(8,128)(2,1)S(1)}, u32[]{:S(2)}, u32[]{:S(2)}) collective-permute-start(bf16[2,112,128]{2,1,0:T(8,128)(2,1)S(1)} %get-tuple-element.32), channel_id=1, source_target_pairs={{0,4},{4,0},{8,12},{12,8},{1,5},{5,1},{9,13},{13,9},{2,6},{6,2},{1... | collective-permute-start | bytes 172040 | tf_op jit(solution)/shard_map/ppermute | solution.py:256
  17.7 0.0 collective-permute-done.4.refs_0_
  17.8 0.0 collective-permute-start.5
  17.8 0.0 collective-permute-done.7.refs_1_
  17.8 1.0 %first.1 = (f32[2,256,1]{2,1,0:T(8,128)S(1)}, f32[2,256,1]{2,1,0:T(8,128)S(1)}, f32[2,256,128]{2,1,0:T(8,128)S(1)}) custom-call(bf16[2,256,128]{2,1,0:T(8,128)(2,1)S(1)} %get-tuple-element.33.q_ref, bf16[2,2,256,128]{3,2,1,0:T(8,128)(2,1)S(1)} %get-tuple-element.34.refs_0_, bf16[2,2,256,128]{3,2,1,0:T(8,128)(2,1)S(1)} %collective-permute-done.7.refs_1_, ...), custom_call_target="tpu_custom_call" | custom-call | flops 1 | bytes 1 | tf_op jit(solution)/shard_map/first/pallas_call | solution.py:290
  18.8 0.0 collective-permute-done.6.refs_0_
  18.8 0.4 %free.1.refs_5_ = bf16[2,32,128]{2,1,0:T(8,128)(2,1)S(1)} custom-call(bf16[2,32,128]{2,1,0:T(8,128)(2,1)S(1)} %get-tuple-element.43.query, bf16[2,2,2,32,128]{4,3,2,1,0:T(8,128)(2,1)S(1)} %pack.1.refs_0_, bf16[2,2,2,32,128]{4,3,2,1,0:T(8,128)(2,1)S(1)} %get-tuple-element.44.refs_1_), custom_call_target="tpu_custom_call" | custom-call | flops 1 | bytes 1 | tf_op jit(solution)/shard_map/free/pallas_call | solution.py:303
  19.2 0.1 collective-permute-done.5.refs_0_
  19.3 1.5 %last.1.refs_1_ = bf16[2,256,256]{2,1,0:T(8,128)(2,1)} custom-call(bf16[2,256,128]{2,1,0:T(8,128)(2,1)S(1)} %get-tuple-element.33.q_ref, bf16[2,2,256,128]{3,2,1,0:T(8,128)(2,1)S(1)} %collective-permute-done.5.refs_0_, f32[2,256,1]{2,1,0:T(8,128)S(1)} %get-tuple-element.39.refs_1_, f32[2,256,1]{2,1,0:T(8,128)S(1)} %get-tuple-element.40.refs_2_, ...), custom_call_target="tpu_custom_call" | custom-call | flops 1 | bytes 1 | tf_op jit(solution)/shard_map/last/pallas_call | solution.py:311
  20.8 0.3 %collective-permute-done.3.refs_0_ = bf16[2,112,128]{2,1,0:T(8,128)(2,1)S(1)} collective-permute-done((bf16[2,112,128]{2,1,0:T(8,128)(2,1)S(1)}, bf16[2,112,128]{2,1,0:T(8,128)(2,1)S(1)}, u32[]{:S(2)}, u32[]{:S(2)}) %collective-permute-start.3) | collective-permute-done | bytes 57376 | tf_op jit(solution)/shard_map/ppermute | solution.py:256
  21.1 0.6 %join.1 = bf16[2,256,256]{2,1,0:T(8,128)(2,1)} custom-call(bf16[2,112,128]{2,1,0:T(8,128)(2,1)S(1)} %collective-permute-done.3.refs_0_, bf16[2,256,256]{2,1,0:T(8,128)(2,1)} %last.1.refs_1_), custom_call_target="tpu_custom_call", output_to_operand_aliasing={{}: (1, {})} | custom-call | flops 1 | bytes 1 | tf_op jit(solution)/shard_map/join/pallas_call | solution.py:323
  (4 shorter events, 0.0 us)
Async XLA Ops:
  1.1 10.5 %collective-permute-start.1 = (bf16[2,2,112,128]{3,2,1,0:T(8,128)(2,1)S(1)}, bf16[2,2,112,128]{3,2,1,0:T(8,128)(2,1)S(1)}, u32[]{:S(2)}, u32[]{:S(2)}) collective-permute-start(bf16[2,2,112,128]{3,2,1,0:T(8,128)(2,1)S(1)} %get-tuple-element.25._.own), channel_id=1, source_target_pairs={{0,8},{4,12},{8,0},{12,4},{1,9},{5,13},{9,1},{13,5},{2,10},{6,14},... | collective-permute-start | bytes 344072 | tf_op jit(solution)/shard_map/ppermute | solution.py:256
  5.2 8.1 %collective-permute-start = (bf16[2,400,128]{2,1,0:T(8,128)(2,1)S(1)}, bf16[2,400,128]{2,1,0:T(8,128)(2,1)S(1)}, u32[]{:S(2)}, u32[]{:S(2)}) collective-permute-start(bf16[2,400,128]{2,1,0:T(8,128)(2,1)S(1)} %get-tuple-element.27), channel_id=1, source_target_pairs={{0,4},{4,0},{8,12},{12,8},{1,5},{5,1},{9,13},{13,9},{2,6},{6,2},{1... | collective-permute-start | bytes 614408 | tf_op jit(solution)/shard_map/ppermute | solution.py:256
  6.8 9.6 %collective-permute-start.2 = (bf16[2,2,112,128]{3,2,1,0:T(8,128)(2,1)S(1)}, bf16[2,2,112,128]{3,2,1,0:T(8,128)(2,1)S(1)}, u32[]{:S(2)}, u32[]{:S(2)}) collective-permute-start(bf16[2,2,112,128]{3,2,1,0:T(8,128)(2,1)S(1)} %get-tuple-element.28), channel_id=1, source_target_pairs={{0,12},{4,8},{8,4},{12,0},{1,13},{5,9},{9,5},{13,1},{2,14},{6,10},... | collective-permute-start | bytes 344072 | tf_op jit(solution)/shard_map/ppermute | solution.py:256
  7.9 9.9 %collective-permute-start.7 = (bf16[2,2,256,128]{3,2,1,0:T(8,128)(2,1)S(1)}, bf16[2,2,256,128]{3,2,1,0:T(8,128)(2,1)S(1)}, u32[]{:S(2)}, u32[]{:S(2)}) collective-permute-start(bf16[2,2,256,128]{3,2,1,0:T(8,128)(2,1)S(1)} %get-tuple-element.34.refs_0_), channel_id=1, source_target_pairs={{0,1},{1,0},{2,3},{3,2},{4,5},{5,4},{6,7},{7,6},{8,9},{9,8},{10,11... | collective-permute-start | bytes 786440 | tf_op jit(solution)/shard_map/ppermute | solution.py:256
  8.0 9.8 %collective-permute-start.4 = (bf16[2,2,256,128]{3,2,1,0:T(8,128)(2,1)S(1)}, bf16[2,2,256,128]{3,2,1,0:T(8,128)(2,1)S(1)}, u32[]{:S(2)}, u32[]{:S(2)}) collective-permute-start(bf16[2,2,256,128]{3,2,1,0:T(8,128)(2,1)S(1)} %get-tuple-element.34.refs_0_), channel_id=1, source_target_pairs={{0,2},{2,0},{1,3},{3,1},{4,6},{6,4},{5,7},{7,5},{8,10},{10,8},{9,1... | collective-permute-start | bytes 786440 | tf_op jit(solution)/shard_map/ppermute | solution.py:256
  13.4 5.4 %collective-permute-start.6 = (bf16[2,2,2,32,128]{4,3,2,1,0:T(8,128)(2,1)S(1)}, bf16[2,2,2,32,128]{4,3,2,1,0:T(8,128)(2,1)S(1)}, u32[]{:S(2)}, u32[]{:S(2)}) collective-permute-start(bf16[2,2,2,32,128]{4,3,2,1,0:T(8,128)(2,1)S(1)} %pack.1.refs_0_), channel_id=1, source_target_pairs={{0,8},{4,12},{8,0},{12,4},{1,9},{5,13},{9,1},{13,5},{2,10},{6,14},... | collective-permute-start | bytes 196616 | tf_op jit(solution)/shard_map/ppermute | solution.py:256
  16.8 4.2 %collective-permute-start.3 = (bf16[2,112,128]{2,1,0:T(8,128)(2,1)S(1)}, bf16[2,112,128]{2,1,0:T(8,128)(2,1)S(1)}, u32[]{:S(2)}, u32[]{:S(2)}) collective-permute-start(bf16[2,112,128]{2,1,0:T(8,128)(2,1)S(1)} %get-tuple-element.32), channel_id=1, source_target_pairs={{0,4},{4,0},{8,12},{12,8},{1,5},{5,1},{9,13},{13,9},{2,6},{6,2},{1... | collective-permute-start | bytes 172040 | tf_op jit(solution)/shard_map/ppermute | solution.py:256
  17.8 1.5 %collective-permute-start.5 = (bf16[2,2,256,128]{3,2,1,0:T(8,128)(2,1)S(1)}, bf16[2,2,256,128]{3,2,1,0:T(8,128)(2,1)S(1)}, u32[]{:S(2)}, u32[]{:S(2)}) collective-permute-start(bf16[2,2,256,128]{3,2,1,0:T(8,128)(2,1)S(1)} %hold.6.refs_2_), channel_id=1, source_target_pairs={{0,1},{1,0},{2,3},{3,2},{4,5},{5,4},{6,7},{7,6},{8,9},{9,8},{10,11... | collective-permute-start | bytes 786440 | tf_op jit(solution)/shard_map/ppermute | solution.py:256

commit v7 on v6

--- a/solution.py
+++ b/solution.py
@@ -145,21 +145,9 @@
         acc_ref[frame] = mix(expo, value)
 
 
-def last_kernel(score_scale, pieces, team, q_ref, *refs):
-    kvs, (top_ref, total_ref, acc_ref), refs = refs[:pieces], refs[pieces : pieces + 3], refs[pieces + 3 :]
-    ready, (out_hbm, o_ref, sems) = refs[:-3], refs[-3:]
-    frames, _, head_width = q_ref.shape
-    homed, free = ready[0].shape[1], sum(ref.shape[1] for ref in ready[1:])
-    starts = [first_row(lax.axis_index("frame") % team, homed, free), homed]
-    copies = []
-
-    def send(src, dst):
-        copies.append(pltpu.make_async_copy(src, dst, sems.at[len(copies)]))
-        copies[-1].start()
-
-    for start, ref in zip(starts, ready):
-        send(ref, out_hbm.at[:, pl.ds(start, ref.shape[1]), head_width:])
-    for frame in range(frames):
+def last_kernel(score_scale, pieces, q_ref, *refs):
+    kvs, (top_ref, total_ref, acc_ref, o_ref) = refs[:pieces], refs[pieces:]
+    for frame in range(q_ref.shape[0]):
         key = jnp.concatenate([kv[0, frame] for kv in kvs])
         value = jnp.concatenate([kv[1, frame] for kv in kvs])
         scores = score(q_ref[frame], key, score_scale)
@@ -168,17 +156,18 @@
         factor = jnp.exp(top_ref[frame] - highest)
         total = total_ref[frame] * factor + jnp.sum(expo, axis=-1, keepdims=True)
         o_ref[frame] = ((acc_ref[frame] * factor + mix(expo, value)) / total).astype(jnp.bfloat16)
-        send(o_ref.at[frame], out_hbm.at[frame, :, :head_width])
-    for copy in copies:
-        copy.wait()
-
-
-def join_kernel(team, free, head_width, *refs):
-    pieces, out_hbm, sems = refs[:-3], refs[-2], refs[-1]
-    copies = []
+
+
+def join_kernel(team, free, spatial, *refs):
+    pieces, out_hbm, sems = refs[:-2], refs[-2], refs[-1]
+    head_width = spatial.shape[2]
+    copies = [(spatial, out_hbm.at[:, :, :head_width])]
     for number, piece in enumerate(pieces):
         rows = piece.shape[1]
-        start = first_row((lax.axis_index("frame") + 1 + number) % team, rows, free)
+        if number < team:
+            start = first_row((lax.axis_index("frame") + number) % team, rows, free)
+        else:
+            start = pieces[0].shape[1]
         copies.append((piece, out_hbm.at[:, pl.ds(start, rows), head_width:]))
     run_copies(copies, sems)
 
@@ -297,9 +286,9 @@
     if free:
         held = hold([*spread, *running], 4000)
         spread, running = held[: len(spread)], held[len(spread) :]
-    ready = [strip_out[0]]
+    pieces = [strip_out[0], *returned]
     if free:
-        ready.append(
+        pieces.append(
             call(
                 functools.partial(free_kernel, team, score_scale),
                 "free",
@@ -308,27 +297,22 @@
                 out_specs=vmem,
             )(spares[1], packed, *spread)
         )
-    out = call(
-        functools.partial(last_kernel, score_scale, len(late), team),
+    spatial = call(
+        functools.partial(last_kernel, score_scale, len(late)),
         "last",
-        out_shape=jax.ShapeDtypeStruct(queries.shape, dtype),
-        in_specs=[vmem] * (4 + len(late) + len(ready)),
-        out_specs=hbm,
-        scratch_shapes=[
-            pltpu.VMEM(whole, dtype),
-            pltpu.SemaphoreType.DMA((frames_dev + len(ready),)),
-        ],
-    )(query_spatial, *late, *running, *ready)
+        out_shape=in_vmem(*whole),
+        in_specs=[vmem] * (4 + len(late)),
+        out_specs=vmem,
+    )(query_spatial, *late, *running)
 
     return call(
-        functools.partial(join_kernel, team, free, head_width),
+        functools.partial(join_kernel, team, free),
         "join",
         out_shape=jax.ShapeDtypeStruct(queries.shape, dtype),
-        in_specs=[vmem] * len(returned) + [hbm],
+        in_specs=[vmem] * (1 + len(pieces)),
         out_specs=hbm,
-        scratch_shapes=[pltpu.SemaphoreType.DMA((max(1, len(returned)),))],
-        input_output_aliases={len(returned): 0},
-    )(*returned, out)
+        scratch_shapes=[pltpu.SemaphoreType.DMA((1 + len(pieces),))],
+    )(spatial, *pieces)
 
 
 def solution(mesh):

time: 21.9 us -> 22 us (level)
  waiting for transfers between devices: 4.68 us -> 5.36 us
  Pallas kernels: 6.28 us -> 5.69 us
    ppermute x8, waiting for transfers between devices: 4.68 us -> 5.36 us  [exchange(): lax.ppermute(array, axis, [(i, partner_of(i, step, size)) for i in range(...]
    pallas_call x2, Pallas kernels: 2.17 us -> 1.59 us  [the longest x1 0.87 us: body(): call(functools.partial(last_kernel, score_scale, len(late)), 'last', out_...]
  transfers between devices with their start and end apart: 8 -> 8, of which waited for: 5 -> 5; matrix products, arithmetic and copies ran while one was open for 0% -> 0% of each run, Pallas kernels for 21% -> 18%
where the time goes in v7:
time: 22 us; the launch traced here: 21.8 us
  starting transfers between devices  10.7 us (49%)
  Pallas kernels  5.69 us (26%)
  waiting for transfers between devices  5.36 us (24%)
    ppermute x8, starting transfers between devices, exchange(): lax.ppermute(array, axis, [(i, partner_of(i, step, size)) for i in range(...  10.7 us
    ppermute x8, waiting for transfers between devices, exchange(): lax.ppermute(array, axis, [(i, partner_of(i, step, size)) for i in range(...  5.36 us
    pallas_call x1, Pallas kernels, body(): call(functools.partial(strips_kernel, team, free, head_width), 'strips',...  1.11 us
    pallas_call x1, Pallas kernels, body(): call(functools.partial(rest_kernel, team, free), 'rest', out_shape=[in_vm...  1.1 us
    pallas_call x1, Pallas kernels, body(): call(functools.partial(first_kernel, score_scale, len(early)), 'first', o...  1.03 us
    pallas_call x1, Pallas kernels, body(): call(functools.partial(last_kernel, score_scale, len(late)), 'last', out_...  0.87 us
    pallas_call x1, Pallas kernels, body(): call(functools.partial(join_kernel, team, free), 'join', out_shape=jax.Sh...  0.72 us
  transfers between devices with their start and end apart: 8, of which 5 were waited for; matrix products, arithmetic and copies ran while one was open for 0% of the time, Pallas kernels for 18%

profile of v7, /device:TPU:0, one launch (start us, length us, event | category | flops | bytes accessed | tf_op | source)
XLA Modules:
  0.0 21.8 jit_solution(16597786529541780618)
XLA Ops:
  0.0 1.1 %strips.1 = (bf16[2,2,112,128]{3,2,1,0:T(8,128)(2,1)S(1)}, bf16[2,2,112,128]{3,2,1,0:T(8,128)(2,1)S(1)}, bf16[2,400,128]{2,1,0:T(8,128)(2,1)S(1)}) custom-call(bf16[2,256,256]{2,1,0:T(8,128)(2,1)} %q_hbm.3, bf16[2,256,256]{2,1,0:T(8,128)(2,1)} %k_hbm.3, bf16[2,256,256]{2,1,0:T(8,128)(2,1)} %v_hbm.3), custom_call_target="tpu_custom_call" | custom-call | flops 1 | bytes 1 | tf_op jit(solution)/shard_map/strips/pallas_call | solution.py:210
  1.1 4.1 %collective-permute-start.5 = (bf16[2,2,112,128]{3,2,1,0:T(8,128)(2,1)S(1)}, bf16[2,2,112,128]{3,2,1,0:T(8,128)(2,1)S(1)}, u32[]{:S(2)}, u32[]{:S(2)}) collective-permute-start(bf16[2,2,112,128]{3,2,1,0:T(8,128)(2,1)S(1)} %get-tuple-element.25._.own), channel_id=1, source_target_pairs={{0,8},{4,12},{8,0},{12,4},{1,9},{5,13},{9,1},{13,5},{2,10},{6,14},... | collective-permute-start | bytes 344072 | tf_op jit(solution)/shard_map/ppermute | solution.py:245
  5.2 1.6 %collective-permute-start.2 = (bf16[2,400,128]{2,1,0:T(8,128)(2,1)S(1)}, bf16[2,400,128]{2,1,0:T(8,128)(2,1)S(1)}, u32[]{:S(2)}, u32[]{:S(2)}) collective-permute-start(bf16[2,400,128]{2,1,0:T(8,128)(2,1)S(1)} %get-tuple-element.29), channel_id=1, source_target_pairs={{0,4},{4,0},{8,12},{12,8},{1,5},{5,1},{9,13},{13,9},{2,6},{6,2},{1... | collective-permute-start | bytes 614408 | tf_op jit(solution)/shard_map/ppermute | solution.py:245
  6.8 0.0 collective-permute-start.6
  6.8 1.1 %rest.1 = (bf16[2,112,128]{2,1,0:T(8,128)(2,1)S(1)}, bf16[2,2,256,128]{3,2,1,0:T(8,128)(2,1)S(1)}, bf16[2,256,128]{2,1,0:T(8,128)(2,1)S(1)}, bf16[2,2,32,128]{3,2,1,0:T(8,128)(2,1)S(1)}, bf16[2,32,128]{2,1,0:T(8,128)(2,1)S(1)}) custom-call(bf16[2,256,256]{2,1,0:T(8,128)(2,1)} %q_hbm.3, bf16[2,256,256]{2,1,0:T(8,128)(2,1)} %k_hbm.3, ...), custom_call_target="tpu_custom_call" | custom-call | flops 1 | bytes 1 | tf_op jit(solution)/shard_map/rest/pallas_call | solution.py:221
  7.9 0.1 collective-permute-start.4
  8.0 1.8 %collective-permute-start = (bf16[2,2,256,128]{3,2,1,0:T(8,128)(2,1)S(1)}, bf16[2,2,256,128]{3,2,1,0:T(8,128)(2,1)S(1)}, u32[]{:S(2)}, u32[]{:S(2)}) collective-permute-start(bf16[2,2,256,128]{3,2,1,0:T(8,128)(2,1)S(1)} %get-tuple-element.27.refs_0_), channel_id=1, source_target_pairs={{0,2},{2,0},{1,3},{3,1},{4,6},{6,4},{5,7},{7,5},{8,10},{10,8},{9,1... | collective-permute-start | bytes 786440 | tf_op jit(solution)/shard_map/ppermute | solution.py:245
  9.8 1.9 %collective-permute-done.5.refs_0_ = bf16[2,2,112,128]{3,2,1,0:T(8,128)(2,1)S(1)} collective-permute-done((bf16[2,2,112,128]{3,2,1,0:T(8,128)(2,1)S(1)}, bf16[2,2,112,128]{3,2,1,0:T(8,128)(2,1)S(1)}, u32[]{:S(2)}, u32[]{:S(2)}) %collective-permute-start.5) | collective-permute-done | bytes 114720 | tf_op jit(solution)/shard_map/ppermute | solution.py:245
  11.7 1.7 %collective-permute-done.2.refs_0_ = bf16[2,400,128]{2,1,0:T(8,128)(2,1)S(1)} collective-permute-done((bf16[2,400,128]{2,1,0:T(8,128)(2,1)S(1)}, bf16[2,400,128]{2,1,0:T(8,128)(2,1)S(1)}, u32[]{:S(2)}, u32[]{:S(2)}) %collective-permute-start.2) | collective-permute-done | bytes 204832 | tf_op jit(solution)/shard_map/ppermute | solution.py:245
  13.3 0.1 pack.1.refs_0_
  13.4 2.3 %collective-permute-start.3 = (bf16[2,2,2,32,128]{4,3,2,1,0:T(8,128)(2,1)S(1)}, bf16[2,2,2,32,128]{4,3,2,1,0:T(8,128)(2,1)S(1)}, u32[]{:S(2)}, u32[]{:S(2)}) collective-permute-start(bf16[2,2,2,32,128]{4,3,2,1,0:T(8,128)(2,1)S(1)} %pack.1.refs_0_), channel_id=1, source_target_pairs={{0,8},{4,12},{8,0},{12,4},{1,9},{5,13},{9,1},{13,5},{2,10},{6,14},... | collective-permute-start | bytes 196616 | tf_op jit(solution)/shard_map/ppermute | solution.py:245
  15.7 0.7 %collective-permute-done.6.refs_2_ = bf16[2,2,112,128]{3,2,1,0:T(8,128)(2,1)S(1)} collective-permute-done((bf16[2,2,112,128]{3,2,1,0:T(8,128)(2,1)S(1)}, bf16[2,2,112,128]{3,2,1,0:T(8,128)(2,1)S(1)}, u32[]{:S(2)}, u32[]{:S(2)}) %collective-permute-start.6) | collective-permute-done | bytes 114720 | tf_op jit(solution)/shard_map/ppermute | solution.py:245
  16.4 0.4 %homed.1 = (bf16[2,112,128]{2,1,0:T(8,128)(2,1)S(1)}, bf16[2,112,128]{2,1,0:T(8,128)(2,1)S(1)}) custom-call(bf16[2,2,112,128]{3,2,1,0:T(8,128)(2,1)S(1)} %get-tuple-element.25._.own, bf16[2,112,128]{2,1,0:T(8,128)(2,1)S(1)} %get-tuple-element.36.query, bf16[2,400,128]{2,1,0:T(8,128)(2,1)S(1)} %get-tuple-element.38.refs_0_, ...), custom_call_target="tpu_custom_call" | custom-call | flops 1 | bytes 1 | tf_op jit(solution)/shard_map/homed/pallas_call | solution.py:267
  16.8 0.9 %collective-permute-start.7 = (bf16[2,112,128]{2,1,0:T(8,128)(2,1)S(1)}, bf16[2,112,128]{2,1,0:T(8,128)(2,1)S(1)}, u32[]{:S(2)}, u32[]{:S(2)}) collective-permute-start(bf16[2,112,128]{2,1,0:T(8,128)(2,1)S(1)} %get-tuple-element.42), channel_id=1, source_target_pairs={{0,4},{4,0},{8,12},{12,8},{1,5},{5,1},{9,13},{13,9},{2,6},{6,2},{1... | collective-permute-start | bytes 172040 | tf_op jit(solution)/shard_map/ppermute | solution.py:245
  17.7 0.0 collective-permute-done.refs_0_
  17.8 0.0 collective-permute-start.1
  17.8 0.0 collective-permute-done.4.refs_1_
  17.8 1.0 %first.1 = (f32[2,256,1]{2,1,0:T(8,128)S(1)}, f32[2,256,1]{2,1,0:T(8,128)S(1)}, f32[2,256,128]{2,1,0:T(8,128)S(1)}) custom-call(bf16[2,256,128]{2,1,0:T(8,128)(2,1)S(1)} %get-tuple-element.26.q_ref, bf16[2,2,256,128]{3,2,1,0:T(8,128)(2,1)S(1)} %get-tuple-element.27.refs_0_, bf16[2,2,256,128]{3,2,1,0:T(8,128)(2,1)S(1)} %collective-permute-done.4.refs_1_, ...), custom_call_target="tpu_custom_call" | custom-call | flops 1 | bytes 1 | tf_op jit(solution)/shard_map/first/pallas_call | solution.py:279
  18.8 0.0 collective-permute-done.3.refs_0_
  18.8 0.4 %free.1.refs_2_ = bf16[2,32,128]{2,1,0:T(8,128)(2,1)S(1)} custom-call(bf16[2,32,128]{2,1,0:T(8,128)(2,1)S(1)} %get-tuple-element.43.query, bf16[2,2,2,32,128]{4,3,2,1,0:T(8,128)(2,1)S(1)} %pack.1.refs_0_, bf16[2,2,2,32,128]{4,3,2,1,0:T(8,128)(2,1)S(1)} %get-tuple-element.44.refs_1_), custom_call_target="tpu_custom_call" | custom-call | flops 1 | bytes 1 | tf_op jit(solution)/shard_map/free/pallas_call | solution.py:292
  19.2 0.1 collective-permute-done.1.refs_0_
  19.3 0.9 %last.1.spatial = bf16[2,256,128]{2,1,0:T(8,128)(2,1)S(1)} custom-call(bf16[2,256,128]{2,1,0:T(8,128)(2,1)S(1)} %get-tuple-element.26.q_ref, bf16[2,2,256,128]{3,2,1,0:T(8,128)(2,1)S(1)} %collective-permute-done.1.refs_0_, f32[2,256,1]{2,1,0:T(8,128)S(1)} %get-tuple-element.33.refs_1_, f32[2,256,1]{2,1,0:T(8,128)S(1)} %get-tuple-element.34.refs_2_, ...), custom_call_target="tpu_custom_call" | custom-call | flops 1 | bytes 1 | tf_op jit(solution)/shard_map/last/pallas_call | solution.py:300
  20.2 0.9 %collective-permute-done.7.refs_1_ = bf16[2,112,128]{2,1,0:T(8,128)(2,1)S(1)} collective-permute-done((bf16[2,112,128]{2,1,0:T(8,128)(2,1)S(1)}, bf16[2,112,128]{2,1,0:T(8,128)(2,1)S(1)}, u32[]{:S(2)}, u32[]{:S(2)}) %collective-permute-start.7) | collective-permute-done | bytes 57376 | tf_op jit(solution)/shard_map/ppermute | solution.py:245
  21.1 0.7 %join.1 = bf16[2,256,256]{2,1,0:T(8,128)(2,1)} custom-call(bf16[2,256,128]{2,1,0:T(8,128)(2,1)S(1)} %last.1.spatial, bf16[2,112,128]{2,1,0:T(8,128)(2,1)S(1)} %get-tuple-element.41.refs_0_, bf16[2,112,128]{2,1,0:T(8,128)(2,1)S(1)} %collective-permute-done.7.refs_1_, bf16[2,32,128]{2,1,0:T(8,128)(2,1)S(1)} %free.1.refs_2_), custom_call_target="tpu_custom_call" | custom-call | flops 1 | bytes 1 | tf_op jit(solution)/shard_map/join/pallas_call | solution.py:308
  (4 shorter events, 0.0 us)
Async XLA Ops:
  1.1 10.5 %collective-permute-start.5 = (bf16[2,2,112,128]{3,2,1,0:T(8,128)(2,1)S(1)}, bf16[2,2,112,128]{3,2,1,0:T(8,128)(2,1)S(1)}, u32[]{:S(2)}, u32[]{:S(2)}) collective-permute-start(bf16[2,2,112,128]{3,2,1,0:T(8,128)(2,1)S(1)} %get-tuple-element.25._.own), channel_id=1, source_target_pairs={{0,8},{4,12},{8,0},{12,4},{1,9},{5,13},{9,1},{13,5},{2,10},{6,14},... | collective-permute-start | bytes 344072 | tf_op jit(solution)/shard_map/ppermute | solution.py:245
  5.2 8.1 %collective-permute-start.2 = (bf16[2,400,128]{2,1,0:T(8,128)(2,1)S(1)}, bf16[2,400,128]{2,1,0:T(8,128)(2,1)S(1)}, u32[]{:S(2)}, u32[]{:S(2)}) collective-permute-start(bf16[2,400,128]{2,1,0:T(8,128)(2,1)S(1)} %get-tuple-element.29), channel_id=1, source_target_pairs={{0,4},{4,0},{8,12},{12,8},{1,5},{5,1},{9,13},{13,9},{2,6},{6,2},{1... | collective-permute-start | bytes 614408 | tf_op jit(solution)/shard_map/ppermute | solution.py:245
  6.8 9.6 %collective-permute-start.6 = (bf16[2,2,112,128]{3,2,1,0:T(8,128)(2,1)S(1)}, bf16[2,2,112,128]{3,2,1,0:T(8,128)(2,1)S(1)}, u32[]{:S(2)}, u32[]{:S(2)}) collective-permute-start(bf16[2,2,112,128]{3,2,1,0:T(8,128)(2,1)S(1)} %get-tuple-element.37), channel_id=1, source_target_pairs={{0,12},{4,8},{8,4},{12,0},{1,13},{5,9},{9,5},{13,1},{2,14},{6,10},... | collective-permute-start | bytes 344072 | tf_op jit(solution)/shard_map/ppermute | solution.py:245
  7.9 9.9 %collective-permute-start.4 = (bf16[2,2,256,128]{3,2,1,0:T(8,128)(2,1)S(1)}, bf16[2,2,256,128]{3,2,1,0:T(8,128)(2,1)S(1)}, u32[]{:S(2)}, u32[]{:S(2)}) collective-permute-start(bf16[2,2,256,128]{3,2,1,0:T(8,128)(2,1)S(1)} %get-tuple-element.27.refs_0_), channel_id=1, source_target_pairs={{0,1},{1,0},{2,3},{3,2},{4,5},{5,4},{6,7},{7,6},{8,9},{9,8},{10,11... | collective-permute-start | bytes 786440 | tf_op jit(solution)/shard_map/ppermute | solution.py:245
  8.0 9.8 %collective-permute-start = (bf16[2,2,256,128]{3,2,1,0:T(8,128)(2,1)S(1)}, bf16[2,2,256,128]{3,2,1,0:T(8,128)(2,1)S(1)}, u32[]{:S(2)}, u32[]{:S(2)}) collective-permute-start(bf16[2,2,256,128]{3,2,1,0:T(8,128)(2,1)S(1)} %get-tuple-element.27.refs_0_), channel_id=1, source_target_pairs={{0,2},{2,0},{1,3},{3,1},{4,6},{6,4},{5,7},{7,5},{8,10},{10,8},{9,1... | collective-permute-start | bytes 786440 | tf_op jit(solution)/shard_map/ppermute | solution.py:245
  13.4 5.4 %collective-permute-start.3 = (bf16[2,2,2,32,128]{4,3,2,1,0:T(8,128)(2,1)S(1)}, bf16[2,2,2,32,128]{4,3,2,1,0:T(8,128)(2,1)S(1)}, u32[]{:S(2)}, u32[]{:S(2)}) collective-permute-start(bf16[2,2,2,32,128]{4,3,2,1,0:T(8,128)(2,1)S(1)} %pack.1.refs_0_), channel_id=1, source_target_pairs={{0,8},{4,12},{8,0},{12,4},{1,9},{5,13},{9,1},{13,5},{2,10},{6,14},... | collective-permute-start | bytes 196616 | tf_op jit(solution)/shard_map/ppermute | solution.py:245
  16.8 4.2 %collective-permute-start.7 = (bf16[2,112,128]{2,1,0:T(8,128)(2,1)S(1)}, bf16[2,112,128]{2,1,0:T(8,128)(2,1)S(1)}, u32[]{:S(2)}, u32[]{:S(2)}) collective-permute-start(bf16[2,112,128]{2,1,0:T(8,128)(2,1)S(1)} %get-tuple-element.42), channel_id=1, source_target_pairs={{0,4},{4,0},{8,12},{12,8},{1,5},{5,1},{9,13},{13,9},{2,6},{6,2},{1... | collective-permute-start | bytes 172040 | tf_op jit(solution)/shard_map/ppermute | solution.py:245
  17.8 1.5 %collective-permute-start.1 = (bf16[2,2,256,128]{3,2,1,0:T(8,128)(2,1)S(1)}, bf16[2,2,256,128]{3,2,1,0:T(8,128)(2,1)S(1)}, u32[]{:S(2)}, u32[]{:S(2)}) collective-permute-start(bf16[2,2,256,128]{3,2,1,0:T(8,128)(2,1)S(1)} %hold.4.refs_2_), channel_id=1, source_target_pairs={{0,1},{1,0},{2,3},{3,2},{4,5},{5,4},{6,7},{7,6},{8,9},{9,8},{10,11... | collective-permute-start | bytes 786440 | tf_op jit(solution)/shard_map/ppermute | solution.py:245

commit v8 on v7

--- a/solution.py
+++ b/solution.py
@@ -158,16 +158,22 @@
         o_ref[frame] = ((acc_ref[frame] * factor + mix(expo, value)) / total).astype(jnp.bfloat16)
 
 
-def join_kernel(team, free, spatial, *refs):
+def ready_kernel(team, free, spatial, *refs):
     pieces, out_hbm, sems = refs[:-2], refs[-2], refs[-1]
-    head_width = spatial.shape[2]
+    head_width, homed = spatial.shape[2], pieces[0].shape[1]
+    starts = [first_row(lax.axis_index("frame") % team, homed, free), homed]
     copies = [(spatial, out_hbm.at[:, :, :head_width])]
+    for start, piece in zip(starts, pieces):
+        copies.append((piece, out_hbm.at[:, pl.ds(start, piece.shape[1]), head_width:]))
+    run_copies(copies, sems)
+
+
+def join_kernel(team, free, head_width, *refs):
+    pieces, out_hbm, sems = refs[:-3], refs[-2], refs[-1]
+    copies = []
     for number, piece in enumerate(pieces):
         rows = piece.shape[1]
-        if number < team:
-            start = first_row((lax.axis_index("frame") + number) % team, rows, free)
-        else:
-            start = pieces[0].shape[1]
+        start = first_row((lax.axis_index("frame") + 1 + number) % team, rows, free)
         copies.append((piece, out_hbm.at[:, pl.ds(start, rows), head_width:]))
     run_copies(copies, sems)
 
@@ -286,7 +292,7 @@
     if free:
         held = hold([*spread, *running], 4000)
         spread, running = held[: len(spread)], held[len(spread) :]
-    pieces = [strip_out[0], *returned]
+    pieces = [strip_out[0]]
     if free:
         pieces.append(
             call(
@@ -305,14 +311,23 @@
         out_specs=vmem,
     )(query_spatial, *late, *running)
 
-    return call(
-        functools.partial(join_kernel, team, free),
-        "join",
+    out = call(
+        functools.partial(ready_kernel, team, free),
+        "ready",
         out_shape=jax.ShapeDtypeStruct(queries.shape, dtype),
         in_specs=[vmem] * (1 + len(pieces)),
         out_specs=hbm,
         scratch_shapes=[pltpu.SemaphoreType.DMA((1 + len(pieces),))],
     )(spatial, *pieces)
+    return call(
+        functools.partial(join_kernel, team, free, head_width),
+        "join",
+        out_shape=jax.ShapeDtypeStruct(queries.shape, dtype),
+        in_specs=[vmem] * len(returned) + [hbm],
+        out_specs=hbm,
+        scratch_shapes=[pltpu.SemaphoreType.DMA((max(1, len(returned)),))],
+        input_output_aliases={len(returned): 0},
+    )(*returned, out)
 
 
 def solution(mesh):

time: 22 us -> 21.9 us (level)
  waiting for transfers between devices: 5.36 us -> 4.65 us
  Pallas kernels: 5.69 us -> 6.3 us
    ppermute x8, waiting for transfers between devices: 5.36 us -> 4.65 us  [exchange(): lax.ppermute(array, axis, [(i, partner_of(i, step, size)) for i in range(...]
    pallas_call x1 -> x2, Pallas kernels: 0.72 us -> 1.33 us  [the longest x1 0.7 us: body(): call(functools.partial(ready_kernel, team, free), 'ready', out_shape=jax....]
  transfers between devices with their start and end apart: 8 -> 8, of which waited for: 5 -> 5; matrix products, arithmetic and copies ran while one was open for 0% -> 0% of each run, Pallas kernels for 18% -> 21%
where the time goes in v8:
time: 21.9 us; the launch traced here: 21.7 us
  starting transfers between devices  10.7 us (49%)
  Pallas kernels  6.3 us (29%)
  waiting for transfers between devices  4.65 us (21%)
    ppermute x8, starting transfers between devices, exchange(): lax.ppermute(array, axis, [(i, partner_of(i, step, size)) for i in range(...  10.7 us
    ppermute x8, waiting for transfers between devices, exchange(): lax.ppermute(array, axis, [(i, partner_of(i, step, size)) for i in range(...  4.65 us
    pallas_call x1, Pallas kernels, body(): call(functools.partial(strips_kernel, team, free, head_width), 'strips',...  1.11 us
    pallas_call x1, Pallas kernels, body(): call(functools.partial(rest_kernel, team, free), 'rest', out_shape=[in_vm...  1.1 us
    pallas_call x1, Pallas kernels, body(): call(functools.partial(first_kernel, score_scale, len(early)), 'first', o...  1.03 us
    pallas_call x1, Pallas kernels, body(): call(functools.partial(last_kernel, score_scale, len(late)), 'last', out_...  0.87 us
    pallas_call x1, Pallas kernels, body(): call(functools.partial(ready_kernel, team, free), 'ready', out_shape=jax....  0.7 us
    pallas_call x1, Pallas kernels, body(): call(functools.partial(join_kernel, team, free, head_width), 'join', out_...  0.63 us
  transfers between devices with their start and end apart: 8, of which 5 were waited for; matrix products, arithmetic and copies ran while one was open for 0% of the time, Pallas kernels for 21%

profile of v8, /device:TPU:0, one launch (start us, length us, event | category | flops | bytes accessed | tf_op | source)
XLA Modules:
  0.0 21.7 jit_solution(16919875843672467234)
XLA Ops:
  0.0 1.1 %strips.1 = (bf16[2,2,112,128]{3,2,1,0:T(8,128)(2,1)S(1)}, bf16[2,2,112,128]{3,2,1,0:T(8,128)(2,1)S(1)}, bf16[2,400,128]{2,1,0:T(8,128)(2,1)S(1)}) custom-call(bf16[2,256,256]{2,1,0:T(8,128)(2,1)} %q_hbm.3, bf16[2,256,256]{2,1,0:T(8,128)(2,1)} %k_hbm.3, bf16[2,256,256]{2,1,0:T(8,128)(2,1)} %v_hbm.3), custom_call_target="tpu_custom_call" | custom-call | flops 1 | bytes 1 | tf_op jit(solution)/shard_map/strips/pallas_call | solution.py:216
  1.1 4.1 %collective-permute-start.1 = (bf16[2,2,112,128]{3,2,1,0:T(8,128)(2,1)S(1)}, bf16[2,2,112,128]{3,2,1,0:T(8,128)(2,1)S(1)}, u32[]{:S(2)}, u32[]{:S(2)}) collective-permute-start(bf16[2,2,112,128]{3,2,1,0:T(8,128)(2,1)S(1)} %get-tuple-element.25._.own), channel_id=1, source_target_pairs={{0,8},{4,12},{8,0},{12,4},{1,9},{5,13},{9,1},{13,5},{2,10},{6,14},... | collective-permute-start | bytes 344072 | tf_op jit(solution)/shard_map/ppermute | solution.py:251
  5.2 1.6 %collective-permute-start = (bf16[2,400,128]{2,1,0:T(8,128)(2,1)S(1)}, bf16[2,400,128]{2,1,0:T(8,128)(2,1)S(1)}, u32[]{:S(2)}, u32[]{:S(2)}) collective-permute-start(bf16[2,400,128]{2,1,0:T(8,128)(2,1)S(1)} %get-tuple-element.27), channel_id=1, source_target_pairs={{0,4},{4,0},{8,12},{12,8},{1,5},{5,1},{9,13},{13,9},{2,6},{6,2},{1... | collective-permute-start | bytes 614408 | tf_op jit(solution)/shard_map/ppermute | solution.py:251
  6.8 0.0 collective-permute-start.2
  6.8 1.1 %rest.1 = (bf16[2,112,128]{2,1,0:T(8,128)(2,1)S(1)}, bf16[2,2,256,128]{3,2,1,0:T(8,128)(2,1)S(1)}, bf16[2,256,128]{2,1,0:T(8,128)(2,1)S(1)}, bf16[2,2,32,128]{3,2,1,0:T(8,128)(2,1)S(1)}, bf16[2,32,128]{2,1,0:T(8,128)(2,1)S(1)}) custom-call(bf16[2,256,256]{2,1,0:T(8,128)(2,1)} %q_hbm.3, bf16[2,256,256]{2,1,0:T(8,128)(2,1)} %k_hbm.3, ...), custom_call_target="tpu_custom_call" | custom-call | flops 1 | bytes 1 | tf_op jit(solution)/shard_map/rest/pallas_call | solution.py:227
  7.9 0.1 collective-permute-start.7
  8.0 1.8 %collective-permute-start.4 = (bf16[2,2,256,128]{3,2,1,0:T(8,128)(2,1)S(1)}, bf16[2,2,256,128]{3,2,1,0:T(8,128)(2,1)S(1)}, u32[]{:S(2)}, u32[]{:S(2)}) collective-permute-start(bf16[2,2,256,128]{3,2,1,0:T(8,128)(2,1)S(1)} %get-tuple-element.34.refs_0_), channel_id=1, source_target_pairs={{0,2},{2,0},{1,3},{3,1},{4,6},{6,4},{5,7},{7,5},{8,10},{10,8},{9,1... | collective-permute-start | bytes 786440 | tf_op jit(solution)/shard_map/ppermute | solution.py:251
  9.8 1.9 %collective-permute-done.1.refs_0_ = bf16[2,2,112,128]{3,2,1,0:T(8,128)(2,1)S(1)} collective-permute-done((bf16[2,2,112,128]{3,2,1,0:T(8,128)(2,1)S(1)}, bf16[2,2,112,128]{3,2,1,0:T(8,128)(2,1)S(1)}, u32[]{:S(2)}, u32[]{:S(2)}) %collective-permute-start.1) | collective-permute-done | bytes 114720 | tf_op jit(solution)/shard_map/ppermute | solution.py:251
  11.7 1.7 %collective-permute-done.refs_0_ = bf16[2,400,128]{2,1,0:T(8,128)(2,1)S(1)} collective-permute-done((bf16[2,400,128]{2,1,0:T(8,128)(2,1)S(1)}, bf16[2,400,128]{2,1,0:T(8,128)(2,1)S(1)}, u32[]{:S(2)}, u32[]{:S(2)}) %collective-permute-start) | collective-permute-done | bytes 204832 | tf_op jit(solution)/shard_map/ppermute | solution.py:251
  13.3 0.1 pack.1.refs_0_
  13.4 2.3 %collective-permute-start.6 = (bf16[2,2,2,32,128]{4,3,2,1,0:T(8,128)(2,1)S(1)}, bf16[2,2,2,32,128]{4,3,2,1,0:T(8,128)(2,1)S(1)}, u32[]{:S(2)}, u32[]{:S(2)}) collective-permute-start(bf16[2,2,2,32,128]{4,3,2,1,0:T(8,128)(2,1)S(1)} %pack.1.refs_0_), channel_id=1, source_target_pairs={{0,8},{4,12},{8,0},{12,4},{1,9},{5,13},{9,1},{13,5},{2,10},{6,14},... | collective-permute-start | bytes 196616 | tf_op jit(solution)/shard_map/ppermute | solution.py:251
  15.7 0.7 %collective-permute-done.2.refs_2_ = bf16[2,2,112,128]{3,2,1,0:T(8,128)(2,1)S(1)} collective-permute-done((bf16[2,2,112,128]{3,2,1,0:T(8,128)(2,1)S(1)}, bf16[2,2,112,128]{3,2,1,0:T(8,128)(2,1)S(1)}, u32[]{:S(2)}, u32[]{:S(2)}) %collective-permute-start.2) | collective-permute-done | bytes 114720 | tf_op jit(solution)/shard_map/ppermute | solution.py:251
  16.4 0.4 %homed.1 = (bf16[2,112,128]{2,1,0:T(8,128)(2,1)S(1)}, bf16[2,112,128]{2,1,0:T(8,128)(2,1)S(1)}) custom-call(bf16[2,2,112,128]{3,2,1,0:T(8,128)(2,1)S(1)} %get-tuple-element.25._.own, bf16[2,112,128]{2,1,0:T(8,128)(2,1)S(1)} %get-tuple-element.26.query, bf16[2,400,128]{2,1,0:T(8,128)(2,1)S(1)} %get-tuple-element.29.refs_0_, ...), custom_call_target="tpu_custom_call" | custom-call | flops 1 | bytes 1 | tf_op jit(solution)/shard_map/homed/pallas_call | solution.py:273
  16.8 0.9 %collective-permute-start.3 = (bf16[2,112,128]{2,1,0:T(8,128)(2,1)S(1)}, bf16[2,112,128]{2,1,0:T(8,128)(2,1)S(1)}, u32[]{:S(2)}, u32[]{:S(2)}) collective-permute-start(bf16[2,112,128]{2,1,0:T(8,128)(2,1)S(1)} %get-tuple-element.32), channel_id=1, source_target_pairs={{0,4},{4,0},{8,12},{12,8},{1,5},{5,1},{9,13},{13,9},{2,6},{6,2},{1... | collective-permute-start | bytes 172040 | tf_op jit(solution)/shard_map/ppermute | solution.py:251
  17.8 0.0 collective-permute-done.4.refs_0_
  17.8 0.0 collective-permute-start.5
  17.8 0.0 collective-permute-done.7.refs_1_
  17.8 1.0 %first.1 = (f32[2,256,1]{2,1,0:T(8,128)S(1)}, f32[2,256,1]{2,1,0:T(8,128)S(1)}, f32[2,256,128]{2,1,0:T(8,128)S(1)}) custom-call(bf16[2,256,128]{2,1,0:T(8,128)(2,1)S(1)} %get-tuple-element.33.q_ref, bf16[2,2,256,128]{3,2,1,0:T(8,128)(2,1)S(1)} %get-tuple-element.34.refs_0_, bf16[2,2,256,128]{3,2,1,0:T(8,128)(2,1)S(1)} %collective-permute-done.7.refs_1_, ...), custom_call_target="tpu_custom_call" | custom-call | flops 1 | bytes 1 | tf_op jit(solution)/shard_map/first/pallas_call | solution.py:285
  18.8 0.0 collective-permute-done.6.refs_0_
  18.8 0.4 %free.1.refs_1_ = bf16[2,32,128]{2,1,0:T(8,128)(2,1)S(1)} custom-call(bf16[2,32,128]{2,1,0:T(8,128)(2,1)S(1)} %get-tuple-element.43.query, bf16[2,2,2,32,128]{4,3,2,1,0:T(8,128)(2,1)S(1)} %pack.1.refs_0_, bf16[2,2,2,32,128]{4,3,2,1,0:T(8,128)(2,1)S(1)} %get-tuple-element.44.refs_1_), custom_call_target="tpu_custom_call" | custom-call | flops 1 | bytes 1 | tf_op jit(solution)/shard_map/free/pallas_call | solution.py:298
  19.2 0.1 collective-permute-done.5.refs_0_
  19.3 0.9 %last.1.spatial = bf16[2,256,128]{2,1,0:T(8,128)(2,1)S(1)} custom-call(bf16[2,256,128]{2,1,0:T(8,128)(2,1)S(1)} %get-tuple-element.33.q_ref, bf16[2,2,256,128]{3,2,1,0:T(8,128)(2,1)S(1)} %collective-permute-done.5.refs_0_, f32[2,256,1]{2,1,0:T(8,128)S(1)} %get-tuple-element.39.refs_1_, f32[2,256,1]{2,1,0:T(8,128)S(1)} %get-tuple-element.40.refs_2_, ...), custom_call_target="tpu_custom_call" | custom-call | flops 1 | bytes 1 | tf_op jit(solution)/shard_map/last/pallas_call | solution.py:306
  20.2 0.7 %ready.1.refs_1_ = bf16[2,256,256]{2,1,0:T(8,128)(2,1)} custom-call(bf16[2,256,128]{2,1,0:T(8,128)(2,1)S(1)} %last.1.spatial, bf16[2,112,128]{2,1,0:T(8,128)(2,1)S(1)} %get-tuple-element.42.refs_0_, bf16[2,32,128]{2,1,0:T(8,128)(2,1)S(1)} %free.1.refs_1_), custom_call_target="tpu_custom_call" | custom-call | flops 1 | bytes 1 | tf_op jit(solution)/shard_map/ready/pallas_call | solution.py:314
  20.9 0.2 %collective-permute-done.3.refs_0_ = bf16[2,112,128]{2,1,0:T(8,128)(2,1)S(1)} collective-permute-done((bf16[2,112,128]{2,1,0:T(8,128)(2,1)S(1)}, bf16[2,112,128]{2,1,0:T(8,128)(2,1)S(1)}, u32[]{:S(2)}, u32[]{:S(2)}) %collective-permute-start.3) | collective-permute-done | bytes 57376 | tf_op jit(solution)/shard_map/ppermute | solution.py:251
  21.1 0.6 %join.1 = bf16[2,256,256]{2,1,0:T(8,128)(2,1)} custom-call(bf16[2,112,128]{2,1,0:T(8,128)(2,1)S(1)} %collective-permute-done.3.refs_0_, bf16[2,256,256]{2,1,0:T(8,128)(2,1)} %ready.1.refs_1_), custom_call_target="tpu_custom_call", output_to_operand_aliasing={{}: (1, {})} | custom-call | flops 1 | bytes 1 | tf_op jit(solution)/shard_map/join/pallas_call | solution.py:322
  (4 shorter events, 0.0 us)
Async XLA Ops:
  1.1 10.5 %collective-permute-start.1 = (bf16[2,2,112,128]{3,2,1,0:T(8,128)(2,1)S(1)}, bf16[2,2,112,128]{3,2,1,0:T(8,128)(2,1)S(1)}, u32[]{:S(2)}, u32[]{:S(2)}) collective-permute-start(bf16[2,2,112,128]{3,2,1,0:T(8,128)(2,1)S(1)} %get-tuple-element.25._.own), channel_id=1, source_target_pairs={{0,8},{4,12},{8,0},{12,4},{1,9},{5,13},{9,1},{13,5},{2,10},{6,14},... | collective-permute-start | bytes 344072 | tf_op jit(solution)/shard_map/ppermute | solution.py:251
  5.2 8.1 %collective-permute-start = (bf16[2,400,128]{2,1,0:T(8,128)(2,1)S(1)}, bf16[2,400,128]{2,1,0:T(8,128)(2,1)S(1)}, u32[]{:S(2)}, u32[]{:S(2)}) collective-permute-start(bf16[2,400,128]{2,1,0:T(8,128)(2,1)S(1)} %get-tuple-element.27), channel_id=1, source_target_pairs={{0,4},{4,0},{8,12},{12,8},{1,5},{5,1},{9,13},{13,9},{2,6},{6,2},{1... | collective-permute-start | bytes 614408 | tf_op jit(solution)/shard_map/ppermute | solution.py:251
  6.8 9.6 %collective-permute-start.2 = (bf16[2,2,112,128]{3,2,1,0:T(8,128)(2,1)S(1)}, bf16[2,2,112,128]{3,2,1,0:T(8,128)(2,1)S(1)}, u32[]{:S(2)}, u32[]{:S(2)}) collective-permute-start(bf16[2,2,112,128]{3,2,1,0:T(8,128)(2,1)S(1)} %get-tuple-element.28), channel_id=1, source_target_pairs={{0,12},{4,8},{8,4},{12,0},{1,13},{5,9},{9,5},{13,1},{2,14},{6,10},... | collective-permute-start | bytes 344072 | tf_op jit(solution)/shard_map/ppermute | solution.py:251
  7.9 9.9 %collective-permute-start.7 = (bf16[2,2,256,128]{3,2,1,0:T(8,128)(2,1)S(1)}, bf16[2,2,256,128]{3,2,1,0:T(8,128)(2,1)S(1)}, u32[]{:S(2)}, u32[]{:S(2)}) collective-permute-start(bf16[2,2,256,128]{3,2,1,0:T(8,128)(2,1)S(1)} %get-tuple-element.34.refs_0_), channel_id=1, source_target_pairs={{0,1},{1,0},{2,3},{3,2},{4,5},{5,4},{6,7},{7,6},{8,9},{9,8},{10,11... | collective-permute-start | bytes 786440 | tf_op jit(solution)/shard_map/ppermute | solution.py:251
  8.0 9.8 %collective-permute-start.4 = (bf16[2,2,256,128]{3,2,1,0:T(8,128)(2,1)S(1)}, bf16[2,2,256,128]{3,2,1,0:T(8,128)(2,1)S(1)}, u32[]{:S(2)}, u32[]{:S(2)}) collective-permute-start(bf16[2,2,256,128]{3,2,1,0:T(8,128)(2,1)S(1)} %get-tuple-element.34.refs_0_), channel_id=1, source_target_pairs={{0,2},{2,0},{1,3},{3,1},{4,6},{6,4},{5,7},{7,5},{8,10},{10,8},{9,1... | collective-permute-start | bytes 786440 | tf_op jit(solution)/shard_map/ppermute | solution.py:251
  13.4 5.4 %collective-permute-start.6 = (bf16[2,2,2,32,128]{4,3,2,1,0:T(8,128)(2,1)S(1)}, bf16[2,2,2,32,128]{4,3,2,1,0:T(8,128)(2,1)S(1)}, u32[]{:S(2)}, u32[]{:S(2)}) collective-permute-start(bf16[2,2,2,32,128]{4,3,2,1,0:T(8,128)(2,1)S(1)} %pack.1.refs_0_), channel_id=1, source_target_pairs={{0,8},{4,12},{8,0},{12,4},{1,9},{5,13},{9,1},{13,5},{2,10},{6,14},... | collective-permute-start | bytes 196616 | tf_op jit(solution)/shard_map/ppermute | solution.py:251
  16.8 4.2 %collective-permute-start.3 = (bf16[2,112,128]{2,1,0:T(8,128)(2,1)S(1)}, bf16[2,112,128]{2,1,0:T(8,128)(2,1)S(1)}, u32[]{:S(2)}, u32[]{:S(2)}) collective-permute-start(bf16[2,112,128]{2,1,0:T(8,128)(2,1)S(1)} %get-tuple-element.32), channel_id=1, source_target_pairs={{0,4},{4,0},{8,12},{12,8},{1,5},{5,1},{9,13},{13,9},{2,6},{6,2},{1... | collective-permute-start | bytes 172040 | tf_op jit(solution)/shard_map/ppermute | solution.py:251
  17.8 1.5 %collective-permute-start.5 = (bf16[2,2,256,128]{3,2,1,0:T(8,128)(2,1)S(1)}, bf16[2,2,256,128]{3,2,1,0:T(8,128)(2,1)S(1)}, u32[]{:S(2)}, u32[]{:S(2)}) collective-permute-start(bf16[2,2,256,128]{3,2,1,0:T(8,128)(2,1)S(1)} %hold.6.refs_2_), channel_id=1, source_target_pairs={{0,1},{1,0},{2,3},{3,2},{4,5},{5,4},{6,7},{7,6},{8,9},{9,8},{10,11... | collective-permute-start | bytes 786440 | tf_op jit(solution)/shard_map/ppermute | solution.py:251

commit v9 on v6

--- a/solution.py
+++ b/solution.py
@@ -126,12 +126,6 @@
     run_copies(copies, sems)
 
 
-def free_kernel(team, score_scale, query, *refs):
-    packs, out = refs[:-1], refs[-1]
-    keys, values = ([p.at[m, n] for p in packs for m in range(team)] for n in range(2))
-    attend_strips([query], keys, values, [out], score_scale)
-
-
 def first_kernel(score_scale, pieces, q_ref, *refs):
     kvs, (top_ref, total_ref, acc_ref) = refs[:pieces], refs[pieces:]
     for frame in range(q_ref.shape[0]):
@@ -146,20 +140,12 @@
 
 
 def last_kernel(score_scale, pieces, team, q_ref, *refs):
-    kvs, (top_ref, total_ref, acc_ref), refs = refs[:pieces], refs[pieces : pieces + 3], refs[pieces + 3 :]
-    ready, (out_hbm, o_ref, sems) = refs[:-3], refs[-3:]
-    frames, _, head_width = q_ref.shape
-    homed, free = ready[0].shape[1], sum(ref.shape[1] for ref in ready[1:])
-    starts = [first_row(lax.axis_index("frame") % team, homed, free), homed]
-    copies = []
-
-    def send(src, dst):
-        copies.append(pltpu.make_async_copy(src, dst, sems.at[len(copies)]))
-        copies[-1].start()
-
-    for start, ref in zip(starts, ready):
-        send(ref, out_hbm.at[:, pl.ds(start, ref.shape[1]), head_width:])
-    for frame in range(frames):
+    kvs, (top_ref, total_ref, acc_ref, own), refs = refs[:pieces], refs[pieces : pieces + 4], refs[pieces + 4 :]
+    (query, *packs), (out_hbm, o_ref, free_ref, sems) = refs[:-4], refs[-4:]
+    head_width, homed, free = q_ref.shape[2], own.shape[1], query.shape[1]
+    keys, values = ([p.at[m, n] for p in packs for m in range(team)] for n in range(2))
+    attend_strips([query], keys, values, [free_ref], score_scale)
+    for frame in range(q_ref.shape[0]):
         key = jnp.concatenate([kv[0, frame] for kv in kvs])
         value = jnp.concatenate([kv[1, frame] for kv in kvs])
         scores = score(q_ref[frame], key, score_scale)
@@ -168,9 +154,13 @@
         factor = jnp.exp(top_ref[frame] - highest)
         total = total_ref[frame] * factor + jnp.sum(expo, axis=-1, keepdims=True)
         o_ref[frame] = ((acc_ref[frame] * factor + mix(expo, value)) / total).astype(jnp.bfloat16)
-        send(o_ref.at[frame], out_hbm.at[frame, :, :head_width])
-    for copy in copies:
-        copy.wait()
+    start = first_row(lax.axis_index("frame") % team, homed, free)
+    copies = [
+        (o_ref, out_hbm.at[:, :, :head_width]),
+        (own, out_hbm.at[:, pl.ds(start, homed), head_width:]),
+        (free_ref, out_hbm.at[:, homed : homed + free, head_width:]),
+    ]
+    run_copies(copies, sems)
 
 
 def join_kernel(team, free, head_width, *refs):
@@ -297,28 +287,18 @@
     if free:
         held = hold([*spread, *running], 4000)
         spread, running = held[: len(spread)], held[len(spread) :]
-    ready = [strip_out[0]]
-    if free:
-        ready.append(
-            call(
-                functools.partial(free_kernel, team, score_scale),
-                "free",
-                out_shape=in_vmem(*spare),
-                in_specs=[vmem] * (2 + len(spread)),
-                out_specs=vmem,
-            )(spares[1], packed, *spread)
-        )
     out = call(
         functools.partial(last_kernel, score_scale, len(late), team),
         "last",
         out_shape=jax.ShapeDtypeStruct(queries.shape, dtype),
-        in_specs=[vmem] * (4 + len(late) + len(ready)),
+        in_specs=[vmem] * (7 + len(late) + len(spread)),
         out_specs=hbm,
         scratch_shapes=[
             pltpu.VMEM(whole, dtype),
-            pltpu.SemaphoreType.DMA((frames_dev + len(ready),)),
+            pltpu.VMEM(spare, dtype),
+            pltpu.SemaphoreType.DMA((3,)),
         ],
-    )(query_spatial, *late, *running, *ready)
+    )(query_spatial, *late, *running, strip_out[0], spares[1], packed, *spread)
 
     return call(
         functools.partial(join_kernel, team, free, head_width),

time: 21.9 us -> 21.9 us (level)
  Pallas kernels: 6.28 us -> 5.97 us
  waiting for transfers between devices: 4.68 us -> 4.99 us
    pallas_call x1 -> x0, Pallas kernels: 0.36 us -> none  [body(): call(functools.partial(free_kernel, team, score_scale), 'free', out_shape...]
    ppermute x8, waiting for transfers between devices: 4.68 us -> 4.99 us  [exchange(): lax.ppermute(array, axis, [(i, partner_of(i, step, size)) for i in range(...]
  transfers between devices with their start and end apart: 8 -> 8, of which waited for: 5 -> 5; matrix products, arithmetic and copies ran while one was open for 0% -> 0% of each run, Pallas kernels for 21% -> 20%
where the time goes in v9:
time: 21.9 us; the launch traced here: 21.7 us
  starting transfers between devices  10.7 us (49%)
  Pallas kernels  5.97 us (27%)
  waiting for transfers between devices  4.99 us (23%)
    ppermute x8, starting transfers between devices, exchange(): lax.ppermute(array, axis, [(i, partner_of(i, step, size)) for i in range(...  10.7 us
    ppermute x8, waiting for transfers between devices, exchange(): lax.ppermute(array, axis, [(i, partner_of(i, step, size)) for i in range(...  4.99 us
    pallas_call x1, Pallas kernels, body(): call(functools.partial(last_kernel, score_scale, len(late), team), 'last'...  1.6 us
    pallas_call x1, Pallas kernels, body(): call(functools.partial(strips_kernel, team, free, head_width), 'strips',...  1.11 us
    pallas_call x1, Pallas kernels, body(): call(functools.partial(rest_kernel, team, free), 'rest', out_shape=[in_vm...  1.1 us
    pallas_call x1, Pallas kernels, body(): call(functools.partial(first_kernel, score_scale, len(early)), 'first', o...  1.03 us
    pallas_call x1, Pallas kernels, body(): call(functools.partial(join_kernel, team, free, head_width), 'join', out_...  0.63 us
  transfers between devices with their start and end apart: 8, of which 5 were waited for; matrix products, arithmetic and copies ran while one was open for 0% of the time, Pallas kernels for 20%

profile of v9, /device:TPU:0, one launch (start us, length us, event | category | flops | bytes accessed | tf_op | source)
XLA Modules:
  0.0 21.7 jit_solution(17701634476826178305)
XLA Ops:
  0.0 1.1 %strips.1 = (bf16[2,2,112,128]{3,2,1,0:T(8,128)(2,1)S(1)}, bf16[2,2,112,128]{3,2,1,0:T(8,128)(2,1)S(1)}, bf16[2,400,128]{2,1,0:T(8,128)(2,1)S(1)}) custom-call(bf16[2,256,256]{2,1,0:T(8,128)(2,1)} %q_hbm.3, bf16[2,256,256]{2,1,0:T(8,128)(2,1)} %k_hbm.3, bf16[2,256,256]{2,1,0:T(8,128)(2,1)} %v_hbm.3), custom_call_target="tpu_custom_call" | custom-call | flops 1 | bytes 1 | tf_op jit(solution)/shard_map/strips/pallas_call | solution.py:211
  1.1 4.1 %collective-permute-start.1 = (bf16[2,2,112,128]{3,2,1,0:T(8,128)(2,1)S(1)}, bf16[2,2,112,128]{3,2,1,0:T(8,128)(2,1)S(1)}, u32[]{:S(2)}, u32[]{:S(2)}) collective-permute-start(bf16[2,2,112,128]{3,2,1,0:T(8,128)(2,1)S(1)} %get-tuple-element.25._.own), channel_id=1, source_target_pairs={{0,8},{4,12},{8,0},{12,4},{1,9},{5,13},{9,1},{13,5},{2,10},{6,14},... | collective-permute-start | bytes 344072 | tf_op jit(solution)/shard_map/ppermute | solution.py:246
  5.2 1.6 %collective-permute-start = (bf16[2,400,128]{2,1,0:T(8,128)(2,1)S(1)}, bf16[2,400,128]{2,1,0:T(8,128)(2,1)S(1)}, u32[]{:S(2)}, u32[]{:S(2)}) collective-permute-start(bf16[2,400,128]{2,1,0:T(8,128)(2,1)S(1)} %get-tuple-element.27), channel_id=1, source_target_pairs={{0,4},{4,0},{8,12},{12,8},{1,5},{5,1},{9,13},{13,9},{2,6},{6,2},{1... | collective-permute-start | bytes 614408 | tf_op jit(solution)/shard_map/ppermute | solution.py:246
  6.8 0.0 collective-permute-start.2
  6.8 1.1 %rest.1 = (bf16[2,112,128]{2,1,0:T(8,128)(2,1)S(1)}, bf16[2,2,256,128]{3,2,1,0:T(8,128)(2,1)S(1)}, bf16[2,256,128]{2,1,0:T(8,128)(2,1)S(1)}, bf16[2,2,32,128]{3,2,1,0:T(8,128)(2,1)S(1)}, bf16[2,32,128]{2,1,0:T(8,128)(2,1)S(1)}) custom-call(bf16[2,256,256]{2,1,0:T(8,128)(2,1)} %q_hbm.3, bf16[2,256,256]{2,1,0:T(8,128)(2,1)} %k_hbm.3, ...), custom_call_target="tpu_custom_call" | custom-call | flops 1 | bytes 1 | tf_op jit(solution)/shard_map/rest/pallas_call | solution.py:222
  7.9 0.1 collective-permute-start.7
  8.0 1.8 %collective-permute-start.4 = (bf16[2,2,256,128]{3,2,1,0:T(8,128)(2,1)S(1)}, bf16[2,2,256,128]{3,2,1,0:T(8,128)(2,1)S(1)}, u32[]{:S(2)}, u32[]{:S(2)}) collective-permute-start(bf16[2,2,256,128]{3,2,1,0:T(8,128)(2,1)S(1)} %get-tuple-element.34.refs_0_), channel_id=1, source_target_pairs={{0,2},{2,0},{1,3},{3,1},{4,6},{6,4},{5,7},{7,5},{8,10},{10,8},{9,1... | collective-permute-start | bytes 786440 | tf_op jit(solution)/shard_map/ppermute | solution.py:246
  9.8 1.9 %collective-permute-done.1.refs_0_ = bf16[2,2,112,128]{3,2,1,0:T(8,128)(2,1)S(1)} collective-permute-done((bf16[2,2,112,128]{3,2,1,0:T(8,128)(2,1)S(1)}, bf16[2,2,112,128]{3,2,1,0:T(8,128)(2,1)S(1)}, u32[]{:S(2)}, u32[]{:S(2)}) %collective-permute-start.1) | collective-permute-done | bytes 114720 | tf_op jit(solution)/shard_map/ppermute | solution.py:246
  11.7 1.7 %collective-permute-done.refs_0_ = bf16[2,400,128]{2,1,0:T(8,128)(2,1)S(1)} collective-permute-done((bf16[2,400,128]{2,1,0:T(8,128)(2,1)S(1)}, bf16[2,400,128]{2,1,0:T(8,128)(2,1)S(1)}, u32[]{:S(2)}, u32[]{:S(2)}) %collective-permute-start) | collective-permute-done | bytes 204832 | tf_op jit(solution)/shard_map/ppermute | solution.py:246
  13.3 0.1 pack.1.refs_6_
  13.4 2.3 %collective-permute-start.6 = (bf16[2,2,2,32,128]{4,3,2,1,0:T(8,128)(2,1)S(1)}, bf16[2,2,2,32,128]{4,3,2,1,0:T(8,128)(2,1)S(1)}, u32[]{:S(2)}, u32[]{:S(2)}) collective-permute-start(bf16[2,2,2,32,128]{4,3,2,1,0:T(8,128)(2,1)S(1)} %pack.1.refs_6_), channel_id=1, source_target_pairs={{0,8},{4,12},{8,0},{12,4},{1,9},{5,13},{9,1},{13,5},{2,10},{6,14},... | collective-permute-start | bytes 196616 | tf_op jit(solution)/shard_map/ppermute | solution.py:246
  15.7 0.7 %collective-permute-done.2.refs_2_ = bf16[2,2,112,128]{3,2,1,0:T(8,128)(2,1)S(1)} collective-permute-done((bf16[2,2,112,128]{3,2,1,0:T(8,128)(2,1)S(1)}, bf16[2,2,112,128]{3,2,1,0:T(8,128)(2,1)S(1)}, u32[]{:S(2)}, u32[]{:S(2)}) %collective-permute-start.2) | collective-permute-done | bytes 114720 | tf_op jit(solution)/shard_map/ppermute | solution.py:246
  16.4 0.4 %homed.1 = (bf16[2,112,128]{2,1,0:T(8,128)(2,1)S(1)}, bf16[2,112,128]{2,1,0:T(8,128)(2,1)S(1)}) custom-call(bf16[2,2,112,128]{3,2,1,0:T(8,128)(2,1)S(1)} %get-tuple-element.25._.own, bf16[2,112,128]{2,1,0:T(8,128)(2,1)S(1)} %get-tuple-element.26.query, bf16[2,400,128]{2,1,0:T(8,128)(2,1)S(1)} %get-tuple-element.29.refs_0_, ...), custom_call_target="tpu_custom_call" | custom-call | flops 1 | bytes 1 | tf_op jit(solution)/shard_map/homed/pallas_call | solution.py:268
  16.8 0.9 %collective-permute-start.3 = (bf16[2,112,128]{2,1,0:T(8,128)(2,1)S(1)}, bf16[2,112,128]{2,1,0:T(8,128)(2,1)S(1)}, u32[]{:S(2)}, u32[]{:S(2)}) collective-permute-start(bf16[2,112,128]{2,1,0:T(8,128)(2,1)S(1)} %get-tuple-element.32), channel_id=1, source_target_pairs={{0,4},{4,0},{8,12},{12,8},{1,5},{5,1},{9,13},{13,9},{2,6},{6,2},{1... | collective-permute-start | bytes 172040 | tf_op jit(solution)/shard_map/ppermute | solution.py:246
  17.8 0.0 collective-permute-done.4.refs_0_
  17.8 0.0 collective-permute-start.5
  17.8 0.0 collective-permute-done.7.refs_1_
  17.8 1.0 %first.1 = (f32[2,256,1]{2,1,0:T(8,128)S(1)}, f32[2,256,1]{2,1,0:T(8,128)S(1)}, f32[2,256,128]{2,1,0:T(8,128)S(1)}) custom-call(bf16[2,256,128]{2,1,0:T(8,128)(2,1)S(1)} %get-tuple-element.33.q_ref, bf16[2,2,256,128]{3,2,1,0:T(8,128)(2,1)S(1)} %get-tuple-element.34.refs_0_, bf16[2,2,256,128]{3,2,1,0:T(8,128)(2,1)S(1)} %collective-permute-done.7.refs_1_, ...), custom_call_target="tpu_custom_call" | custom-call | flops 1 | bytes 1 | tf_op jit(solution)/shard_map/first/pallas_call | solution.py:280
  18.8 0.0 collective-permute-done.6.refs_0_
  18.8 0.5 %collective-permute-done.5.refs_0_ = bf16[2,2,256,128]{3,2,1,0:T(8,128)(2,1)S(1)} collective-permute-done((bf16[2,2,256,128]{3,2,1,0:T(8,128)(2,1)S(1)}, bf16[2,2,256,128]{3,2,1,0:T(8,128)(2,1)S(1)}, u32[]{:S(2)}, u32[]{:S(2)}) %collective-permute-start.5) | collective-permute-done | bytes 262176 | tf_op jit(solution)/shard_map/ppermute | solution.py:246
  19.3 1.6 %last.1.refs_1_ = bf16[2,256,256]{2,1,0:T(8,128)(2,1)} custom-call(bf16[2,256,128]{2,1,0:T(8,128)(2,1)S(1)} %get-tuple-element.33.q_ref, bf16[2,2,256,128]{3,2,1,0:T(8,128)(2,1)S(1)} %collective-permute-done.5.refs_0_, f32[2,256,1]{2,1,0:T(8,128)S(1)} %get-tuple-element.39.refs_1_, f32[2,256,1]{2,1,0:T(8,128)S(1)} %get-tuple-element.40.refs_2_, ...), custom_call_target="tpu_custom_call" | custom-call | flops 1 | bytes 1 | tf_op jit(solution)/shard_map/last/pallas_call | solution.py:290
  20.9 0.2 collective-permute-done.3.refs_0_
  21.1 0.6 %join.1 = bf16[2,256,256]{2,1,0:T(8,128)(2,1)} custom-call(bf16[2,112,128]{2,1,0:T(8,128)(2,1)S(1)} %collective-permute-done.3.refs_0_, bf16[2,256,256]{2,1,0:T(8,128)(2,1)} %last.1.refs_1_), custom_call_target="tpu_custom_call", output_to_operand_aliasing={{}: (1, {})} | custom-call | flops 1 | bytes 1 | tf_op jit(solution)/shard_map/join/pallas_call | solution.py:303
  (4 shorter events, 0.0 us)
Async XLA Ops:
  1.1 10.5 %collective-permute-start.1 = (bf16[2,2,112,128]{3,2,1,0:T(8,128)(2,1)S(1)}, bf16[2,2,112,128]{3,2,1,0:T(8,128)(2,1)S(1)}, u32[]{:S(2)}, u32[]{:S(2)}) collective-permute-start(bf16[2,2,112,128]{3,2,1,0:T(8,128)(2,1)S(1)} %get-tuple-element.25._.own), channel_id=1, source_target_pairs={{0,8},{4,12},{8,0},{12,4},{1,9},{5,13},{9,1},{13,5},{2,10},{6,14},... | collective-permute-start | bytes 344072 | tf_op jit(solution)/shard_map/ppermute | solution.py:246
  5.2 8.1 %collective-permute-start = (bf16[2,400,128]{2,1,0:T(8,128)(2,1)S(1)}, bf16[2,400,128]{2,1,0:T(8,128)(2,1)S(1)}, u32[]{:S(2)}, u32[]{:S(2)}) collective-permute-start(bf16[2,400,128]{2,1,0:T(8,128)(2,1)S(1)} %get-tuple-element.27), channel_id=1, source_target_pairs={{0,4},{4,0},{8,12},{12,8},{1,5},{5,1},{9,13},{13,9},{2,6},{6,2},{1... | collective-permute-start | bytes 614408 | tf_op jit(solution)/shard_map/ppermute | solution.py:246
  6.8 9.6 %collective-permute-start.2 = (bf16[2,2,112,128]{3,2,1,0:T(8,128)(2,1)S(1)}, bf16[2,2,112,128]{3,2,1,0:T(8,128)(2,1)S(1)}, u32[]{:S(2)}, u32[]{:S(2)}) collective-permute-start(bf16[2,2,112,128]{3,2,1,0:T(8,128)(2,1)S(1)} %get-tuple-element.28), channel_id=1, source_target_pairs={{0,12},{4,8},{8,4},{12,0},{1,13},{5,9},{9,5},{13,1},{2,14},{6,10},... | collective-permute-start | bytes 344072 | tf_op jit(solution)/shard_map/ppermute | solution.py:246
  7.9 9.9 %collective-permute-start.7 = (bf16[2,2,256,128]{3,2,1,0:T(8,128)(2,1)S(1)}, bf16[2,2,256,128]{3,2,1,0:T(8,128)(2,1)S(1)}, u32[]{:S(2)}, u32[]{:S(2)}) collective-permute-start(bf16[2,2,256,128]{3,2,1,0:T(8,128)(2,1)S(1)} %get-tuple-element.34.refs_0_), channel_id=1, source_target_pairs={{0,1},{1,0},{2,3},{3,2},{4,5},{5,4},{6,7},{7,6},{8,9},{9,8},{10,11... | collective-permute-start | bytes 786440 | tf_op jit(solution)/shard_map/ppermute | solution.py:246
  8.0 9.8 %collective-permute-start.4 = (bf16[2,2,256,128]{3,2,1,0:T(8,128)(2,1)S(1)}, bf16[2,2,256,128]{3,2,1,0:T(8,128)(2,1)S(1)}, u32[]{:S(2)}, u32[]{:S(2)}) collective-permute-start(bf16[2,2,256,128]{3,2,1,0:T(8,128)(2,1)S(1)} %get-tuple-element.34.refs_0_), channel_id=1, source_target_pairs={{0,2},{2,0},{1,3},{3,1},{4,6},{6,4},{5,7},{7,5},{8,10},{10,8},{9,1... | collective-permute-start | bytes 786440 | tf_op jit(solution)/shard_map/ppermute | solution.py:246
  13.4 5.4 %collective-permute-start.6 = (bf16[2,2,2,32,128]{4,3,2,1,0:T(8,128)(2,1)S(1)}, bf16[2,2,2,32,128]{4,3,2,1,0:T(8,128)(2,1)S(1)}, u32[]{:S(2)}, u32[]{:S(2)}) collective-permute-start(bf16[2,2,2,32,128]{4,3,2,1,0:T(8,128)(2,1)S(1)} %pack.1.refs_6_), channel_id=1, source_target_pairs={{0,8},{4,12},{8,0},{12,4},{1,9},{5,13},{9,1},{13,5},{2,10},{6,14},... | collective-permute-start | bytes 196616 | tf_op jit(solution)/shard_map/ppermute | solution.py:246
  16.8 4.2 %collective-permute-start.3 = (bf16[2,112,128]{2,1,0:T(8,128)(2,1)S(1)}, bf16[2,112,128]{2,1,0:T(8,128)(2,1)S(1)}, u32[]{:S(2)}, u32[]{:S(2)}) collective-permute-start(bf16[2,112,128]{2,1,0:T(8,128)(2,1)S(1)} %get-tuple-element.32), channel_id=1, source_target_pairs={{0,4},{4,0},{8,12},{12,8},{1,5},{5,1},{9,13},{13,9},{2,6},{6,2},{1... | collective-permute-start | bytes 172040 | tf_op jit(solution)/shard_map/ppermute | solution.py:246
  17.8 1.5 %collective-permute-start.5 = (bf16[2,2,256,128]{3,2,1,0:T(8,128)(2,1)S(1)}, bf16[2,2,256,128]{3,2,1,0:T(8,128)(2,1)S(1)}, u32[]{:S(2)}, u32[]{:S(2)}) collective-permute-start(bf16[2,2,256,128]{3,2,1,0:T(8,128)(2,1)S(1)} %hold.6.refs_2_), channel_id=1, source_target_pairs={{0,1},{1,0},{2,3},{3,2},{4,5},{5,4},{6,7},{7,6},{8,9},{9,8},{10,11... | collective-permute-start | bytes 786440 | tf_op jit(solution)/shard_map/ppermute | solution.py:246
